TPU v7x, 128 devices: a whole 4x4x4 slice. The times are simulated.
128 devices in a mesh: expert: 32 (over z, x, core), dp: 4 (over y).
Axes of the slice: x: 4, y: 4, z: 4, core: 2. Of those that a mesh axis runs over, the one named last changes fastest.
Arguments:
- tokens: bfloat16 [65536, 4096], P(('expert', 'dp')), may hold values from -6 to 6
- out_grad: bfloat16 [65536, 4096], P(('expert', 'dp')), may hold values from -6 to 6
- gates: bfloat16 [128, 2, 24], P(('expert', 'dp')), may hold values from 0.049804688 to 1
- picks: int32 [128, 2, 24], P(('expert', 'dp')), may hold values from 0 to 511, as said below
- counts: int32 [128, 2], P(('expert', 'dp')), may hold values from 1 to 24, as said below
- w_in: bfloat16 [32, 4096, 512], P('expert'), may hold values from -0.09375 to 0.09375
- w_out: bfloat16 [32, 4096, 512], P('expert'), may hold values from -0.0625 to 0.0625
Outputs:
- tokens_grad: bfloat16 [65536, 4096], P(('expert', 'dp'))
- gates_grad: float32 [128, 2, 24], P(('expert', 'dp'))
- w_in_grad: bfloat16 [32, 4096, 512], P('expert', 'dp')
- w_out_grad: bfloat16 [32, 4096, 512], P('expert', 'dp')
Inputs may be any that keep to these rules, and one draw needn't show every extreme that they name: picks[j, k, :] are 24 distinct rows of device j's tokens; slots at and beyond counts[j, k] hold rows too, but are not live. `counts`: in every draw some device fills all 24 slots of some expert.
All inputs are finite; a program needn't handle non-finite values.
Results may differ from a plain program's by a relative error of at most 0.013.
Values may be sent and summed in bfloat16 or wider, within the bound.
No kernel may reach another device: no remote copies, remote signals or barrier semaphores. Data moves between devices by JAX's collectives and lax.ppermute only.
A program may use at most 192 MiB of HBM per device.

v0:
```python
import jax
import jax.numpy as jnp
from jax import lax
from jax.sharding import PartitionSpec as P

FF = 8192


def local(tokens, out_grad, gates, picks, counts, w_in, w_out):
    t_dev, model_width = tokens.shape
    expert_count = picks.shape[1]
    slot_count = picks.shape[2]
    part_units = w_in.shape[2]
    part_count = FF // part_units
    expert_devices = lax.axis_size("expert")
    row_index = picks[0].reshape(-1)
    picked_x = tokens[row_index].reshape(expert_count, slot_count, model_width)
    picked_dy = out_grad[row_index].reshape(expert_count, slot_count, model_width)
    live = jnp.arange(slot_count)[None, :] < counts[0][:, None]
    scale = jnp.where(live, gates[0], jnp.zeros_like(gates[0]))

    def spread(values):
        wide = jnp.broadcast_to(values[:, None], (expert_count, part_count) + values.shape[1:])
        return wide.reshape((expert_devices,) + values.shape[1:])

    got_x, got_dy, got_scale = (
        lax.all_to_all(spread(picked_x), "expert", split_axis=0, concat_axis=0, tiled=True),
        lax.all_to_all(spread(picked_dy), "expert", split_axis=0, concat_axis=0, tiled=True),
        lax.all_to_all(spread(scale), "expert", split_axis=0, concat_axis=0, tiled=True),
    )
    row_count = expert_devices * slot_count
    rows_x = got_x.reshape(row_count, model_width)
    rows_dy = got_dy.reshape(row_count, model_width)
    rows_scale = got_scale.reshape(row_count)
    scaled_dy = (rows_scale.astype(jnp.float32)[:, None] * rows_dy.astype(jnp.float32)).astype(
        jnp.bfloat16
    )
    weight_in = w_in[0]
    weight_out = w_out[0]
    pre = jnp.dot(rows_x, weight_in, preferred_element_type=jnp.float32)
    hidden, gelu_back = jax.vjp(jax.nn.gelu, pre)
    hidden = hidden.astype(jnp.bfloat16)
    part_out = lax.dot_general(
        hidden, weight_out, (((1,), (1,)), ((), ())), preferred_element_type=jnp.float32
    )
    gate_part = jnp.sum(rows_dy.astype(jnp.float32) * part_out, axis=-1)
    hidden_grad = jnp.dot(scaled_dy, weight_out, preferred_element_type=jnp.float32)
    pre_grad = gelu_back(hidden_grad)[0].astype(jnp.bfloat16)
    row_part = lax.dot_general(
        pre_grad, weight_in, (((1,), (1,)), ((), ())), preferred_element_type=jnp.float32
    )
    columns = rows_x
    w_in_grad = lax.psum_scatter(
        lax.dot_general(
            columns, pre_grad, (((0,), (0,)), ((), ())), preferred_element_type=jnp.float32
        ).astype(jnp.bfloat16),
        "dp",
        scatter_dimension=0,
        tiled=True,
    )[None]
    columns = scaled_dy
    w_out_grad = lax.psum_scatter(
        lax.dot_general(
            columns, hidden, (((0,), (0,)), ((), ())), preferred_element_type=jnp.float32
        ).astype(jnp.bfloat16),
        "dp",
        scatter_dimension=0,
        tiled=True,
    )[None]
    back_rows, back_gates = (
        lax.all_to_all(
            row_part.reshape(expert_devices, slot_count, model_width).astype(jnp.bfloat16),
            "expert",
            split_axis=0,
            concat_axis=0,
            tiled=True,
        ).astype(jnp.float32),
        lax.all_to_all(
            gate_part.reshape(expert_devices, slot_count).astype(jnp.bfloat16),
            "expert",
            split_axis=0,
            concat_axis=0,
            tiled=True,
        ).astype(jnp.float32),
    )
    summed_rows = jnp.sum(
        back_rows.reshape(expert_count, part_count, slot_count, model_width), axis=1
    )
    summed_gates = jnp.sum(back_gates.reshape(expert_count, part_count, slot_count), axis=1)
    empty_rows = jnp.zeros((t_dev, model_width), jnp.float32)
    tokens_grad = (
        empty_rows.at[row_index].add(summed_rows.reshape(-1, model_width)).astype(jnp.bfloat16)
    )
    gates_grad = jnp.where(live, summed_gates, jnp.zeros_like(summed_gates))[None]
    return (tokens_grad, gates_grad, w_in_grad, w_out_grad)


def solution(mesh):
    placed = (
        P(("expert", "dp"), None),
        P(("expert", "dp"), None),
        P(("expert", "dp"), None, None),
        P(("expert", "dp"), None, None),
        P(("expert", "dp"), None),
        P("expert", None, None),
        P("expert", None, None),
    )
    return jax.shard_map(
        local,
        mesh=mesh,
        in_specs=placed,
        out_specs=(
            P(("expert", "dp"), None),
            P(("expert", "dp"), None, None),
            P("expert", "dp", None),
            P("expert", "dp", None),
        ),
        check_vma=False,
    )
```

profile of v0, /device:TPU:0, one launch (start us, length us, event | category | flops | bytes accessed | tf_op | source)
XLA Modules:
  0.0 351.0 jit_solution(430367959723586983)
XLA Ops:
  7.2 0.7 compare_select_fusion.2
  7.9 0.6 copy.12
  8.5 8.2 %all-to-all-start = ((bf16[32,1,24]{2,1,0:T(2,128)(2,1)}), bf16[32,1,24]{2,1,0:T(2,128)(2,1)S(1)}, u32[]{:S(2)}, u32[]{:S(2)}) async-start(bf16[32,1,24]{2,1,0:T(2,128)(2,1)} %copy.12), calls=%async_computation | async-start | bytes 32768 | tf_op jit(solution)/shard_map/all_to_all | solution.py:29
  16.8 0.8 reshape_squeeze.3
  17.6 3.9 %gather_fusion.1 = bf16[48,4096]{1,0:T(8,128)(2,1)S(1)} fusion(bf16[512,4096]{1,0:T(8,128)(2,1)} %param.7, s32[1024]{0:T(1024)S(1)} %pad_clamp_fusion), kind=kCustom, calls=%fused_computation.1 | custom fusion | bytes 786624 | tf_op jit(solution)/shard_map/gather | solution.py:17
  21.5 2.6 all-to-all-done
  24.1 3.4 broadcast_in_dim.47
  27.5 4.9 %all-to-all-start.2 = ((bf16[32,24,4096]{2,1,0:T(8,128)(2,1)}), bf16[32,24,4096]{2,1,0:T(8,128)(2,1)}, u32[]{:S(2)}, u32[]{:S(2)}) async-start(bf16[32,24,4096]{2,1,0:T(8,128)(2,1)} %bitcast.52), calls=%async_computation.2 | async-start | bytes 12582912 | tf_op jit(solution)/shard_map/all_to_all | solution.py:27
  32.4 3.9 %gather_fusion = bf16[48,4096]{1,0:T(8,128)(2,1)S(1)} fusion(bf16[512,4096]{1,0:T(8,128)(2,1)} %param.8, s32[1024]{0:T(1024)S(1)} %pad_clamp_fusion), kind=kCustom, calls=%fused_computation | custom fusion | bytes 786624 | tf_op jit(solution)/shard_map/gather | solution.py:18
  36.3 74.0 %all-to-all-done.2 = bf16[32,24,4096]{2,1,0:T(8,128)(2,1)} async-done(((bf16[32,24,4096]{2,1,0:T(8,128)(2,1)}), bf16[32,24,4096]{2,1,0:T(8,128)(2,1)}, u32[]{:S(2)}, u32[]{:S(2)}) %all-to-all-start.2) | async-done | bytes 6291488 | tf_op jit(solution)/shard_map/all_to_all | solution.py:27
  110.3 3.4 broadcast_in_dim.45
  113.7 4.9 %all-to-all-start.1 = ((bf16[32,24,4096]{2,1,0:T(8,128)(2,1)}), bf16[32,24,4096]{2,1,0:T(8,128)(2,1)}, u32[]{:S(2)}, u32[]{:S(2)}) async-start(bf16[32,24,4096]{2,1,0:T(8,128)(2,1)} %bitcast.51), calls=%async_computation.1 | async-start | bytes 12582912 | tf_op jit(solution)/shard_map/all_to_all | solution.py:28
  118.6 0.2 reduce-scatter.3.cloned.1.call-start
  118.8 6.7 %fusion.4 = f32[768,512]{1,0:T(8,128)S(1)} fusion(bf16[768,4096]{1,0:T(8,128)(2,1)} %bitcast.11, bf16[1,4096,512]{2,1,0:T(8,128)(2,1)} %param.12), kind=kOutput, calls=%fused_computation.14 | convolution fusion | flops 3221225472 | bytes 12058624 | tf_op jit(solution)/shard_map/dot_general | solution.py:40
  125.6 70.9 %all-to-all-done.1 = bf16[32,24,4096]{2,1,0:T(8,128)(2,1)} async-done(((bf16[32,24,4096]{2,1,0:T(8,128)(2,1)}), bf16[32,24,4096]{2,1,0:T(8,128)(2,1)}, u32[]{:S(2)}, u32[]{:S(2)}) %all-to-all-start.1) | async-done | bytes 6291488 | tf_op jit(solution)/shard_map/all_to_all | solution.py:28
  196.5 0.0 copy-start.1
  196.5 5.0 %fusion = bf16[32,24,4096]{2,1,0:T(8,128)(2,1)S(1)} fusion(bf16[32,24,4096]{2,1,0:T(8,128)(2,1)} %all-to-all-done.1, f32[32,24]{1,0:T(8,128)S(1)} %bitcast.57), kind=kLoop, calls=%fused_computation.7 | loop fusion | flops 9437184 | bytes 12585984 | tf_op jit(solution)/shard_map/convert_element_type | solution.py:35
  201.5 0.0 copy-done.1
  201.5 4.2 %fusion.17 = bf16[768,512]{1,0:T(8,128)(2,1)S(1)} fusion(f32[768,512]{1,0:T(8,128)S(1)} %fusion.4, bf16[768,4096]{1,0:T(8,128)(2,1)S(1)} %bitcast.53, bf16[1,4096,512]{2,1,0:T(8,128)(2,1)S(1)} %copy-done.1), kind=kOutput, calls=%fused_computation.29 | convolution fusion | flops 3229089792 | bytes 12845056 | tf_op jit(solution)/shard_map/dot_general | solution.py:47
  205.7 7.9 %convolution_convert_fusion.2 = bf16[4096,512]{1,0:T(8,128)(2,1)} fusion(bf16[768,4096]{1,0:T(8,128)(2,1)} %bitcast.11, bf16[768,512]{1,0:T(8,128)(2,1)S(1)} %fusion.17), kind=kOutput, calls=%fused_computation.12 | convolution fusion | flops 3223322624 | bytes 11272192 | tf_op jit(solution)/shard_map/dot_general | solution.py:54
  213.6 0.0 reduce-scatter.3.cloned.1.call-update
  213.7 0.3 reduce-scatter.5.cloned.1.call-start
  213.9 0.1 convert_reduce_fusion.1
  214.0 0.1 reshape.178
  214.1 4.8 %fusion.2 = bf16[768,4096]{1,0:T(8,128)(2,1)S(1)} fusion(bf16[32,24,4096]{2,1,0:T(8,128)(2,1)} %all-to-all-done.1, f32[768]{0:T(1024)S(1)} %reshape.178), kind=kLoop, calls=%fused_computation.9 | loop fusion | flops 9437184 | bytes 12585984 | tf_op jit(solution)/shard_map/convert_element_type | solution.py:35
  218.9 5.3 %convolution_convert_fusion.1 = bf16[4096,512]{1,0:T(8,128)(2,1)} fusion(bf16[768,4096]{1,0:T(8,128)(2,1)S(1)} %fusion.2, f32[768,512]{1,0:T(8,128)S(1)} %fusion.4), kind=kOutput, calls=%fused_computation.11 | convolution fusion | flops 3226861568 | bytes 12058624 | tf_op jit(solution)/shard_map/dot_general | solution.py:63
  224.2 0.0 reduce-scatter.5.cloned.1.call-update
  224.2 7.1 %fusion.1 = bf16[768]{0:T(1024)(128)(2,1)S(1)} fusion(bf16[32,24,4096]{2,1,0:T(8,128)(2,1)} %all-to-all-done.1, bf16[1,4096,512]{2,1,0:T(8,128)(2,1)} %param.13, f32[768,512]{1,0:T(8,128)S(1)} %fusion.4), kind=kOutput, calls=%fused_computation.8 | convolution fusion | flops 3234200832 | bytes 12060160 | tf_op jit(solution)/shard_map/dot_general | solution.py:43
  231.3 0.7 convert_element_type.101
  232.1 3.8 %all-to-all-start.4 = ((bf16[32,1,24]{2,1,0:T(2,128)(2,1)}), bf16[32,1,24]{2,1,0:T(2,128)(2,1)S(1)}, u32[]{:S(2)}, u32[]{:S(2)}) async-start(bf16[32,1,24]{2,1,0:T(2,128)(2,1)} %convert_element_type.101), calls=%async_computation.4 | async-start | bytes 32768 | tf_op jit(solution)/shard_map/all_to_all | solution.py:78
  235.9 7.5 %convolution_convert_fusion = bf16[32,24,4096]{2,1,0:T(8,128)(2,1)} fusion(bf16[32,24,512]{2,1,0:T(8,128)(2,1)S(1)} %bitcast.64, bf16[1,4096,512]{2,1,0:T(8,128)(2,1)} %param.12), kind=kOutput, calls=%fused_computation.10 | convolution fusion | flops 3224371200 | bytes 11272192 | tf_op jit(solution)/shard_map/dot_general | solution.py:49
  243.4 0.0 copy-start
  243.4 0.0 all-to-all-done.4
  243.4 7.6 %all-to-all-start.3 = ((bf16[32,24,4096]{2,1,0:T(8,128)(2,1)}), bf16[32,24,4096]{2,1,0:T(8,128)(2,1)}, u32[]{:S(2)}, u32[]{:S(2)}) async-start(bf16[32,24,4096]{2,1,0:T(8,128)(2,1)} %convolution_convert_fusion), calls=%async_computation.3 | async-start | bytes 12582912 | tf_op jit(solution)/shard_map/all_to_all | solution.py:71
  251.1 0.0 copy-done
  251.1 0.6 compare_select_fusion.1
  251.8 77.2 %all-to-all-done.3 = bf16[32,24,4096]{2,1,0:T(8,128)(2,1)} async-done(((bf16[32,24,4096]{2,1,0:T(8,128)(2,1)}), bf16[32,24,4096]{2,1,0:T(8,128)(2,1)}, u32[]{:S(2)}, u32[]{:S(2)}) %all-to-all-start.3) | async-done | bytes 6291488 | tf_op jit(solution)/shard_map/all_to_all | solution.py:71
  328.9 3.9 %convert_reduce_fusion = f32[2,24,4096]{2,1,0:T(8,128)S(1)} fusion(bf16[32,24,4096]{2,1,0:T(8,128)(2,1)} %all-to-all-done.3), kind=kLoop, calls=%fused_computation.3 | loop fusion | flops 6094848 | bytes 7077888 | tf_op jit(solution)/shard_map/reduce_sum | solution.py:86
  332.8 5.3 %scatter_custom_fusion = f32[512,4096]{1,0:T(8,128)} fusion(s32[48]{0:T(128)S(1)} %fusion.20, f32[48,4096]{1,0:T(8,128)S(1)} %bitcast.56, f32[]{:T(128)} %constant.10.clone.1), kind=kCustom, calls=%fused_computation.19 | custom fusion | flops 196608 | bytes 8388612 | tf_op jit(solution)/shard_map/scatter-add | solution.py:92
  338.1 6.0 %convert_element_type.84 = bf16[512,4096]{1,0:T(8,128)(2,1)} convert(f32[512,4096]{1,0:T(8,128)} %scatter_custom_fusion) | non-fusion elementwise | flops 2097152 | bytes 12582912 | tf_op jit(solution)/shard_map/convert_element_type | solution.py:92
  344.1 0.0 reduce-scatter.3.cloned.1.call-done
  344.1 0.0 reduce-scatter.5.cloned.1.call-done
  (6 shorter events, 0.1 us)
Async XLA Ops:
  8.5 15.5 %all-to-all-start = ((bf16[32,1,24]{2,1,0:T(2,128)(2,1)}), bf16[32,1,24]{2,1,0:T(2,128)(2,1)S(1)}, u32[]{:S(2)}, u32[]{:S(2)}) async-start(bf16[32,1,24]{2,1,0:T(2,128)(2,1)} %copy.12), calls=%async_computation | async-start | bytes 32768 | tf_op jit(solution)/shard_map/all_to_all | solution.py:29
  27.5 82.8 %all-to-all-start.2 = ((bf16[32,24,4096]{2,1,0:T(8,128)(2,1)}), bf16[32,24,4096]{2,1,0:T(8,128)(2,1)}, u32[]{:S(2)}, u32[]{:S(2)}) async-start(bf16[32,24,4096]{2,1,0:T(8,128)(2,1)} %bitcast.52), calls=%async_computation.2 | async-start | bytes 12582912 | tf_op jit(solution)/shard_map/all_to_all | solution.py:27
  113.7 82.8 %all-to-all-start.1 = ((bf16[32,24,4096]{2,1,0:T(8,128)(2,1)}), bf16[32,24,4096]{2,1,0:T(8,128)(2,1)}, u32[]{:S(2)}, u32[]{:S(2)}) async-start(bf16[32,24,4096]{2,1,0:T(8,128)(2,1)} %bitcast.51), calls=%async_computation.1 | async-start | bytes 12582912 | tf_op jit(solution)/shard_map/all_to_all | solution.py:28
  118.6 225.6 %reduce-scatter.3.cloned.1.call-start = ((), (), s32[]{:S(2)}) async-start(), calls=%async_computation.7 | async-start | bytes 5242880 | tf_op jit(solution)/shard_map/reduce_scatter | solution.py:53
  196.5 5.0 %copy-start.1 = (bf16[1,4096,512]{2,1,0:T(8,128)(2,1)S(1)}, bf16[1,4096,512]{2,1,0:T(8,128)(2,1)}, u32[]{:S(2)}) copy-start(bf16[1,4096,512]{2,1,0:T(8,128)(2,1)} %param.13) | copy-start | bytes 12582916
  213.7 130.5 %reduce-scatter.5.cloned.1.call-start = ((), (), s32[]{:S(2)}) async-start(), calls=%async_computation.8 | async-start | bytes 5242880 | tf_op jit(solution)/shard_map/reduce_scatter | solution.py:62
  232.1 11.4 %all-to-all-start.4 = ((bf16[32,1,24]{2,1,0:T(2,128)(2,1)}), bf16[32,1,24]{2,1,0:T(2,128)(2,1)S(1)}, u32[]{:S(2)}, u32[]{:S(2)}) async-start(bf16[32,1,24]{2,1,0:T(2,128)(2,1)} %convert_element_type.101), calls=%async_computation.4 | async-start | bytes 32768 | tf_op jit(solution)/shard_map/all_to_all | solution.py:78
  243.4 7.7 %copy-start = (s32[1,2]{1,0:T(1,128)S(1)}, s32[1,2]{1,0:T(1,128)}, u32[]{:S(2)}) copy-start(s32[1,2]{1,0:T(1,128)} %param.11) | copy-start | bytes 28
  243.4 85.5 %all-to-all-start.3 = ((bf16[32,24,4096]{2,1,0:T(8,128)(2,1)}), bf16[32,24,4096]{2,1,0:T(8,128)(2,1)}, u32[]{:S(2)}, u32[]{:S(2)}) async-start(bf16[32,24,4096]{2,1,0:T(8,128)(2,1)} %convolution_convert_fusion), calls=%async_computation.3 | async-start | bytes 12582912 | tf_op jit(solution)/shard_map/all_to_all | solution.py:71
Sparse Core Ops, SparseCore 0:
  213.8 43.7 reduce-scatter.2
  260.7 46.5 reduce-scatter.4
where the time goes:
time: 352 us; the launch traced here: 351 us
  waiting for transfers between devices  225 us (64%)
  matrix products  38.8 us (11%)
  starting transfers between devices  30 us (9%)
  other arithmetic  26.5 us (8%)
  local copies, waits for them, and re-layouts  16.8 us (5%)
  between operations  14.2 us (4%)
    all_to_all x1, waiting for transfers between devices, local(): lax.all_to_all(row_part.reshape(expert_devices, slot_count, model_width)....  77.2 us
    all_to_all x1, waiting for transfers between devices, local(): lax.all_to_all(spread(picked_x), 'expert', split_axis=0, concat_axis=0, t...  74 us
    all_to_all x1, waiting for transfers between devices, local(): lax.all_to_all(spread(picked_dy), 'expert', split_axis=0, concat_axis=0,...  70.9 us
    convert_element_type x2, other arithmetic, local(): (rows_scale.astype(jnp.float32)[:, None] * rows_dy.astype(jnp.float32)).a...  9.8 us
    all_to_all x1, starting transfers between devices, local(): lax.all_to_all(spread(scale), 'expert', split_axis=0, concat_axis=0, tile...  8.24 us
    dot_general x1, matrix products, local(): lax.dot_general(columns, pre_grad, (((0,), (0,)), ((), ())), preferred_el...  7.93 us
    all_to_all x1, starting transfers between devices, local(): lax.all_to_all(row_part.reshape(expert_devices, slot_count, model_width)....  7.64 us
    dot_general x1, matrix products, local(): lax.dot_general(pre_grad, weight_in, (((1,), (1,)), ((), ())), preferred_...  7.51 us
  transfers between devices with their start and end apart: 7, of which 4 were waited for; matrix products, arithmetic and copies ran while one was open for 16% of the time, Pallas kernels for 0%

commit v1 on v0

v1 whole, which is shorter than its diff:
```python
import jax
import jax.numpy as jnp
from jax import lax
from jax.sharding import Mesh
from jax.sharding import PartitionSpec as P

GROUP = ("zz", "x", "c")
SWAP = [(0, 1), (1, 0)]
F32 = jnp.float32
BF16 = jnp.bfloat16


def rows_of(picks, t_dev, weights):
    hit = picks.reshape(-1, 1) == jnp.arange(t_dev)[None, :]
    return jnp.where(hit, weights.reshape(-1, 1), jnp.zeros((), BF16))


def local(tokens, out_grad, gates, picks, counts, w_in, w_out):
    t_dev, width = tokens.shape
    experts, slots = picks.shape[1:]
    parts = lax.axis_size("zz") * lax.axis_size("x") * lax.axis_size("c")
    k = lax.axis_index("k")
    live = jnp.arange(slots)[None, :] < counts[0][:, None]
    scale = jnp.where(live, gates[0], jnp.zeros_like(gates[0]))
    select = rows_of(picks[0], t_dev, jnp.ones((experts * slots,), BF16))
    scaled_select = rows_of(picks[0], t_dev, scale)

    def collect(table, sel):
        picked = jnp.dot(sel, table, preferred_element_type=F32).astype(BF16)
        picked = picked.reshape(experts, slots, width)
        mine = lax.dynamic_index_in_dim(picked, k, 0, keepdims=False)
        other = lax.dynamic_index_in_dim(picked, 1 - k, 0, keepdims=False)
        swapped = lax.ppermute(other, "k", SWAP)
        first = jnp.where(k == 0, mine, swapped)
        second = jnp.where(k == 0, swapped, mine)
        both = jnp.concatenate([first, second], 0)
        return lax.all_gather(both, GROUP, axis=0, tiled=True)

    rows_x = collect(tokens, select)
    rows_dy = collect(out_grad, scaled_select)
    weight_in = w_in[0]
    weight_out = w_out[0]
    pre = jnp.dot(rows_x, weight_in, preferred_element_type=F32)
    hidden, gelu_back = jax.vjp(jax.nn.gelu, pre)
    hidden = hidden.astype(BF16)
    out_part = lax.dot_general(
        rows_dy, hidden, (((0,), (0,)), ((), ())), preferred_element_type=F32
    ).astype(BF16)
    w_out_grad = lax.psum_scatter(out_part, "dp", scatter_dimension=0, tiled=True)
    hidden_grad = jnp.dot(rows_dy, weight_out, preferred_element_type=F32)
    gate_part = jnp.sum(hidden.astype(F32) * hidden_grad, axis=-1)
    pre_grad = gelu_back(hidden_grad)[0].astype(BF16)
    in_part = lax.dot_general(
        rows_x, pre_grad, (((0,), (0,)), ((), ())), preferred_element_type=F32
    ).astype(BF16)
    w_in_grad = lax.psum_scatter(in_part, "dp", scatter_dimension=0, tiled=True)

    def by_home(v):
        v = v.reshape((parts, 2, slots) + v.shape[1:])
        return jnp.swapaxes(v, 0, 1).reshape((2 * parts * slots,) + v.shape[3:])

    row_part = lax.dot_general(
        by_home(pre_grad), weight_in, (((1,), (1,)), ((), ())), preferred_element_type=F32
    ).astype(BF16)
    gate_part = by_home(gate_part)
    back = lax.all_to_all(
        row_part.reshape(2 * parts, slots, width), ("k",) + GROUP, split_axis=0, concat_axis=0, tiled=True
    )
    back_gates = lax.all_to_all(
        gate_part.reshape(2 * parts, slots).astype(BF16),
        ("k",) + GROUP,
        split_axis=0,
        concat_axis=0,
        tiled=True,
    )
    sums = jnp.sum(back.reshape(experts, parts, slots, width).astype(F32), axis=1)
    sums = sums.reshape(experts * slots, width)
    high = sums.astype(BF16)
    low = (sums - high.astype(F32)).astype(BF16)
    tokens_grad = lax.dot_general(
        jnp.concatenate([select, select], 0),
        jnp.concatenate([high, low], 0),
        (((0,), (0,)), ((), ())),
        preferred_element_type=F32,
    ).astype(BF16)
    gate_sum = jnp.sum(back_gates.reshape(experts, parts, slots).astype(F32), axis=1)
    gates_grad = jnp.where(live, gate_sum / gates[0].astype(F32), jnp.zeros_like(gate_sum))
    return (tokens_grad, gates_grad[None], w_in_grad[None], w_out_grad[None])


def solution(mesh):
    experts_axis, dp = mesh.devices.shape
    fine = Mesh(mesh.devices.reshape(2, 2, 4, 2, dp), ("k", "zz", "x", "c", "dp"))
    expert = ("k", "zz", "x", "c")
    rows = expert + ("dp",)
    placed = (
        P(rows, None),
        P(rows, None),
        P(rows, None, None),
        P(rows, None, None),
        P(rows, None),
        P(expert, None, None),
        P(expert, None, None),
    )
    return jax.shard_map(
        local,
        mesh=fine,
        in_specs=placed,
        out_specs=(
            P(rows, None),
            P(rows, None, None),
            P(expert, "dp", None),
            P(expert, "dp", None),
        ),
        check_vma=False,
    )
```

time: 352 us -> 247 us (0.70)
  waiting for transfers between devices: 225 us -> 157 us
  other arithmetic: 26.5 us -> 6.39 us
  local copies, waits for them, and re-layouts: 16.8 us -> 1.76 us
  starting transfers between devices: 30 us -> 21.8 us
  matrix products: 38.8 us -> 45.6 us
    all_to_all x5 -> x2, waiting for transfers between devices: 225 us -> 77.1 us  [the longest x1 77.1 us: local(): lax.all_to_all(row_part.reshape(2 * parts, slots, width), ('k',) + GROUP,...]
    all_gather x0 -> x2, waiting for transfers between devices: none -> 71 us  [collect(): return lax.all_gather(both, GROUP, axis=0, tiled=True)]
    convert_element_type x6 -> x2, other arithmetic: 15.9 us -> 0.08 us  [the longest x1 0.06 us: local(): low = (sums - high.astype(F32)).astype(BF16)]
    all_to_all x5 -> x2, starting transfers between devices: 29.5 us -> 14.2 us  [the longest x1 7.33 us: local(): lax.all_to_all(row_part.reshape(2 * parts, slots, width), ('k',) + GROUP,...]
    ppermute x0 -> x2, waiting for transfers between devices: none -> 9.25 us  [collect(): swapped = lax.ppermute(other, 'k', SWAP)]
    gather x2 -> x0, local copies, waits for them, and re-layouts: 7.78 us -> none  [the longest x1 3.89 us: local(): out_grad[row_index].reshape(expert_count, slot_count, model_width)]
    ppermute x0 -> x2, starting transfers between devices: none -> 7.36 us  [collect(): swapped = lax.ppermute(other, 'k', SWAP)]
    broadcast_in_dim x3 -> x0, local copies, waits for them, and re-layouts: 6.83 us -> none  [spread(): jnp.broadcast_to(values[:, None], (expert_count, part_count) + values.sha...]
  transfers between devices with their start and end apart: 7 -> 8, of which waited for: 4 -> 5; matrix products, arithmetic and copies ran while one was open for 16% -> 14% of each run, Pallas kernels for 0% -> 0%
where the time goes in v1:
time: 247 us
  waiting for transfers between devices  157 us (64%)
  matrix products  45.6 us (18%)
  starting transfers between devices  21.8 us (9%)
  between operations  13.9 us (6%)
  other arithmetic  6.39 us (3%)
    all_to_all x1, waiting for transfers between devices, local(): lax.all_to_all(row_part.reshape(2 * parts, slots, width), ('k',) + GROUP,...  77.1 us
    all_gather x2, waiting for transfers between devices, collect(): return lax.all_gather(both, GROUP, axis=0, tiled=True)  71 us
    ppermute x2, waiting for transfers between devices, collect(): swapped = lax.ppermute(other, 'k', SWAP)  9.25 us
    dot_general x1, matrix products, local(): hidden_grad = jnp.dot(rows_dy, weight_out, preferred_element_type=F32)  8.58 us
    dot_general x1, matrix products, local(): lax.dot_general(rows_dy, hidden, (((0,), (0,)), ((), ())), preferred_elem...  8.17 us
    dot_general x1, matrix products, local(): lax.dot_general(by_home(pre_grad), weight_in, (((1,), (1,)), ((), ())), p...  7.62 us
    ppermute x2, starting transfers between devices, collect(): swapped = lax.ppermute(other, 'k', SWAP)  7.36 us
    all_to_all x1, starting transfers between devices, local(): lax.all_to_all(row_part.reshape(2 * parts, slots, width), ('k',) + GROUP,...  7.33 us
  transfers between devices with their start and end apart: 8, of which 5 were waited for; matrix products, arithmetic and copies ran while one was open for 14% of the time, Pallas kernels for 0%

profile of v1, /device:TPU:0, one launch (start us, length us, event | category | flops | bytes accessed | tf_op | source)
XLA Modules:
  0.0 246.9 jit_solution(11102024474070853435)
XLA Ops:
  7.2 0.0 all-gather.5.cloned.1.call-start
  7.2 0.8 eq.10
  8.0 3.1 %convolution_convert_fusion.4 = bf16[48,4096]{1,0:T(8,128)(2,1)S(1)} fusion(bf16[512,4096]{1,0:T(8,128)(2,1)} %param.7, s32[48]{0:T(128)S(1)} %eq.10), kind=kOutput, calls=%fused_computation.5 | convolution fusion | flops 201572352 | bytes 4587712 | tf_op jit(solution)/shard_map/dot_general | solution.py:29
  11.1 0.0 copy-start
  11.1 0.0 copy-start.1
  11.1 4.0 %collective-permute-start.1 = (bf16[24,4096]{1,0:T(8,128)(2,1)S(1)}, bf16[24,4096]{1,0:T(8,128)(2,1)S(1)}, u32[]{:S(2)}, u32[]{:S(2)}) collective-permute-start(bf16[24,4096]{1,0:T(8,128)(2,1)S(1)} %dynamic-slice_bitcast_fusion), channel_id=1, source_target_pairs={{0,64},{64,0},{1,65},{65,1},{2,66},{66,2},{3,67},{67,3},{4,68},{68... | collective-permute-start | bytes 589832 | tf_op jit(solution)/shard_map/ppermute | solution.py:33
  15.1 4.9 %collective-permute-done.1 = bf16[24,4096]{1,0:T(8,128)(2,1)S(1)} collective-permute-done((bf16[24,4096]{1,0:T(8,128)(2,1)S(1)}, bf16[24,4096]{1,0:T(8,128)(2,1)S(1)}, u32[]{:S(2)}, u32[]{:S(2)}) %collective-permute-start.1) | collective-permute-done | bytes 196640 | tf_op jit(solution)/shard_map/ppermute | solution.py:33
  20.1 0.8 pad_maximum_fusion.1
  20.9 0.0 all-gather.5.cloned.1.call-update
  20.9 0.0 all-gather.3.cloned.1.call-start
  20.9 0.0 copy-done
  20.9 0.1 iota_compare_fusion.1
  21.0 0.1 lt.48
  21.1 0.0 copy-done.1
  21.1 0.1 squeeze.23
  21.2 3.1 %convolution_convert_fusion.5 = bf16[48,4096]{1,0:T(8,128)(2,1)S(1)} fusion(bf16[512,4096]{1,0:T(8,128)(2,1)} %param.8, s32[48]{0:T(128)S(1)} %eq.10, bf16[48]{0:T(256)(128)(2,1)S(1)} %broadcast_select_fusion), kind=kOutput, calls=%fused_computation.6 | convolution fusion | flops 201572352 | bytes 4587808 | tf_op jit(solution)/shard_map/dot_general | solution.py:29
  24.3 3.3 %collective-permute-start = (bf16[24,4096]{1,0:T(8,128)(2,1)S(1)}, bf16[24,4096]{1,0:T(8,128)(2,1)S(1)}, u32[]{:S(2)}, u32[]{:S(2)}) collective-permute-start(bf16[24,4096]{1,0:T(8,128)(2,1)S(1)} %dynamic-slice_bitcast_fusion.1), channel_id=1, source_target_pairs={{0,64},{64,0},{1,65},{65,1},{2,66},{66,2},{3,67},{67,3},{4,68},{68... | collective-permute-start | bytes 589832 | tf_op jit(solution)/shard_map/ppermute | solution.py:33
  27.6 4.3 %collective-permute-done = bf16[24,4096]{1,0:T(8,128)(2,1)S(1)} collective-permute-done((bf16[24,4096]{1,0:T(8,128)(2,1)S(1)}, bf16[24,4096]{1,0:T(8,128)(2,1)S(1)}, u32[]{:S(2)}, u32[]{:S(2)}) %collective-permute-start) | collective-permute-done | bytes 196640 | tf_op jit(solution)/shard_map/ppermute | solution.py:33
  32.0 0.8 pad_maximum_fusion
  32.8 0.0 all-gather.3.cloned.1.call-update
  32.8 0.0 reduce-scatter.3.cloned.1.call-start
  32.9 32.3 %all-gather.5.cloned.1.call-done = bf16[768,4096]{1,0:T(8,128)(2,1)} async-done(((bf16[48,4096]{1,0:T(8,128)(2,1)}), bf16[768,4096]{1,0:T(8,128)(2,1)}) %all-gather.5.cloned.1.call-update) | async-done | bytes 6291472 | tf_op jit(solution)/shard_map/all_gather | solution.py:37
  65.1 6.7 %fusion.1 = f32[768,512]{1,0:T(8,128)S(1)} fusion(bf16[768,4096]{1,0:T(8,128)(2,1)} %all-gather.5.cloned.1.call-done, bf16[1,4096,512]{2,1,0:T(8,128)(2,1)} %param.12), kind=kOutput, calls=%fused_computation.8 | convolution fusion | flops 3221225472 | bytes 12058624 | tf_op jit(solution)/shard_map/dot_general | solution.py:43
  71.9 38.7 %all-gather.3.cloned.1.call-done = bf16[768,4096]{1,0:T(8,128)(2,1)} async-done(((bf16[48,4096]{1,0:T(8,128)(2,1)}), bf16[768,4096]{1,0:T(8,128)(2,1)}) %all-gather.3.cloned.1.call-update) | async-done | bytes 6291472 | tf_op jit(solution)/shard_map/all_gather | solution.py:37
  110.6 0.0 copy-start.2
  110.6 8.6 %multiply_reduce_fusion = (bf16[768]{0:T(1024)(128)(2,1)S(1)}, bf16[768,512]{1,0:T(8,128)(2,1)S(1)}) fusion(f32[768,512]{1,0:T(8,128)S(1)} %fusion.1, bf16[768,4096]{1,0:T(8,128)(2,1)} %all-gather.3.cloned.1.call-done, bf16[1,4096,512]{2,1,0:T(8,128)(2,1)} %param.13), kind=kOutput, calls=%fused_computation.21 | convolution fusion | flops 3231055104 | bytes 12846592 | tf_op jit(solution)/shard_map/dot_general | solution.py:50
  119.2 0.0 copy-done.2
  119.2 5.1 %convolution_convert_fusion.3 = bf16[4096,512]{1,0:T(8,128)(2,1)} fusion(bf16[768,4096]{1,0:T(8,128)(2,1)S(1)} %copy-done.2, bf16[768,512]{1,0:T(8,128)(2,1)S(1)} %get-tuple-element.7), kind=kOutput, calls=%fused_computation.4 | convolution fusion | flops 3223322624 | bytes 11272192 | tf_op jit(solution)/shard_map/dot_general | solution.py:53
  124.3 0.0 reduce-scatter.3.cloned.1.call-update
  124.3 0.0 reduce-scatter.5.cloned.1.call-start
  124.3 8.2 %convolution_convert_fusion.2 = bf16[4096,512]{1,0:T(8,128)(2,1)} fusion(bf16[768,4096]{1,0:T(8,128)(2,1)} %all-gather.3.cloned.1.call-done, f32[768,512]{1,0:T(8,128)S(1)} %fusion.1), kind=kOutput, calls=%fused_computation.3 | convolution fusion | flops 3226861568 | bytes 12058624 | tf_op jit(solution)/shard_map/dot_general | solution.py:46
  132.5 0.0 reduce-scatter.5.cloned.1.call-update
  132.5 0.1 copy.14
  132.6 0.1 convert_element_type.87
  132.7 0.6 copy.16
  133.3 6.9 %all-to-all-start.1 = ((bf16[32,1,24]{2,1,0:T(2,128)(2,1)}), bf16[32,1,24]{2,1,0:T(2,128)(2,1)S(1)}, u32[]{:S(2)}, u32[]{:S(2)}) async-start(bf16[32,1,24]{2,1,0:T(2,128)(2,1)} %copy.16), calls=%async_computation.1 | async-start | bytes 32768 | tf_op jit(solution)/shard_map/all_to_all | solution.py:69
  140.2 7.6 %convolution_convert_fusion = bf16[768,4096]{1,0:T(8,128)(2,1)} fusion(bf16[768,512]{1,0:T(8,128)(2,1)S(1)} %bitcast.62, bf16[1,4096,512]{2,1,0:T(8,128)(2,1)} %param.12), kind=kOutput, calls=%fused_computation.1 | convolution fusion | flops 3224371200 | bytes 11272192 | tf_op jit(solution)/shard_map/dot_general | solution.py:62
  147.9 0.0 all-to-all-done.1
  147.9 7.3 %all-to-all-start = ((bf16[32,24,4096]{2,1,0:T(8,128)(2,1)}), bf16[32,24,4096]{2,1,0:T(8,128)(2,1)}, u32[]{:S(2)}, u32[]{:S(2)}) async-start(bf16[32,24,4096]{2,1,0:T(8,128)(2,1)} %bitcast.56), calls=%async_computation | async-start | bytes 12582912 | tf_op jit(solution)/shard_map/all_to_all | solution.py:66
  155.2 0.1 fusion.20
  155.3 0.6 compare_select_fusion
  156.0 77.1 %all-to-all-done = bf16[32,24,4096]{2,1,0:T(8,128)(2,1)} async-done(((bf16[32,24,4096]{2,1,0:T(8,128)(2,1)}), bf16[32,24,4096]{2,1,0:T(8,128)(2,1)}, u32[]{:S(2)}, u32[]{:S(2)}) %all-to-all-start) | async-done | bytes 6291488 | tf_op jit(solution)/shard_map/all_to_all | solution.py:66
  233.1 3.9 %convert_reduce_fusion = f32[2,24,4096]{2,1,0:T(8,128)S(1)} fusion(bf16[32,24,4096]{2,1,0:T(8,128)(2,1)} %all-to-all-done), kind=kLoop, calls=%fused_computation | loop fusion | flops 6094848 | bytes 7077888 | tf_op jit(solution)/shard_map/reduce_sum | solution.py:76
  237.0 0.1 fusion.15
  237.0 3.3 %convolution_convert_fusion.1 = bf16[512,4096]{1,0:T(8,128)(2,1)} fusion(bf16[48,4096]{1,0:T(8,128)(2,1)S(1)} %get-tuple-element.4, bf16[48,4096]{1,0:T(8,128)(2,1)S(1)} %get-tuple-element.5, bf16[48,512]{1,0:T(8,128)(2,1)S(1)} %fusion.20), kind=kOutput, calls=%fused_computation.2 | convolution fusion | flops 406519808 | bytes 5029888 | tf_op jit(solution)/shard_map/dot_general | solution.py:80
  240.3 0.0 reduce-scatter.3.cloned.1.call-done
  240.3 0.0 reduce-scatter.5.cloned.1.call-done
  (8 shorter events, 0.2 us)
Async XLA Ops:
  7.2 58.0 %all-gather.5.cloned.1.call-start = ((), (), s32[]{:S(2)}) async-start(), calls=%async_computation.5 | async-start | bytes 6684672 | tf_op jit(solution)/shard_map/all_gather | solution.py:37
  11.1 9.9 %copy-start = (s32[1,2]{1,0:T(1,128)S(1)}, s32[1,2]{1,0:T(1,128)}, u32[]{:S(2)}) copy-start(s32[1,2]{1,0:T(1,128)} %param.11) | copy-start | bytes 28
  11.1 10.0 %copy-start.1 = (bf16[1,2,24]{2,1,0:T(2,128)(2,1)S(1)}, bf16[1,2,24]{2,1,0:T(2,128)(2,1)}, u32[]{:S(2)}) copy-start(bf16[1,2,24]{2,1,0:T(2,128)(2,1)} %param.9) | copy-start | bytes 292
  11.1 8.9 %collective-permute-start.1 = (bf16[24,4096]{1,0:T(8,128)(2,1)S(1)}, bf16[24,4096]{1,0:T(8,128)(2,1)S(1)}, u32[]{:S(2)}, u32[]{:S(2)}) collective-permute-start(bf16[24,4096]{1,0:T(8,128)(2,1)S(1)} %dynamic-slice_bitcast_fusion), channel_id=1, source_target_pairs={{0,64},{64,0},{1,65},{65,1},{2,66},{66,2},{3,67},{67,3},{4,68},{68... | collective-permute-start | bytes 589832 | tf_op jit(solution)/shard_map/ppermute | solution.py:33
  20.9 89.7 %all-gather.3.cloned.1.call-start = ((), (), s32[]{:S(2)}) async-start(), calls=%async_computation.4 | async-start | bytes 6684672 | tf_op jit(solution)/shard_map/all_gather | solution.py:37
  24.3 7.7 %collective-permute-start = (bf16[24,4096]{1,0:T(8,128)(2,1)S(1)}, bf16[24,4096]{1,0:T(8,128)(2,1)S(1)}, u32[]{:S(2)}, u32[]{:S(2)}) collective-permute-start(bf16[24,4096]{1,0:T(8,128)(2,1)S(1)} %dynamic-slice_bitcast_fusion.1), channel_id=1, source_target_pairs={{0,64},{64,0},{1,65},{65,1},{2,66},{66,2},{3,67},{67,3},{4,68},{68... | collective-permute-start | bytes 589832 | tf_op jit(solution)/shard_map/ppermute | solution.py:33
  32.8 207.5 %reduce-scatter.3.cloned.1.call-start = ((), (), s32[]{:S(2)}) async-start(), calls=%async_computation.6 | async-start | bytes 5242880 | tf_op jit(solution)/shard_map/reduce_scatter | solution.py:56
  110.6 8.6 %copy-start.2 = (bf16[768,4096]{1,0:T(8,128)(2,1)S(1)}, bf16[768,4096]{1,0:T(8,128)(2,1)}, u32[]{:S(2)}) copy-start(bf16[768,4096]{1,0:T(8,128)(2,1)} %all-gather.5.cloned.1.call-done) | copy-start | bytes 18874372
  124.3 116.1 %reduce-scatter.5.cloned.1.call-start = ((), (), s32[]{:S(2)}) async-start(), calls=%async_computation.7 | async-start | bytes 5242880 | tf_op jit(solution)/shard_map/reduce_scatter | solution.py:49
  133.3 14.5 %all-to-all-start.1 = ((bf16[32,1,24]{2,1,0:T(2,128)(2,1)}), bf16[32,1,24]{2,1,0:T(2,128)(2,1)S(1)}, u32[]{:S(2)}, u32[]{:S(2)}) async-start(bf16[32,1,24]{2,1,0:T(2,128)(2,1)} %copy.16), calls=%async_computation.1 | async-start | bytes 32768 | tf_op jit(solution)/shard_map/all_to_all | solution.py:69
  147.9 85.2 %all-to-all-start = ((bf16[32,24,4096]{2,1,0:T(8,128)(2,1)}), bf16[32,24,4096]{2,1,0:T(8,128)(2,1)}, u32[]{:S(2)}, u32[]{:S(2)}) async-start(bf16[32,24,4096]{2,1,0:T(8,128)(2,1)} %bitcast.56), calls=%async_computation | async-start | bytes 12582912 | tf_op jit(solution)/shard_map/all_to_all | solution.py:66
Sparse Core Ops, SparseCore 0:
  21.0 44.0 all-gather.4
  67.4 43.1 all-gather.2
  124.4 47.6 reduce-scatter.2
  175.0 46.4 reduce-scatter.4

commit v2 on v1

v2 whole, which is shorter than its diff:
```python
import jax
import jax.numpy as jnp
from jax import lax
from jax.experimental import pallas as pl
from jax.experimental.pallas import tpu as pltpu
from jax.sharding import Mesh
from jax.sharding import PartitionSpec as P

F32 = jnp.float32
BF16 = jnp.bfloat16
UP = [(0, 1), (1, 2), (2, 3), (3, 0)]
DOWN = [(0, 3), (1, 0), (2, 1), (3, 2)]
PAIR = [(0, 1), (1, 0)]
X_OFFSETS = (0, 3, 1, 2)
LANES = 128
ROOT = 0.7978845608028654
CUBE = 0.044715
ANYWHERE = pl.BlockSpec(memory_space=pl.ANY)
IN_VMEM = pl.BlockSpec(memory_space=pltpu.VMEM)
IN_SMEM = pl.BlockSpec(memory_space=pltpu.SMEM)


def over_z(v, flip):
    return lax.ppermute(v, ("k", "zz"), [(i, i ^ flip) for i in range(4)])


def params(steps=0, mib=60):
    kind = ("arbitrary",) * steps if steps else None
    return pltpu.CompilerParams(vmem_limit_bytes=mib << 20, dimension_semantics=kind)


def rows_dot(a, b):
    return lax.dot_general(a, b, (((0,), (0,)), ((), ())), preferred_element_type=F32)


def pick_rows(tokens, out_grad, gates, picks, counts):
    t_dev, width = tokens.shape
    experts, slots = picks.shape
    chunk = 1024

    def body(place_ref, t_ref, g_ref, gate_ref, pick_ref, count_ref, mine_ref, other_ref, dy_ref):
        k = place_ref[0]

        def both(first, second):
            swap = k != 0
            return jnp.concatenate([jnp.where(swap, second, first), jnp.where(swap, first, second)], 1)

        gate = gate_ref[...].astype(F32)
        slot = lax.broadcasted_iota(jnp.int32, (1, slots), 1)
        scale = [jnp.where(slot < count_ref[0, e], gate[e : e + 1, :], 0.0) for e in range(2)]
        index = both(pick_ref[0:1, :], pick_ref[1:2, :])
        hit = lax.broadcasted_iota(jnp.int32, (t_dev, experts * slots), 0) == index
        picked = rows_dot(jnp.where(hit, 1.0, 0.0).astype(BF16), t_ref[...])
        mine_ref[...] = picked[:slots].astype(BF16)
        other_ref[...] = picked[slots:].astype(BF16)
        scaled = jnp.where(hit, both(*scale), 0.0).astype(BF16)
        dy_ref[...] = rows_dot(scaled, g_ref[...]).astype(BF16)

    columns = lambda i, *_: (0, i)
    fixed = lambda i, *_: (0, 0)
    return pl.pallas_call(
        body,
        grid_spec=pltpu.PrefetchScalarGridSpec(
            num_scalar_prefetch=1,
            grid=(width // chunk,),
            in_specs=[
                pl.BlockSpec((t_dev, chunk), columns),
                pl.BlockSpec((t_dev, chunk), columns),
                pl.BlockSpec((experts, slots), fixed),
                pl.BlockSpec((experts, slots), fixed),
                pl.BlockSpec((1, experts), fixed, memory_space=pltpu.SMEM),
            ],
            out_specs=[
                pl.BlockSpec((slots, chunk), columns),
                pl.BlockSpec((slots, chunk), columns),
                pl.BlockSpec((experts * slots, chunk), columns),
            ],
        ),
        out_shape=[
            jax.ShapeDtypeStruct((slots, width), BF16),
            jax.ShapeDtypeStruct((slots, width), BF16),
            jax.ShapeDtypeStruct((experts * slots, width), BF16),
        ],
        compiler_params=params(1, 60),
        name="pick_rows",
    )(lax.axis_index("k").reshape(1), tokens, out_grad, gates, picks, counts)


def stack_rows(groups, after=()):
    flat = [block for group in groups for block in group]
    slots = 24
    width = flat[0][0].shape[1]
    chunk = 2048
    n = len(flat)

    def body(*refs):
        place = 0
        for out_ref, group in zip(refs[n + len(after) :], groups):
            rows = []
            for _, first in group:
                rows.append(refs[place][...].astype(F32)[first : first + slots])
                place += 1
            out_ref[...] = jnp.concatenate(rows, 0).astype(BF16)

    return pl.pallas_call(
        body,
        grid=(width // chunk,),
        in_specs=[pl.BlockSpec((v.shape[0], chunk), lambda i: (0, i)) for v, _ in flat]
        + [ANYWHERE] * len(after),
        out_specs=[pl.BlockSpec((slots * len(g), chunk), lambda i: (0, i)) for g in groups],
        out_shape=[jax.ShapeDtypeStruct((slots * len(g), width), BF16) for g in groups],
        compiler_params=params(1, 16),
        name="stack_rows",
    )(*[v for v, _ in flat], *after)


def gate_lanes(gate_sum):
    lane = lax.broadcasted_iota(jnp.int32, gate_sum.shape, 1)
    high = gate_sum.astype(BF16).astype(F32)
    return jnp.where(lane == 0, high, jnp.where(lane == 1, gate_sum - high, 0.0))


def hidden_pass(rows_x, weight, slots):
    count, width = rows_x.shape
    units = weight.shape[1]
    steps = 4
    chunk = width // steps

    def body(place_ref, x_hbm, w_hbm, hidden_ref, slope_ref, x_v, w_v, pre, hid, sems):
        copies = []
        for i in range(steps):
            span = pl.ds(i * chunk, chunk)
            group = [
                pltpu.make_async_copy(x_hbm.at[:, span], x_v.at[:, span], sems.at[i, 0]),
                pltpu.make_async_copy(w_hbm.at[span, :], w_v.at[span, :], sems.at[i, 1]),
            ]
            for copy in group:
                copy.start()
            copies.append(group)
        for i in range(steps):
            span = pl.ds(i * chunk, chunk)
            for copy in copies[i]:
                copy.wait()
            part = jnp.dot(x_v[:, span], w_v[span, :], preferred_element_type=F32)
            if i == 0:
                pre[...] = part
            else:
                pre[...] += part

        core = place_ref[0]
        me_x = place_ref[1]

        @pl.loop(0, 4)
        def _(z):
            for step_x in range(4):
                x = (me_x + X_OFFSETS[step_x]) % 4
                for from_core in range(2):
                    source = ((x * 2 + (core ^ from_core)) * 4 + z) * slots
                    v = pre[pl.ds(pl.multiple_of(source, 8), slots), :]
                    here = ((z * 2 + from_core) * 4 + step_x) * slots
                    here = pl.ds(pl.multiple_of(here, 8), slots)
                    t = jnp.tanh(ROOT * (v + CUBE * (v * v * v)))
                    cdf = 0.5 * (1.0 + t)
                    hid[here, :] = v * cdf
                    slope_ref[here, :] = cdf + 0.5 * v * (1.0 - t * t) * (
                        ROOT * (1.0 + 3.0 * CUBE * (v * v))
                    )

        hidden_ref[...] = hid[...].astype(BF16)

    return pl.pallas_call(
        body,
        in_specs=[IN_SMEM, ANYWHERE, ANYWHERE],
        out_specs=[IN_VMEM] * 2,
        out_shape=[
            jax.ShapeDtypeStruct((count, units), BF16),
            jax.ShapeDtypeStruct((count, units), F32),
        ],
        scratch_shapes=[
            pltpu.VMEM((count, width), BF16),
            pltpu.VMEM((width, units), BF16),
            pltpu.VMEM((count, units), F32),
            pltpu.VMEM((count, units), F32),
            pltpu.SemaphoreType.DMA((steps, 2)),
        ],
        compiler_params=params(),
        name="hidden_pass",
    )(jnp.stack([lax.axis_index("c"), lax.axis_index("x")]), rows_x, weight)


def core_pass(rows_x, hidden, slope, pieces, weight_in, weight_out, slots):
    count, width = rows_x.shape
    units = weight_in.shape[1]
    steps = 4
    chunk = width // steps
    piece = width // 8
    parts = len(pieces)
    part_rows = count // parts

    def body(place_ref, hidden_ref, slope_ref, x_hbm, *refs):
        piece_refs = refs[:parts]
        w1_hbm, w2_hbm = refs[parts : parts + 2]
        pre_x_ref, dy_out, row_out, far_up, far_down = refs[parts + 2 : parts + 7]
        (
            x_v, dy_v, w1_v, w2_v, grad, pre_x, pre_home, gate_home, pre_b, row_v, up_v, down_v, sems, late_sems, out_sems,
        ) = refs[parts + 7 :]
        core = place_ref[0]
        spot = place_ref[1]
        dp = place_ref[2]
        me_x = place_ref[3]
        far = pl.multiple_of(((dp + 2) % 4) * 2 * piece, LANES)
        copies = []
        for i in range(steps):
            span = pl.ds(i * chunk, chunk)
            group = [(w2_hbm.at[span, :], w2_v.at[span, :])] + [
                (ref.at[:, span], dy_v.at[pl.ds(j * part_rows, part_rows), span])
                for j, ref in enumerate(piece_refs)
            ]
            group = [
                pltpu.make_async_copy(src, dst, sems.at[i, j]) for j, (src, dst) in enumerate(group)
            ]
            for copy in group:
                copy.start()
            copies.append(group)
        late = [
            pltpu.make_async_copy(x_hbm.at[:, pl.ds(far, 2 * piece)], x_v, late_sems.at[0]),
            pltpu.make_async_copy(w1_hbm, w1_v, late_sems.at[1]),
        ]
        for copy in late:
            copy.start()
        for i in range(steps):
            span = pl.ds(i * chunk, chunk)
            for copy in copies[i]:
                copy.wait()
            part = jnp.dot(dy_v[:, span], w2_v[span, :], preferred_element_type=F32)
            if i == 0:
                grad[...] = part
            else:
                grad[...] += part
        outs = [pltpu.make_async_copy(dy_v, dy_out, out_sems.at[0])]
        outs[0].start()

        @pl.loop(0, 4)
        def _(z):
            home_z = z ^ spot
            for step_x in range(4):
                x = (me_x + X_OFFSETS[step_x]) % 4
                for from_core in range(2):
                    home = (((home_z % 2) * 4 + x) * 2 + (core ^ from_core)) * 2 + home_z // 2
                    home = pl.ds(pl.multiple_of(home * slots, 8), slots)
                    source = ((x * 2 + (core ^ from_core)) * 4 + z) * slots
                    there = pl.ds(pl.multiple_of(source, 8), slots)
                    here = ((z * 2 + from_core) * 4 + step_x) * slots
                    here = pl.ds(pl.multiple_of(here, 8), slots)
                    p = grad[here, :] * slope_ref[here, :]
                    pre_home[home, :] = p
                    pre_x[there, :] = p

        for i in range(4):
            span = pl.ds(i * (count // 4), count // 4)
            grad[span, :] = grad[span, :] * hidden_ref[span, :].astype(F32)

        @pl.loop(0, 4)
        def _(z):
            home_z = z ^ spot
            for step_x in range(4):
                x = (me_x + X_OFFSETS[step_x]) % 4
                for from_core in range(2):
                    home = (((home_z % 2) * 4 + x) * 2 + (core ^ from_core)) * 2 + home_z // 2
                    home = pl.ds(pl.multiple_of(home * slots, 8), slots)
                    here = ((z * 2 + from_core) * 4 + step_x) * slots
                    here = pl.ds(pl.multiple_of(here, 8), slots)
                    gate_home[home, :] = jnp.broadcast_to(
                        jnp.sum(grad[here, :], -1, keepdims=True), (slots, LANES)
                    )

        pre_x_ref[...] = pre_x[...].astype(BF16)
        pre_b[...] = pre_home[...].astype(BF16)
        late[0].wait()
        for side, buffer, out in ((0, up_v, far_up), (1, down_v, far_down)):
            cols = pl.ds(pl.multiple_of(far + side * piece, LANES), piece)
            buffer[:piece, :] = rows_dot(x_v[:, side * piece : (side + 1) * piece], pre_x_ref[...]).astype(BF16)
            buffer[piece:, :] = rows_dot(dy_v[:, cols], hidden_ref[...]).astype(BF16)
            outs.append(pltpu.make_async_copy(buffer, out, out_sems.at[1 + side]))
            outs[-1].start()
        late[1].wait()
        row_v[:, width:] = gate_lanes(gate_home[...]).astype(BF16)
        for i in range(steps):
            span = pl.ds(i * chunk, chunk)
            row_v[:, span] = lax.dot_general(
                pre_b[...], w1_v[span, :], (((1,), (1,)), ((), ())), preferred_element_type=F32
            ).astype(BF16)
            if i == steps - 1:
                span = pl.ds(i * chunk, chunk + LANES)
            outs.append(pltpu.make_async_copy(row_v.at[:, span], row_out.at[:, span], out_sems.at[3 + i]))
            outs[-1].start()
        for copy in outs:
            copy.wait()

    place = jnp.stack(
        [
            lax.axis_index("c"),
            lax.axis_index("k") * 2 + lax.axis_index("zz"),
            lax.axis_index("dp"),
            lax.axis_index("x"),
        ]
    )
    return pl.pallas_call(
        body,
        in_specs=[IN_SMEM, IN_VMEM, IN_VMEM] + [ANYWHERE] * (3 + parts),
        out_specs=[IN_VMEM] + [ANYWHERE] * 4,
        out_shape=[
            jax.ShapeDtypeStruct((count, units), BF16),
            jax.ShapeDtypeStruct((count, width), BF16),
            jax.ShapeDtypeStruct((count, width + LANES), BF16),
            jax.ShapeDtypeStruct((2 * piece, units), BF16),
            jax.ShapeDtypeStruct((2 * piece, units), BF16),
        ],
        scratch_shapes=[
            pltpu.VMEM((count, 2 * piece), BF16),
            pltpu.VMEM((count, width), BF16),
            pltpu.VMEM((width, units), BF16),
            pltpu.VMEM((width, units), BF16),
            pltpu.VMEM((count, units), F32),
            pltpu.VMEM((count, units), F32),
            pltpu.VMEM((count, units), F32),
            pltpu.VMEM((count, LANES), F32),
            pltpu.VMEM((count, units), BF16),
            pltpu.VMEM((count, width + LANES), BF16),
            pltpu.VMEM((2 * piece, units), BF16),
            pltpu.VMEM((2 * piece, units), BF16),
            pltpu.SemaphoreType.DMA((steps, 1 + parts)),
            pltpu.SemaphoreType.DMA((2,)),
            pltpu.SemaphoreType.DMA((3 + steps,)),
        ],
        compiler_params=params(),
        name="core_pass",
    )(place, hidden, slope, rows_x, *pieces, weight_in, weight_out)


def slice_grads(lefts, rights, jobs, extras, out_count, kind=BF16, after=()):
    count, width = lefts[0].shape
    units = rights[0].shape[1]
    piece = width // 8
    n = len(extras)

    def body(place_ref, x_hbm, dy_hbm, *refs):
        right_refs = refs[:2]
        extra_refs = refs[2 : 2 + n]
        outs = refs[2 + n + len(after) :][:out_count]
        buffers, sems = refs[-2:]
        copies = []
        for i, (m, shift, side, _, _, _) in enumerate(jobs):
            start = ((place_ref[0] + shift) % 4) * 2 * piece + side * piece
            cols = pl.ds(pl.multiple_of(start, LANES), piece)
            copies.append(
                pltpu.make_async_copy((x_hbm, dy_hbm)[m].at[:, cols], buffers.at[i], sems.at[i])
            )
            copies[-1].start()
        for i, (m, _, _, out, row, adds) in enumerate(jobs):
            copies[i].wait()
            part = rows_dot(buffers[i], right_refs[m][...])
            for index, first in adds:
                part += extra_refs[index][first : first + piece, :].astype(F32)
            outs[out][row : row + piece, :] = part.astype(kind)

    return pl.pallas_call(
        body,
        in_specs=[IN_SMEM, ANYWHERE, ANYWHERE] + [IN_VMEM] * (2 + n) + [ANYWHERE] * len(after),
        out_specs=[IN_VMEM] * out_count,
        out_shape=[jax.ShapeDtypeStruct((2 * piece, units), kind)] * out_count,
        scratch_shapes=[
            pltpu.VMEM((len(jobs), count, piece), BF16),
            pltpu.SemaphoreType.DMA((len(jobs),)),
        ],
        compiler_params=params(),
        name="slice_grads",
    )(lax.axis_index("dp").reshape(1), *lefts, *rights, *extras, *after)


def add_up(own_in, own_out, near_up, near_down, sum_up, sum_down):
    rows, units = own_in.shape
    half = rows // 2

    def body(in_ref, out_ref, near_up_ref, near_down_ref, sum_up_ref, sum_down_ref, *results):
        side = pl.program_id(0)
        for m, (own, result) in enumerate(zip((in_ref, out_ref), results)):
            span = slice(m * half, (m + 1) * half)

            @pl.when(side == 0)
            def _():
                total = own[...] + near_down_ref[span, :].astype(F32) + sum_up_ref[span, :].astype(F32)
                result[...] = total.astype(BF16)

            @pl.when(side == 1)
            def _():
                total = own[...] + near_up_ref[span, :].astype(F32) + sum_down_ref[span, :].astype(F32)
                result[...] = total.astype(BF16)

    own_spec = pl.BlockSpec((half, units), lambda i: (i, 0))
    full = pl.BlockSpec((rows, units), lambda i: (0, 0))
    return pl.pallas_call(
        body,
        grid=(2,),
        in_specs=[own_spec, own_spec] + [full] * 4,
        out_specs=[own_spec, own_spec],
        out_shape=[jax.ShapeDtypeStruct((rows, units), BF16)] * 2,
        compiler_params=params(1),
        name="add_up",
    )(own_in, own_out, near_up, near_down, sum_up, sum_down)


def unpick(got, swapped, picks, t_dev, width):
    chunk = 1024
    experts, slots = picks.shape

    def body(place_ref, got_ref, swapped_ref, pick_ref, out_ref):
        k = place_ref[0]
        got = got_ref[...].astype(F32)
        mine = jnp.where(k == 0, got[:slots], got[slots:])
        values = jnp.concatenate([mine, swapped_ref[...].astype(F32)], 0).astype(BF16)
        index = pick_ref[...]
        index = jnp.concatenate(
            [jnp.where(k == 0, index[i : i + 1], index[1 - i : 2 - i]) for i in range(2)], 1
        )
        row = lax.broadcasted_iota(jnp.int32, (t_dev, experts * slots), 0)
        hit = jnp.where(row == index, 1.0, 0.0).astype(BF16)
        out_ref[...] = jnp.dot(hit, values, preferred_element_type=F32).astype(BF16)

    return pl.pallas_call(
        body,
        grid_spec=pltpu.PrefetchScalarGridSpec(
            num_scalar_prefetch=1,
            grid=(width // chunk,),
            in_specs=[
                pl.BlockSpec((experts * slots, chunk), lambda i, *_: (0, i)),
                pl.BlockSpec((slots, chunk), lambda i, *_: (0, i)),
                pl.BlockSpec((experts, slots), lambda i, *_: (0, 0)),
            ],
            out_specs=pl.BlockSpec((t_dev, chunk), lambda i, *_: (0, i)),
        ),
        out_shape=jax.ShapeDtypeStruct((t_dev, width), BF16),
        compiler_params=params(1),
        name="unpick",
    )(lax.axis_index("k").reshape(1), got, swapped, picks)


def local(tokens, out_grad, gates, picks, counts, w_in, w_out):
    t_dev, width = tokens.shape
    experts, slots = picks.shape[1:]
    weight_in = w_in[0]
    weight_out = w_out[0]
    k = lax.axis_index("k")
    mine, other, both_dy = pick_rows(tokens, out_grad, gates[0], picks[0], counts)

    below = lax.ppermute(both_dy, "x", UP)
    above = lax.ppermute(both_dy, "x", DOWN)
    pass_mine, pass_other = stack_rows([[(below, 0)], [(above, slots)]])
    far_mine = lax.ppermute(pass_mine, "x", UP)
    far_other = lax.ppermute(pass_other, "x", DOWN)
    z_blocks = [mine, over_z(mine, 1), over_z(other, 2), over_z(other, 3)]
    (z_rows,) = stack_rows([[(v, 0) for v in z_blocks]], (pass_mine, pass_other))
    rows_x = lax.all_gather(z_rows, ("x", "c"), axis=0, tiled=True)

    x_mine, x_other = stack_rows(
        [
            [(both_dy, 0), (below, 0), (above, 0), (far_mine, 0)],
            [(both_dy, slots), (below, slots), (above, slots), (far_other, 0)],
        ]
    )
    pieces = []
    for block in (x_mine, over_z(x_mine, 1), over_z(x_other, 2), over_z(x_other, 3)):
        pieces += [block, lax.ppermute(block, "c", PAIR)]

    hidden, slope = hidden_pass(rows_x, weight_in, slots)
    pre_x, rows_dy, payload, far_up, far_down = core_pass(
        rows_x, hidden, slope, pieces, weight_in, weight_out, slots
    )
    lefts, rights = (rows_x, rows_dy), (pre_x, hidden)
    half = width // 8
    far_up = lax.ppermute(far_up, "dp", UP)
    far_down = lax.ppermute(far_down, "dp", DOWN)
    near_up, near_down = slice_grads(
        lefts,
        rights,
        [(m, s, side, out, m * half, ()) for s, side, out in ((1, 1, 0), (3, 0, 1)) for m in range(2)],
        (),
        2,
    )
    near_up = lax.ppermute(near_up, "dp", UP)
    near_down = lax.ppermute(near_down, "dp", DOWN)
    got = lax.psum_scatter(payload, ("zz", "x", "c"), scatter_dimension=0, tiled=True)
    own_in, own_out = slice_grads(
        lefts,
        rights,
        [(m, 0, side, m, side * half, ()) for m in range(2) for side in range(2)],
        (),
        2,
        F32,
    )
    sum_up, sum_down = slice_grads(
        lefts,
        rights,
        [
            (m, s, side, out, m * half, ((out, m * half),))
            for s, side, out in ((1, 0, 0), (3, 1, 1))
            for m in range(2)
        ],
        (far_up, far_down),
        2,
        after=(own_in,),
    )
    sum_up = lax.ppermute(sum_up, "dp", UP)
    sum_down = lax.ppermute(sum_down, "dp", DOWN)
    send = lax.dynamic_slice_in_dim(got, (1 - k) * slots, slots, 0)
    swapped = lax.ppermute(send, "k", PAIR)
    tokens_grad = unpick(got, swapped, picks[0], t_dev, width)
    w_in_grad, w_out_grad = add_up(
        own_in, own_out, near_up, near_down, sum_up, sum_down
    )
    keep = lax.dynamic_slice_in_dim(got, k * slots, slots, 0)[:, width : width + 2].astype(F32)
    gate_sum = jnp.stack([jnp.sum(keep, -1), jnp.sum(swapped[:, width : width + 2].astype(F32), -1)])
    gate_sum = jnp.where(k == 0, gate_sum, gate_sum[::-1])
    live = jnp.arange(slots)[None, :] < counts[0][:, None]
    gates_grad = jnp.where(live, gate_sum / gates[0].astype(F32), jnp.zeros_like(gate_sum))
    return (tokens_grad, gates_grad[None], w_in_grad[None], w_out_grad[None])


def solution(mesh):
    dp = mesh.devices.shape[1]
    fine = Mesh(mesh.devices.reshape(2, 2, 4, 2, dp), ("k", "zz", "x", "c", "dp"))
    expert = ("k", "zz", "x", "c")
    rows = expert + ("dp",)
    placed = (
        P(rows, None),
        P(rows, None),
        P(rows, None, None),
        P(rows, None, None),
        P(rows, None),
        P(expert, None, None),
        P(expert, None, None),
    )
    return jax.shard_map(
        local,
        mesh=fine,
        in_specs=placed,
        out_specs=(
            P(rows, None),
            P(rows, None, None),
            P(expert, "dp", None),
            P(expert, "dp", None),
        ),
        check_vma=False,
    )
```

time: 247 us -> 203 us (0.82)
  waiting for transfers between devices: 157 us -> 89.7 us
  Pallas kernels: 0 us -> 60.2 us
  matrix products: 45.6 us -> 0 us
  starting transfers between devices: 21.8 us -> 29.8 us
  local copies, waits for them, and re-layouts: 1.76 us -> 5 us
  other arithmetic: 6.39 us -> 3.53 us
    all_to_all x2 -> x0, waiting for transfers between devices: 77.1 us -> none  [the longest x1 77.1 us: local(): lax.all_to_all(row_part.reshape(2 * parts, slots, width), ('k',) + GROUP,...]
    all_gather x2 -> x1, waiting for transfers between devices: 71 us -> 0.01 us  [local(): rows_x = lax.all_gather(z_rows, ('x', 'c'), axis=0, tiled=True)]
    pallas_call x0 -> x11, Pallas kernels: none -> 60.2 us  [the longest x3 18.9 us: slice_grads(): pl.pallas_call(body, in_specs=[IN_SMEM, ANYWHERE, ANYWHERE] + [IN_VMEM] *...]
    ppermute x2 -> x21, waiting for transfers between devices: 9.25 us -> 55.6 us  [the longest x6 39.3 us: over_z(): return lax.ppermute(v, ('k', 'zz'), [(i, i ^ flip) for i in range(4)])]
    dot_general x8 -> x0, matrix products: 45.6 us -> none  [the longest x1 8.58 us: local(): hidden_grad = jnp.dot(rows_dy, weight_out, preferred_element_type=F32)]
    reduce_scatter x2 -> x1, waiting for transfers between devices: 0.01 us -> 34.1 us  [local(): lax.psum_scatter(payload, ('zz', 'x', 'c'), scatter_dimension=0, tiled=True)]
    ppermute x2 -> x21, starting transfers between devices: 7.36 us -> 29.7 us  [the longest x6 10.4 us: over_z(): return lax.ppermute(v, ('k', 'zz'), [(i, i ^ flip) for i in range(4)])]
    all_to_all x2 -> x0, starting transfers between devices: 14.2 us -> none  [the longest x1 7.33 us: local(): lax.all_to_all(row_part.reshape(2 * parts, slots, width), ('k',) + GROUP,...]
  transfers between devices with their start and end apart: 8 -> 23, of which waited for: 5 -> 11; matrix products, arithmetic and copies ran while one was open for 14% -> 2% of each run, Pallas kernels for 0% -> 16%
where the time goes in v2:
time: 203 us
  waiting for transfers between devices  89.7 us (44%)
  Pallas kernels  60.2 us (30%)
  starting transfers between devices  29.8 us (15%)
  between operations  14.3 us (7%)
  local copies, waits for them, and re-layouts  5 us (2%)
  other arithmetic  3.53 us (2%)
    ppermute x6, waiting for transfers between devices, over_z(): return lax.ppermute(v, ('k', 'zz'), [(i, i ^ flip) for i in range(4)])  39.3 us
    reduce_scatter x1, waiting for transfers between devices, local(): lax.psum_scatter(payload, ('zz', 'x', 'c'), scatter_dimension=0, tiled=True)  34.1 us
    pallas_call x3, Pallas kernels, slice_grads(): pl.pallas_call(body, in_specs=[IN_SMEM, ANYWHERE, ANYWHERE] + [IN_VMEM] *...  18.9 us
    pallas_call x1, Pallas kernels, core_pass(): pl.pallas_call(body, in_specs=[IN_SMEM, IN_VMEM, IN_VMEM] + [ANYWHERE] *...  15.9 us
    ppermute x6, starting transfers between devices, over_z(): return lax.ppermute(v, ('k', 'zz'), [(i, i ^ flip) for i in range(4)])  10.4 us
    pallas_call x1, Pallas kernels, hidden_pass(): pl.pallas_call(body, in_specs=[IN_SMEM, ANYWHERE, ANYWHERE], out_specs=[I...  8.56 us
    ppermute x1, waiting for transfers between devices, local(): far_up = lax.ppermute(far_up, 'dp', UP)  8.52 us
    pallas_call x1, Pallas kernels, pick_rows(): pl.pallas_call(body, grid_spec=pltpu.PrefetchScalarGridSpec(num_scalar_pr...  5.84 us
  transfers between devices with their start and end apart: 23, of which 11 were waited for; matrix products, arithmetic and copies ran while one was open for 2% of the time, Pallas kernels for 16%

profile of v2, /device:TPU:0, one launch (start us, length us, event | category | flops | bytes accessed | tf_op | source)
XLA Modules:
  0.0 202.5 jit_solution(5936926105010710150)
XLA Ops:
  7.2 0.0 all-gather.2.cloned.1.call-start
  7.2 5.8 %pick_rows.1 = (bf16[24,4096]{1,0:T(8,128)(2,1)}, bf16[24,4096]{1,0:T(8,128)(2,1)}, bf16[48,4096]{1,0:T(8,128)(2,1)}) custom-call(s32[1]{0:T(128)} %bitcast.place_ref, bf16[512,4096]{1,0:T(8,128)(2,1)} %t_ref.1, bf16[512,4096]{1,0:T(8,128)(2,1)} %g_ref.1, bf16[2,24]{1,0:T(2,128)(2,1)} %bitcast.26, s32[2,24]{1,0:T(2,128)} %bitcast.24, s32[1,2]{1,0:T(1,128)} %count_ref.1), custom_call_target="tpu_custom_call" | custom-call | tf_op jit(solution)/shard_map/pick_rows/pallas_call | solution.py:61
  13.1 1.6 collective-permute-start.3
  14.6 1.7 collective-permute-start.4
  16.3 2.0 collective-permute-start
  18.3 3.6 %collective-permute-start.1 = (bf16[24,4096]{1,0:T(8,128)(2,1)}, bf16[24,4096]{1,0:T(8,128)(2,1)S(1)}, u32[]{:S(2)}, u32[]{:S(2)}) collective-permute-start(bf16[24,4096]{1,0:T(8,128)(2,1)} %get-tuple-element.27), channel_id=1, source_target_pairs={{0,64},{32,96},{64,0},{96,32},{1,65},{33,97},{65,1},{97,33},{2,66}... | collective-permute-start | bytes 589832 | tf_op jit(solution)/shard_map/ppermute | solution.py:24
  21.9 0.0 collective-permute-start.2
  21.9 3.3 %collective-permute-done.3.refs_0_.refs_1_.refs_5_ = bf16[48,4096]{1,0:T(8,128)(2,1)S(1)} collective-permute-done((bf16[48,4096]{1,0:T(8,128)(2,1)}, bf16[48,4096]{1,0:T(8,128)(2,1)S(1)}, u32[]{:S(2)}, u32[]{:S(2)}) %collective-permute-start.3) | collective-permute-done | bytes 393248 | tf_op jit(solution)/shard_map/ppermute | solution.py:456
  25.2 0.2 collective-permute-done.4.refs_1_.refs_2_.refs_6_
  25.4 0.2 stack_rows.3
  25.6 0.0 collective-permute-done.refs_1_
  25.6 4.9 %collective-permute-done.1.refs_2_ = bf16[24,4096]{1,0:T(8,128)(2,1)S(1)} collective-permute-done((bf16[24,4096]{1,0:T(8,128)(2,1)}, bf16[24,4096]{1,0:T(8,128)(2,1)S(1)}, u32[]{:S(2)}, u32[]{:S(2)}) %collective-permute-start.1) | collective-permute-done | bytes 196640 | tf_op jit(solution)/shard_map/ppermute | solution.py:24
  30.5 2.5 %collective-permute-done.2.refs_3_ = bf16[24,4096]{1,0:T(8,128)(2,1)S(1)} collective-permute-done((bf16[24,4096]{1,0:T(8,128)(2,1)}, bf16[24,4096]{1,0:T(8,128)(2,1)S(1)}, u32[]{:S(2)}, u32[]{:S(2)}) %collective-permute-start.2) | collective-permute-done | bytes 196640 | tf_op jit(solution)/shard_map/ppermute | solution.py:24
  32.9 0.9 copy-done.2
  33.9 1.0 stack_rows.4
  34.8 0.0 all-gather.2.cloned.1.call-update
  34.9 0.0 reduce-scatter.2.cloned.1.call-start
  34.9 0.3 collective-permute-start.5
  35.3 3.0 %collective-permute-start.6 = (bf16[24,4096]{1,0:T(8,128)(2,1)S(1)}, bf16[24,4096]{1,0:T(8,128)(2,1)S(1)}, u32[]{:S(2)}, u32[]{:S(2)}) collective-permute-start(bf16[24,4096]{1,0:T(8,128)(2,1)S(1)} %get-tuple-element.30.refs_5_), channel_id=1, source_target_pairs={{0,24},{8,0},{16,8},{24,16},{1,25},{9,1},{17,9},{25,17},{2,26},{10... | collective-permute-start | bytes 589832 | tf_op jit(solution)/shard_map/ppermute | solution.py:460
  38.2 3.7 %collective-permute-done.5.refs_3_ = bf16[24,4096]{1,0:T(8,128)(2,1)S(1)} collective-permute-done((bf16[24,4096]{1,0:T(8,128)(2,1)S(1)}, bf16[24,4096]{1,0:T(8,128)(2,1)S(1)}, u32[]{:S(2)}, u32[]{:S(2)}) %collective-permute-start.5) | collective-permute-done | bytes 196640 | tf_op jit(solution)/shard_map/ppermute | solution.py:459
  41.9 0.0 collective-permute-done.6.refs_7_
  41.9 1.0 copy-done
  43.0 0.5 stack_rows.5
  43.5 0.1 collective-permute-start.8
  43.6 1.6 collective-permute-start.10
  45.1 3.1 %collective-permute-start.12 = (bf16[96,4096]{1,0:T(8,128)(2,1)S(1)}, bf16[96,4096]{1,0:T(8,128)(2,1)S(1)}, u32[]{:S(2)}, u32[]{:S(2)}) collective-permute-start(bf16[96,4096]{1,0:T(8,128)(2,1)S(1)} %get-tuple-element.34), channel_id=1, source_target_pairs={{0,96},{32,64},{64,32},{96,0},{1,97},{33,65},{65,33},{97,1},{2,98}... | collective-permute-start | bytes 2359304 | tf_op jit(solution)/shard_map/ppermute | solution.py:24
  48.2 0.0 collective-permute-start.7
  48.2 15.8 %collective-permute-done.8.refs_2_ = bf16[96,4096]{1,0:T(8,128)(2,1)S(1)} collective-permute-done((bf16[96,4096]{1,0:T(8,128)(2,1)S(1)}, bf16[96,4096]{1,0:T(8,128)(2,1)S(1)}, u32[]{:S(2)}, u32[]{:S(2)}) %collective-permute-start.8) | collective-permute-done | bytes 786464 | tf_op jit(solution)/shard_map/ppermute | solution.py:24
  64.0 13.6 %collective-permute-done.10.refs_4_ = bf16[96,4096]{1,0:T(8,128)(2,1)S(1)} collective-permute-done((bf16[96,4096]{1,0:T(8,128)(2,1)S(1)}, bf16[96,4096]{1,0:T(8,128)(2,1)S(1)}, u32[]{:S(2)}, u32[]{:S(2)}) %collective-permute-start.10) | collective-permute-done | bytes 786464 | tf_op jit(solution)/shard_map/ppermute | solution.py:24
  77.7 0.0 collective-permute-start.11
  77.7 2.6 %collective-permute-done.12.refs_6_ = bf16[96,4096]{1,0:T(8,128)(2,1)S(1)} collective-permute-done((bf16[96,4096]{1,0:T(8,128)(2,1)S(1)}, bf16[96,4096]{1,0:T(8,128)(2,1)S(1)}, u32[]{:S(2)}, u32[]{:S(2)}) %collective-permute-start.12) | collective-permute-done | bytes 786464 | tf_op jit(solution)/shard_map/ppermute | solution.py:24
  80.2 0.0 collective-permute-start.13
  80.2 0.7 pad_add_fusion.1.place_ref
  80.9 0.6 pad_add_fusion.place_ref
  81.5 8.6 %hidden_pass.1 = (bf16[768,512]{1,0:T(8,128)(2,1)}, f32[768,512]{1,0:T(8,128)}) custom-call(s32[2]{0:T(128)} %pad_add_fusion.1.place_ref, bf16[768,4096]{1,0:T(8,128)(2,1)} %all-gather.2.cloned.1.call-done.x_hbm, bf16[4096,512]{1,0:T(8,128)(2,1)} %bitcast.17), custom_call_target="tpu_custom_call" | custom-call | tf_op jit(solution)/shard_map/hidden_pass/pallas_call | solution.py:171
  90.1 0.0 collective-permute-done.7.refs_1_
  90.2 0.0 collective-permute-done.9.refs_3_
  90.2 0.0 collective-permute-done.13.refs_7_
  90.2 15.9 %core_pass.1 = (bf16[768,512]{1,0:T(8,128)(2,1)}, bf16[768,4096]{1,0:T(8,128)(2,1)}, bf16[768,4224]{1,0:T(8,128)(2,1)}, bf16[1024,512]{1,0:T(8,128)(2,1)}, bf16[1024,512]{1,0:T(8,128)(2,1)}) custom-call(s32[4]{0:T(128)} %pad_add_fusion.place_ref, bf16[768,512]{1,0:T(8,128)(2,1)} %get-tuple-element.31.hidden_ref.refs_1_, ...), custom_call_target="tpu_custom_call" | custom-call | tf_op jit(solution)/shard_map/core_pass/pallas_call | solution.py:308
  106.1 0.0 reduce-scatter.2.cloned.1.call-update
  106.1 1.6 collective-permute-start.17
  107.7 1.7 collective-permute-start.18
  109.4 5.9 %slice_grads.4 = (bf16[1024,512]{1,0:T(8,128)(2,1)}, bf16[1024,512]{1,0:T(8,128)(2,1)}) custom-call(s32[1]{0:T(128)} %bitcast.3.place_ref, bf16[768,4096]{1,0:T(8,128)(2,1)} %all-gather.2.cloned.1.call-done.x_hbm, bf16[768,4096]{1,0:T(8,128)(2,1)} %get-tuple-element.36.dy_hbm, bf16[768,512]{1,0:T(8,128)(2,1)} %get-tuple-element.37.refs_0_, ...), custom_call_target="tpu_custom_call" | custom-call | tf_op jit(solution)/shard_map/slice_grads/pallas_call | solution.py:367
  115.3 0.4 collective-permute-start.15
  115.8 2.9 %collective-permute-start.16 = (bf16[1024,512]{1,0:T(8,128)(2,1)}, bf16[1024,512]{1,0:T(8,128)(2,1)S(1)}, u32[]{:S(2)}, u32[]{:S(2)}) collective-permute-start(bf16[1024,512]{1,0:T(8,128)(2,1)} %get-tuple-element.41), channel_id=1, source_target_pairs={{0,3},{1,0},{2,1},{3,2},{4,7},{5,4},{6,5},{7,6},{8,11},{9,8},{10,9... | collective-permute-start | bytes 3145736 | tf_op jit(solution)/shard_map/ppermute | solution.py:491
  118.6 6.4 %slice_grads.3 = (f32[1024,512]{1,0:T(8,128)}, f32[1024,512]{1,0:T(8,128)}) custom-call(s32[1]{0:T(128)} %bitcast.3.place_ref, bf16[768,4096]{1,0:T(8,128)(2,1)} %all-gather.2.cloned.1.call-done.x_hbm, bf16[768,4096]{1,0:T(8,128)(2,1)} %get-tuple-element.36.dy_hbm, bf16[768,512]{1,0:T(8,128)(2,1)} %get-tuple-element.37.refs_0_, ...), custom_call_target="tpu_custom_call" | custom-call | tf_op jit(solution)/shard_map/slice_grads/pallas_call | solution.py:367
  125.0 8.5 %collective-permute-done.17.refs_2_ = bf16[1024,512]{1,0:T(8,128)(2,1)S(1)} collective-permute-done((bf16[1024,512]{1,0:T(8,128)(2,1)}, bf16[1024,512]{1,0:T(8,128)(2,1)S(1)}, u32[]{:S(2)}, u32[]{:S(2)}) %collective-permute-start.17) | collective-permute-done | bytes 1048608 | tf_op jit(solution)/shard_map/ppermute | solution.py:481
  133.5 0.5 collective-permute-done.18.refs_3_
  134.1 0.5 copy-done.6
  134.5 6.6 %slice_grads.5 = (bf16[1024,512]{1,0:T(8,128)(2,1)}, bf16[1024,512]{1,0:T(8,128)(2,1)}) custom-call(s32[1]{0:T(128)} %bitcast.3.place_ref, bf16[768,4096]{1,0:T(8,128)(2,1)} %all-gather.2.cloned.1.call-done.x_hbm, bf16[768,4096]{1,0:T(8,128)(2,1)} %get-tuple-element.36.dy_hbm, bf16[768,512]{1,0:T(8,128)(2,1)} %get-tuple-element.37.refs_0_, ...), custom_call_target="tpu_custom_call" | custom-call | tf_op jit(solution)/shard_map/slice_grads/pallas_call | solution.py:367
  141.1 1.2 collective-permute-start.19
  142.3 2.1 %collective-permute-start.20 = (bf16[1024,512]{1,0:T(8,128)(2,1)}, bf16[1024,512]{1,0:T(8,128)(2,1)}, u32[]{:S(2)}, u32[]{:S(2)}) collective-permute-start(bf16[1024,512]{1,0:T(8,128)(2,1)} %get-tuple-element.45), channel_id=1, source_target_pairs={{0,3},{1,0},{2,1},{3,2},{4,7},{5,4},{6,5},{7,6},{8,11},{9,8},{10,9... | collective-permute-start | bytes 3145736 | tf_op jit(solution)/shard_map/ppermute | solution.py:514
  144.4 34.1 %reduce-scatter.2.cloned.1.call-done.got_ref = bf16[48,4224]{1,0:T(8,128)(2,1)} async-done(((bf16[768,4224]{1,0:T(8,128)(2,1)}), bf16[48,4224]{1,0:T(8,128)(2,1)}) %reduce-scatter.2.cloned.1.call-update) | async-done | bytes 405520 | tf_op jit(solution)/shard_map/reduce_scatter | solution.py:492
  178.5 0.9 constant_dynamic-slice_fusion
  179.4 2.9 %collective-permute-start.14 = (bf16[24,4224]{1,0:T(8,128)(2,1)S(1)}, bf16[24,4224]{1,0:T(8,128)(2,1)S(1)}, u32[]{:S(2)}, u32[]{:S(2)}) collective-permute-start(bf16[24,4224]{1,0:T(8,128)(2,1)S(1)} %constant_dynamic-slice_fusion), channel_id=1, source_target_pairs={{0,64},{64,0},{1,65},{65,1},{2,66},{66,2},{3,67},{67,3},{4,68},{68... | collective-permute-start | bytes 608264 | tf_op jit(solution)/shard_map/ppermute | solution.py:516
  182.4 0.0 collective-permute-done.15.near_up_ref
  182.4 0.9 copy-done.3
  183.3 0.4 copy-done.4
  183.7 0.3 copy-done.5
  184.0 4.7 %add_up.1 = (bf16[1024,512]{1,0:T(8,128)(2,1)}, bf16[1024,512]{1,0:T(8,128)(2,1)}) custom-call(f32[1024,512]{1,0:T(8,128)} %get-tuple-element.38.refs_4_.in_ref, f32[1024,512]{1,0:T(8,128)} %get-tuple-element.39.out_ref, bf16[1024,512]{1,0:T(8,128)(2,1)} %copy-done.3, bf16[1024,512]{1,0:T(8,128)(2,1)} %copy-done.4, bf16[1024,512]{1,0:T(8,128)(2,1)} %copy-done.5, ...), custom_call_target="tpu_custom_call" | custom-call | tf_op jit(solution)/shard_map/add_up/pallas_call | solution.py:402
  188.7 0.8 convert_reduce_fusion.1
  189.5 0.1 convert_reduce_fusion
  189.7 1.3 fusion
  191.0 4.7 %unpick.1 = bf16[512,4096]{1,0:T(8,128)(2,1)} custom-call(s32[1]{0:T(128)} %bitcast.place_ref, bf16[48,4224]{1,0:T(8,128)(2,1)} %reduce-scatter.2.cloned.1.call-done.got_ref, bf16[24,4224]{1,0:T(8,128)(2,1)} %copy-done.10, s32[2,24]{1,0:T(2,128)} %bitcast.25), custom_call_target="tpu_custom_call" | custom-call | tf_op jit(solution)/shard_map/unpick/pallas_call | solution.py:430
  (25 shorter events, 0.1 us)
Async XLA Ops:
  7.2 74.4 %all-gather.2.cloned.1.call-start = ((), (), s32[]{:S(2)}) async-start(), calls=%async_computation.1 | async-start | bytes 7077888 | tf_op jit(solution)/shard_map/all_gather | solution.py:463
  13.1 12.2 %collective-permute-start.3 = (bf16[48,4096]{1,0:T(8,128)(2,1)}, bf16[48,4096]{1,0:T(8,128)(2,1)S(1)}, u32[]{:S(2)}, u32[]{:S(2)}) collective-permute-start(bf16[48,4096]{1,0:T(8,128)(2,1)} %get-tuple-element.28.refs_0_.refs_4_), channel_id=1, source_target_pairs={{0,8},{8,16},{16,24},{24,0},{1,9},{9,17},{17,25},{25,1},{2,10},{10... | collective-permute-start | bytes 1179656 | tf_op jit(solution)/shard_map/ppermute | solution.py:456
  14.6 10.8 %collective-permute-start.4 = (bf16[48,4096]{1,0:T(8,128)(2,1)}, bf16[48,4096]{1,0:T(8,128)(2,1)S(1)}, u32[]{:S(2)}, u32[]{:S(2)}) collective-permute-start(bf16[48,4096]{1,0:T(8,128)(2,1)} %get-tuple-element.28.refs_0_.refs_4_), channel_id=1, source_target_pairs={{0,24},{8,0},{16,8},{24,16},{1,25},{9,1},{17,9},{25,17},{2,26},{10... | collective-permute-start | bytes 1179656 | tf_op jit(solution)/shard_map/ppermute | solution.py:457
  16.3 9.3 %collective-permute-start = (bf16[24,4096]{1,0:T(8,128)(2,1)}, bf16[24,4096]{1,0:T(8,128)(2,1)S(1)}, u32[]{:S(2)}, u32[]{:S(2)}) collective-permute-start(bf16[24,4096]{1,0:T(8,128)(2,1)} %get-tuple-element.26.refs_0_), channel_id=1, source_target_pairs={{0,32},{32,0},{64,96},{96,64},{1,33},{33,1},{65,97},{97,65},{2,34}... | collective-permute-start | bytes 589832 | tf_op jit(solution)/shard_map/ppermute | solution.py:24
  18.3 12.2 %collective-permute-start.1 = (bf16[24,4096]{1,0:T(8,128)(2,1)}, bf16[24,4096]{1,0:T(8,128)(2,1)S(1)}, u32[]{:S(2)}, u32[]{:S(2)}) collective-permute-start(bf16[24,4096]{1,0:T(8,128)(2,1)} %get-tuple-element.27), channel_id=1, source_target_pairs={{0,64},{32,96},{64,0},{96,32},{1,65},{33,97},{65,1},{97,33},{2,66}... | collective-permute-start | bytes 589832 | tf_op jit(solution)/shard_map/ppermute | solution.py:24
  21.9 11.0 %collective-permute-start.2 = (bf16[24,4096]{1,0:T(8,128)(2,1)}, bf16[24,4096]{1,0:T(8,128)(2,1)S(1)}, u32[]{:S(2)}, u32[]{:S(2)}) collective-permute-start(bf16[24,4096]{1,0:T(8,128)(2,1)} %get-tuple-element.27), channel_id=1, source_target_pairs={{0,96},{32,64},{64,32},{96,0},{1,97},{33,65},{65,33},{97,1},{2,98}... | collective-permute-start | bytes 589832 | tf_op jit(solution)/shard_map/ppermute | solution.py:24
  32.9 0.9 copy-start.2
  34.9 143.6 %reduce-scatter.2.cloned.1.call-start = ((), (), s32[]{:S(2)}) async-start(), calls=%async_computation.2 | async-start | bytes 6893568 | tf_op jit(solution)/shard_map/reduce_scatter | solution.py:492
  34.9 7.0 %collective-permute-start.5 = (bf16[24,4096]{1,0:T(8,128)(2,1)S(1)}, bf16[24,4096]{1,0:T(8,128)(2,1)S(1)}, u32[]{:S(2)}, u32[]{:S(2)}) collective-permute-start(bf16[24,4096]{1,0:T(8,128)(2,1)S(1)} %get-tuple-element.29.refs_4_), channel_id=1, source_target_pairs={{0,8},{8,16},{16,24},{24,0},{1,9},{9,17},{17,25},{25,1},{2,10},{10... | collective-permute-start | bytes 589832 | tf_op jit(solution)/shard_map/ppermute | solution.py:459
  35.3 6.7 %collective-permute-start.6 = (bf16[24,4096]{1,0:T(8,128)(2,1)S(1)}, bf16[24,4096]{1,0:T(8,128)(2,1)S(1)}, u32[]{:S(2)}, u32[]{:S(2)}) collective-permute-start(bf16[24,4096]{1,0:T(8,128)(2,1)S(1)} %get-tuple-element.30.refs_5_), channel_id=1, source_target_pairs={{0,24},{8,0},{16,8},{24,16},{1,25},{9,1},{17,9},{25,17},{2,26},{10... | collective-permute-start | bytes 589832 | tf_op jit(solution)/shard_map/ppermute | solution.py:460
  41.9 1.0 copy-start
  43.5 46.7 %copy-start.1 = (bf16[96,4096]{1,0:T(8,128)(2,1)}, bf16[96,4096]{1,0:T(8,128)(2,1)S(1)}, u32[]{:S(2)}) copy-start(bf16[96,4096]{1,0:T(8,128)(2,1)S(1)} %get-tuple-element.33.refs_0_) | copy-start | bytes 2359300
  43.5 20.6 %collective-permute-start.8 = (bf16[96,4096]{1,0:T(8,128)(2,1)S(1)}, bf16[96,4096]{1,0:T(8,128)(2,1)S(1)}, u32[]{:S(2)}, u32[]{:S(2)}) collective-permute-start(bf16[96,4096]{1,0:T(8,128)(2,1)S(1)} %get-tuple-element.33.refs_0_), channel_id=1, source_target_pairs={{0,32},{32,0},{64,96},{96,64},{1,33},{33,1},{65,97},{97,65},{2,34}... | collective-permute-start | bytes 2359304 | tf_op jit(solution)/shard_map/ppermute | solution.py:24
  43.6 34.1 %collective-permute-start.10 = (bf16[96,4096]{1,0:T(8,128)(2,1)S(1)}, bf16[96,4096]{1,0:T(8,128)(2,1)S(1)}, u32[]{:S(2)}, u32[]{:S(2)}) collective-permute-start(bf16[96,4096]{1,0:T(8,128)(2,1)S(1)} %get-tuple-element.34), channel_id=1, source_target_pairs={{0,64},{32,96},{64,0},{96,32},{1,65},{33,97},{65,1},{97,33},{2,66}... | collective-permute-start | bytes 2359304 | tf_op jit(solution)/shard_map/ppermute | solution.py:24
  45.1 35.1 %collective-permute-start.12 = (bf16[96,4096]{1,0:T(8,128)(2,1)S(1)}, bf16[96,4096]{1,0:T(8,128)(2,1)S(1)}, u32[]{:S(2)}, u32[]{:S(2)}) collective-permute-start(bf16[96,4096]{1,0:T(8,128)(2,1)S(1)} %get-tuple-element.34), channel_id=1, source_target_pairs={{0,96},{32,64},{64,32},{96,0},{1,97},{33,65},{65,33},{97,1},{2,98}... | collective-permute-start | bytes 2359304 | tf_op jit(solution)/shard_map/ppermute | solution.py:24
  48.2 41.9 %collective-permute-start.7 = (bf16[96,4096]{1,0:T(8,128)(2,1)S(1)}, bf16[96,4096]{1,0:T(8,128)(2,1)}, u32[]{:S(2)}, u32[]{:S(2)}) collective-permute-start(bf16[96,4096]{1,0:T(8,128)(2,1)S(1)} %get-tuple-element.33.refs_0_), channel_id=1, source_target_pairs={{0,4},{4,0},{1,5},{5,1},{2,6},{6,2},{3,7},{7,3},{8,12},{12,8},{9,1... | collective-permute-start | bytes 2359304 | tf_op jit(solution)/shard_map/ppermute | solution.py:473
  64.0 26.1 %copy-start.7 = (bf16[96,4096]{1,0:T(8,128)(2,1)}, bf16[96,4096]{1,0:T(8,128)(2,1)S(1)}, u32[]{:S(2)}) copy-start(bf16[96,4096]{1,0:T(8,128)(2,1)S(1)} %collective-permute-done.8.refs_2_) | copy-start | bytes 2359300
  64.0 26.1 %collective-permute-start.9 = (bf16[96,4096]{1,0:T(8,128)(2,1)S(1)}, bf16[96,4096]{1,0:T(8,128)(2,1)}, u32[]{:S(2)}, u32[]{:S(2)}) collective-permute-start(bf16[96,4096]{1,0:T(8,128)(2,1)S(1)} %collective-permute-done.8.refs_2_), channel_id=1, source_target_pairs={{0,4},{4,0},{1,5},{5,1},{2,6},{6,2},{3,7},{7,3},{8,12},{12,8},{9,1... | collective-permute-start | bytes 2359304 | tf_op jit(solution)/shard_map/ppermute | solution.py:473
  77.7 12.5 %copy-start.8 = (bf16[96,4096]{1,0:T(8,128)(2,1)}, bf16[96,4096]{1,0:T(8,128)(2,1)S(1)}, u32[]{:S(2)}) copy-start(bf16[96,4096]{1,0:T(8,128)(2,1)S(1)} %collective-permute-done.10.refs_4_) | copy-start | bytes 2359300
  77.7 12.5 %collective-permute-start.11 = (bf16[96,4096]{1,0:T(8,128)(2,1)S(1)}, bf16[96,4096]{1,0:T(8,128)(2,1)}, u32[]{:S(2)}, u32[]{:S(2)}) collective-permute-start(bf16[96,4096]{1,0:T(8,128)(2,1)S(1)} %collective-permute-done.10.refs_4_), channel_id=1, source_target_pairs={{0,4},{4,0},{1,5},{5,1},{2,6},{6,2},{3,7},{7,3},{8,12},{12,8},{9,1... | collective-permute-start | bytes 2359304 | tf_op jit(solution)/shard_map/ppermute | solution.py:473
  80.2 9.9 %copy-start.9 = (bf16[96,4096]{1,0:T(8,128)(2,1)}, bf16[96,4096]{1,0:T(8,128)(2,1)S(1)}, u32[]{:S(2)}) copy-start(bf16[96,4096]{1,0:T(8,128)(2,1)S(1)} %collective-permute-done.12.refs_6_) | copy-start | bytes 2359300
  80.2 10.0 %collective-permute-start.13 = (bf16[96,4096]{1,0:T(8,128)(2,1)S(1)}, bf16[96,4096]{1,0:T(8,128)(2,1)}, u32[]{:S(2)}, u32[]{:S(2)}) collective-permute-start(bf16[96,4096]{1,0:T(8,128)(2,1)S(1)} %collective-permute-done.12.refs_6_), channel_id=1, source_target_pairs={{0,4},{4,0},{1,5},{5,1},{2,6},{6,2},{3,7},{7,3},{8,12},{12,8},{9,1... | collective-permute-start | bytes 2359304 | tf_op jit(solution)/shard_map/ppermute | solution.py:473
  106.1 27.4 %collective-permute-start.17 = (bf16[1024,512]{1,0:T(8,128)(2,1)}, bf16[1024,512]{1,0:T(8,128)(2,1)S(1)}, u32[]{:S(2)}, u32[]{:S(2)}) collective-permute-start(bf16[1024,512]{1,0:T(8,128)(2,1)} %get-tuple-element.42), channel_id=1, source_target_pairs={{0,1},{1,2},{2,3},{3,0},{4,5},{5,6},{6,7},{7,4},{8,9},{9,10},{10,1... | collective-permute-start | bytes 3145736 | tf_op jit(solution)/shard_map/ppermute | solution.py:481
  107.7 26.3 %collective-permute-start.18 = (bf16[1024,512]{1,0:T(8,128)(2,1)}, bf16[1024,512]{1,0:T(8,128)(2,1)}, u32[]{:S(2)}, u32[]{:S(2)}) collective-permute-start(bf16[1024,512]{1,0:T(8,128)(2,1)} %get-tuple-element.43), channel_id=1, source_target_pairs={{0,3},{1,0},{2,1},{3,2},{4,7},{5,4},{6,5},{7,6},{8,11},{9,8},{10,9... | collective-permute-start | bytes 3145736 | tf_op jit(solution)/shard_map/ppermute | solution.py:482
  115.3 67.0 %collective-permute-start.15 = (bf16[1024,512]{1,0:T(8,128)(2,1)}, bf16[1024,512]{1,0:T(8,128)(2,1)S(1)}, u32[]{:S(2)}, u32[]{:S(2)}) collective-permute-start(bf16[1024,512]{1,0:T(8,128)(2,1)} %get-tuple-element.40), channel_id=1, source_target_pairs={{0,1},{1,2},{2,3},{3,0},{4,5},{5,6},{6,7},{7,4},{8,9},{9,10},{10,1... | collective-permute-start | bytes 3145736 | tf_op jit(solution)/shard_map/ppermute | solution.py:490
  115.8 66.6 %collective-permute-start.16 = (bf16[1024,512]{1,0:T(8,128)(2,1)}, bf16[1024,512]{1,0:T(8,128)(2,1)S(1)}, u32[]{:S(2)}, u32[]{:S(2)}) collective-permute-start(bf16[1024,512]{1,0:T(8,128)(2,1)} %get-tuple-element.41), channel_id=1, source_target_pairs={{0,3},{1,0},{2,1},{3,2},{4,7},{5,4},{6,5},{7,6},{8,11},{9,8},{10,9... | collective-permute-start | bytes 3145736 | tf_op jit(solution)/shard_map/ppermute | solution.py:491
  133.5 1.0 copy-start.6
  141.1 41.3 %collective-permute-start.19 = (bf16[1024,512]{1,0:T(8,128)(2,1)}, bf16[1024,512]{1,0:T(8,128)(2,1)S(1)}, u32[]{:S(2)}, u32[]{:S(2)}) collective-permute-start(bf16[1024,512]{1,0:T(8,128)(2,1)} %get-tuple-element.44), channel_id=1, source_target_pairs={{0,1},{1,2},{2,3},{3,0},{4,5},{5,6},{6,7},{7,4},{8,9},{9,10},{10,1... | collective-permute-start | bytes 3145736 | tf_op jit(solution)/shard_map/ppermute | solution.py:513
  142.3 40.1 %collective-permute-start.20 = (bf16[1024,512]{1,0:T(8,128)(2,1)}, bf16[1024,512]{1,0:T(8,128)(2,1)}, u32[]{:S(2)}, u32[]{:S(2)}) collective-permute-start(bf16[1024,512]{1,0:T(8,128)(2,1)} %get-tuple-element.45), channel_id=1, source_target_pairs={{0,3},{1,0},{2,1},{3,2},{4,7},{5,4},{6,5},{7,6},{8,11},{9,8},{10,9... | collective-permute-start | bytes 3145736 | tf_op jit(solution)/shard_map/ppermute | solution.py:514
  179.4 10.1 %collective-permute-start.14 = (bf16[24,4224]{1,0:T(8,128)(2,1)S(1)}, bf16[24,4224]{1,0:T(8,128)(2,1)S(1)}, u32[]{:S(2)}, u32[]{:S(2)}) collective-permute-start(bf16[24,4224]{1,0:T(8,128)(2,1)S(1)} %constant_dynamic-slice_fusion), channel_id=1, source_target_pairs={{0,64},{64,0},{1,65},{65,1},{2,66},{66,2},{3,67},{67,3},{4,68},{68... | collective-permute-start | bytes 608264 | tf_op jit(solution)/shard_map/ppermute | solution.py:516
  182.4 1.0 copy-start.3
  182.4 1.4 copy-start.4
  182.4 1.6 copy-start.5
  189.5 1.5 copy-start.10
Sparse Core Ops, SparseCore 0:
  35.0 38.5 all-gather.1
  106.2 72.2 reduce-scatter.1

commit v3 on v2

v3 whole, which is shorter than its diff:
```python
import jax
import jax.numpy as jnp
from jax import lax
from jax.experimental import pallas as pl
from jax.experimental.pallas import tpu as pltpu
from jax.sharding import Mesh
from jax.sharding import PartitionSpec as P

F32 = jnp.float32
BF16 = jnp.bfloat16
UP = [(0, 1), (1, 2), (2, 3), (3, 0)]
DOWN = [(0, 3), (1, 0), (2, 1), (3, 2)]
PAIR = [(0, 1), (1, 0)]
X_OFFSETS = (0, 3, 1, 2)
LANES = 128
ROOT = 0.7978845608028654
CUBE = 0.044715
ANYWHERE = pl.BlockSpec(memory_space=pl.ANY)
IN_VMEM = pl.BlockSpec(memory_space=pltpu.VMEM)
IN_SMEM = pl.BlockSpec(memory_space=pltpu.SMEM)


def over_z(v, flip):
    return lax.ppermute(v, ("k", "zz"), [(i, i ^ flip) for i in range(4)])


def params(steps=0, mib=60):
    kind = ("arbitrary",) * steps if steps else None
    return pltpu.CompilerParams(vmem_limit_bytes=mib << 20, dimension_semantics=kind)


def rows_dot(a, b):
    return lax.dot_general(a, b, (((0,), (0,)), ((), ())), preferred_element_type=F32)


def pick_rows(tokens, out_grad, gates, picks, counts):
    t_dev, width = tokens.shape
    experts, slots = picks.shape
    steps = 4
    chunk = width // steps

    def body(k_ref, dp_ref, t_hbm, g_hbm, gate_ref, pick_ref, count_ref, mine_ref, other_ref, dy_ref, t_v, g_v, sems):
        k = k_ref[0]
        copies = []
        for i in range(steps):
            start = pl.multiple_of(((dp_ref[0] + i) % steps) * chunk, LANES)
            copies.append(pltpu.make_async_copy(g_hbm.at[:, pl.ds(start, chunk)], g_v.at[i], sems.at[0, i]))
            copies[-1].start()
        for i in range(steps):
            copies.append(pltpu.make_async_copy(t_hbm.at[:, pl.ds(i * chunk, chunk)], t_v.at[i], sems.at[1, i]))
            copies[-1].start()

        def both(first, second):
            swap = k != 0
            return jnp.concatenate([jnp.where(swap, second, first), jnp.where(swap, first, second)], 1)

        index = both(pick_ref[0:1, :], pick_ref[1:2, :])
        hit = lax.broadcasted_iota(jnp.int32, (t_dev, experts * slots), 0) == index
        gate = gate_ref[...].astype(F32)
        slot = lax.broadcasted_iota(jnp.int32, (1, slots), 1)
        scale = [jnp.where(slot < count_ref[0, e], gate[e : e + 1, :], 0.0) for e in range(2)]
        plain = jnp.where(hit, 1.0, 0.0).T.astype(BF16)
        scaled = jnp.where(hit, both(*scale), 0.0).T.astype(BF16)

        def split(picked, i):
            span = slice(i * chunk, (i + 1) * chunk)
            mine_ref[:, span] = picked[:slots].astype(BF16)
            other_ref[:, span] = picked[slots:].astype(BF16)

        for i in range(steps):
            copies[i].wait()
            picked = jnp.dot(scaled, g_v[i], preferred_element_type=F32)
            if i == 0:
                split(picked, steps)
            else:
                dy_ref[:, (i - 1) * chunk : i * chunk] = picked.astype(BF16)
        for i in range(steps):
            copies[steps + i].wait()
            split(jnp.dot(plain, t_v[i], preferred_element_type=F32), i)

    return pl.pallas_call(
        body,
        in_specs=[IN_SMEM, IN_SMEM, ANYWHERE, ANYWHERE, IN_VMEM, IN_VMEM, IN_SMEM],
        out_specs=[IN_VMEM] * 3,
        out_shape=[
            jax.ShapeDtypeStruct((slots, width + chunk), BF16),
            jax.ShapeDtypeStruct((slots, width + chunk), BF16),
            jax.ShapeDtypeStruct((experts * slots, width - chunk), BF16),
        ],
        scratch_shapes=[
            pltpu.VMEM((steps, t_dev, chunk), BF16),
            pltpu.VMEM((steps, t_dev, chunk), BF16),
            pltpu.SemaphoreType.DMA((2, steps)),
        ],
        compiler_params=params(),
        name="pick_rows",
    )(lax.axis_index("k").reshape(1), lax.axis_index("dp").reshape(1), tokens, out_grad, gates, picks, counts)


def stack_rows(groups, after=()):
    flat = [block for group in groups for block in group]
    slots = 24
    width = flat[0][0].shape[1]
    chunk = width // 2
    n = len(flat)

    def body(*refs):
        place = 0
        for out_ref, group in zip(refs[n + len(after) :], groups):
            rows = []
            for _, first in group:
                rows.append(refs[place][...].astype(F32)[first : first + slots])
                place += 1
            out_ref[...] = jnp.concatenate(rows, 0).astype(BF16)

    return pl.pallas_call(
        body,
        grid=(width // chunk,),
        in_specs=[pl.BlockSpec((v.shape[0], chunk), lambda i: (0, i)) for v, _ in flat]
        + [ANYWHERE] * len(after),
        out_specs=[pl.BlockSpec((slots * len(g), chunk), lambda i: (0, i)) for g in groups],
        out_shape=[jax.ShapeDtypeStruct((slots * len(g), width), BF16) for g in groups],
        compiler_params=params(1, 16),
        name="stack_rows",
    )(*[v for v, _ in flat], *after)


def gate_lanes(gate_sum):
    lane = lax.broadcasted_iota(jnp.int32, gate_sum.shape, 1)
    high = gate_sum.astype(BF16).astype(F32)
    return jnp.where(lane == 0, high, jnp.where(lane == 1, gate_sum - high, 0.0))


def grad_pass(pieces, weight):
    parts = len(pieces)
    rows, width = pieces[0].shape
    units = weight.shape[1]
    count = parts * rows
    steps = 3
    chunk = width // steps

    def body(place_ref, *refs):
        piece_refs = refs[:parts]
        w_hbm, grad, dy_out, dy_v, w_v, sems, out_sems = refs[parts:]
        copies = []
        outs = []
        for i in range(steps):
            span = pl.ds(i * chunk, chunk)
            start = pl.multiple_of(((place_ref[0] + 1 + i) % 4) * chunk, LANES)
            group = [(w_hbm.at[pl.ds(start, chunk), :], w_v.at[span, :])] + [
                (ref.at[:, span], dy_v.at[pl.ds(j * rows, rows), span])
                for j, ref in enumerate(piece_refs)
            ]
            group = [
                pltpu.make_async_copy(src, dst, sems.at[i, j]) for j, (src, dst) in enumerate(group)
            ]
            for copy in group:
                copy.start()
            copies.append(group)
        for i in range(steps):
            span = pl.ds(i * chunk, chunk)
            for copy in copies[i]:
                copy.wait()
            outs.append(pltpu.make_async_copy(dy_v.at[:, span], dy_out.at[:, span], out_sems.at[i]))
            outs[-1].start()
            part = jnp.dot(dy_v[:, span], w_v[span, :], preferred_element_type=F32)
            if i == 0:
                grad[...] = part
            else:
                grad[...] += part
        for out in outs:
            out.wait()

    return pl.pallas_call(
        body,
        in_specs=[IN_SMEM] + [ANYWHERE] * (parts + 1),
        out_specs=[IN_VMEM, ANYWHERE],
        out_shape=[
            jax.ShapeDtypeStruct((count, units), F32),
            jax.ShapeDtypeStruct((count, width), BF16),
        ],
        scratch_shapes=[
            pltpu.VMEM((count, width), BF16),
            pltpu.VMEM((width, units), BF16),
            pltpu.SemaphoreType.DMA((steps, 1 + parts)),
            pltpu.SemaphoreType.DMA((steps,)),
        ],
        compiler_params=params(),
        name="grad_pass",
    )(lax.axis_index("dp").reshape(1), *pieces, weight)


def core_pass(rows_x, grads, rows_dy, weight_in, weight_out, slots):
    count = rows_x.shape[0]
    width, units = weight_in.shape
    steps = 4
    chunk = width // steps
    piece = chunk // 2

    def body(place_ref, grad_ref, x_hbm, dy_hbm, w1_hbm, w2_hbm, *refs):
        pre_x_ref, hidden_x_ref, hidden_ref, row_out, far_up, far_down = refs[:6]
        (
            x_v, dy_v, far_v, w1_v, w2_v, pre, grad, hid, pre_home, gate_home, pre_b, row_v, up_v, down_v, sems, out_sems,
        ) = refs[6:]
        core = place_ref[0]
        spot = place_ref[1]
        dp = place_ref[2]
        me_x = place_ref[3]
        own = pl.ds(pl.multiple_of(dp * chunk, LANES), chunk)
        late = [
            pltpu.make_async_copy(x_hbm.at[:, pl.ds(width, chunk)], dy_v, sems.at[steps, 0]),
            pltpu.make_async_copy(w2_hbm.at[own, :], w2_v, sems.at[steps, 1]),
            pltpu.make_async_copy(dy_hbm.at[:, pl.ds(chunk, chunk)], far_v, sems.at[steps, 2]),
        ]
        copies = []
        for i in range(steps):
            span = pl.ds(i * chunk, chunk)
            group = [
                pltpu.make_async_copy(x_hbm.at[:, span], x_v.at[:, span], sems.at[i, 0]),
                pltpu.make_async_copy(w1_hbm.at[span, :], w1_v.at[span, :], sems.at[i, 1]),
            ]
            for copy in group:
                copy.start()
            copies.append(group)
        for copy in late:
            copy.start()
        for i in range(steps):
            span = pl.ds(i * chunk, chunk)
            for copy in copies[i]:
                copy.wait()
            part = jnp.dot(x_v[:, span], w1_v[span, :], preferred_element_type=F32)
            if i == 0:
                pre[...] = part
            else:
                pre[...] += part
        late[0].wait()
        late[1].wait()
        grad[...] = jnp.dot(dy_v[...], w2_v[...], preferred_element_type=F32)

        @pl.loop(0, 4)
        def _(z):
            home_z = z ^ spot
            for step_x in range(4):
                x = (me_x + X_OFFSETS[step_x]) % 4
                for from_core in range(2):
                    home = (((home_z % 2) * 4 + x) * 2 + (core ^ from_core)) * 2 + home_z // 2
                    home = pl.ds(pl.multiple_of(home * slots, 8), slots)
                    source = ((x * 2 + (core ^ from_core)) * 4 + z) * slots
                    there = pl.ds(pl.multiple_of(source, 8), slots)
                    here = ((z * 2 + from_core) * 4 + step_x) * slots
                    here = pl.ds(pl.multiple_of(here, 8), slots)
                    v = pre[there, :]
                    u = grad[there, :] + grad_ref[here, :]
                    t = jnp.tanh(ROOT * (v + CUBE * (v * v * v)))
                    cdf = 0.5 * (1.0 + t)
                    h = (v * cdf).astype(BF16).astype(F32)
                    slope = cdf + 0.5 * v * (1.0 - t * t) * (ROOT * (1.0 + 3.0 * CUBE * (v * v)))
                    p = u * slope
                    gate_home[home, :] = jnp.broadcast_to(
                        jnp.sum(h * u, -1, keepdims=True), (slots, LANES)
                    )
                    pre_home[home, :] = p
                    hid[here, :] = h
                    grad[there, :] = h
                    pre[there, :] = p

        pre_x_ref[...] = pre[...].astype(BF16)
        hidden_x_ref[...] = grad[...].astype(BF16)
        hidden_ref[...] = hid[...].astype(BF16)
        pre_b[...] = pre_home[...].astype(BF16)
        late[2].wait()
        outs = []
        for side, buffer, out in ((0, up_v, far_up), (1, down_v, far_down)):
            start = pl.multiple_of(((dp + 2) % 4) * chunk + side * piece, LANES)
            buffer[:piece, :] = rows_dot(x_v[:, pl.ds(start, piece)], pre_x_ref[...]).astype(BF16)
            buffer[piece:, :] = rows_dot(
                far_v[:, side * piece : (side + 1) * piece], hidden_ref[...]
            ).astype(BF16)
            outs.append(pltpu.make_async_copy(buffer, out, out_sems.at[side]))
            outs[-1].start()
        row_v[:, width:] = gate_lanes(gate_home[...]).astype(BF16)
        for i in range(steps):
            span = pl.ds(i * chunk, chunk)
            row_v[:, span] = lax.dot_general(
                pre_b[...], w1_v[span, :], (((1,), (1,)), ((), ())), preferred_element_type=F32
            ).astype(BF16)
            if i == steps - 1:
                span = pl.ds(i * chunk, chunk + LANES)
            outs.append(pltpu.make_async_copy(row_v.at[:, span], row_out.at[:, span], out_sems.at[2 + i]))
            outs[-1].start()
        for copy in outs:
            copy.wait()

    place = jnp.stack(
        [
            lax.axis_index("c"),
            lax.axis_index("k") * 2 + lax.axis_index("zz"),
            lax.axis_index("dp"),
            lax.axis_index("x"),
        ]
    )
    return pl.pallas_call(
        body,
        in_specs=[IN_SMEM, IN_VMEM] + [ANYWHERE] * 4,
        out_specs=[IN_VMEM] * 3 + [ANYWHERE] * 3,
        out_shape=[
            jax.ShapeDtypeStruct((count, units), BF16),
            jax.ShapeDtypeStruct((count, units), BF16),
            jax.ShapeDtypeStruct((count, units), BF16),
            jax.ShapeDtypeStruct((count, width + LANES), BF16),
            jax.ShapeDtypeStruct((chunk, units), BF16),
            jax.ShapeDtypeStruct((chunk, units), BF16),
        ],
        scratch_shapes=[
            pltpu.VMEM((count, width), BF16),
            pltpu.VMEM((count, chunk), BF16),
            pltpu.VMEM((count, chunk), BF16),
            pltpu.VMEM((width, units), BF16),
            pltpu.VMEM((chunk, units), BF16),
            pltpu.VMEM((count, units), F32),
            pltpu.VMEM((count, units), F32),
            pltpu.VMEM((count, units), F32),
            pltpu.VMEM((count, units), F32),
            pltpu.VMEM((count, LANES), F32),
            pltpu.VMEM((count, units), BF16),
            pltpu.VMEM((count, width + LANES), BF16),
            pltpu.VMEM((chunk, units), BF16),
            pltpu.VMEM((chunk, units), BF16),
            pltpu.SemaphoreType.DMA((steps + 1, 3)),
            pltpu.SemaphoreType.DMA((2 + steps,)),
        ],
        compiler_params=params(),
        name="core_pass",
    )(place, grads, rows_x, rows_dy, weight_in, weight_out)


def slice_grads(lefts, rights, jobs, extras, out_count, kind=BF16, after=()):
    count = lefts[0].shape[0]
    width = 4 * (lefts[1].shape[1] // 3)
    units = rights[0].shape[1]
    piece = width // 8
    n = len(extras)

    def body(place_ref, x_hbm, dy_hbm, *refs):
        right_refs = refs[:3]
        extra_refs = refs[3 : 3 + n]
        outs = refs[3 + n + len(after) :][:out_count]
        buffers, sems = refs[-2:]
        copies = []
        for i, (m, shift, side, _, _, _) in enumerate(jobs):
            start = ((place_ref[0] + shift) % 4) * 2 * piece + side * piece
            left = x_hbm.at[:, pl.ds(pl.multiple_of(start, LANES), piece)]
            if m == 1 and shift == 0:
                left = x_hbm.at[:, pl.ds(width + side * piece, piece)]
            elif m == 1:
                left = dy_hbm.at[:, pl.ds((2 * (shift - 1) + side) * piece, piece)]
            copies.append(pltpu.make_async_copy(left, buffers.at[i], sems.at[i]))
            copies[-1].start()
        for i, (m, shift, _, out, row, adds) in enumerate(jobs):
            copies[i].wait()
            right = right_refs[2 if m == 1 and shift == 0 else m]
            part = rows_dot(buffers[i], right[...])
            for index, first in adds:
                part += extra_refs[index][first : first + piece, :].astype(F32)
            outs[out][row : row + piece, :] = part.astype(kind)

    return pl.pallas_call(
        body,
        in_specs=[IN_SMEM, ANYWHERE, ANYWHERE] + [IN_VMEM] * (3 + n) + [ANYWHERE] * len(after),
        out_specs=[IN_VMEM] * out_count,
        out_shape=[jax.ShapeDtypeStruct((2 * piece, units), kind)] * out_count,
        scratch_shapes=[
            pltpu.VMEM((len(jobs), count, piece), BF16),
            pltpu.SemaphoreType.DMA((len(jobs),)),
        ],
        compiler_params=params(),
        name="slice_grads",
    )(lax.axis_index("dp").reshape(1), *lefts, *rights, *extras, *after)


def add_up(own_in, own_out, near_up, near_down, sum_up, sum_down):
    rows, units = own_in.shape
    half = rows // 2

    def body(in_ref, out_ref, near_up_ref, near_down_ref, sum_up_ref, sum_down_ref, *results):
        side = pl.program_id(0)
        for m, (own, result) in enumerate(zip((in_ref, out_ref), results)):
            span = slice(m * half, (m + 1) * half)

            @pl.when(side == 0)
            def _():
                total = own[...].astype(F32) + near_down_ref[span, :].astype(F32) + sum_up_ref[span, :].astype(F32)
                result[...] = total.astype(BF16)

            @pl.when(side == 1)
            def _():
                total = own[...].astype(F32) + near_up_ref[span, :].astype(F32) + sum_down_ref[span, :].astype(F32)
                result[...] = total.astype(BF16)

    own_spec = pl.BlockSpec((half, units), lambda i: (i, 0))
    full = pl.BlockSpec((rows, units), lambda i: (0, 0))
    return pl.pallas_call(
        body,
        grid=(2,),
        in_specs=[own_spec, own_spec] + [full] * 4,
        out_specs=[own_spec, own_spec],
        out_shape=[jax.ShapeDtypeStruct((rows, units), BF16)] * 2,
        compiler_params=params(1),
        name="add_up",
    )(own_in, own_out, near_up, near_down, sum_up, sum_down)


def partner_rows(got, slots):
    chunk = got.shape[1] // 3

    def body(place_ref, got_ref, out_ref):
        rows = got_ref[...].astype(F32)
        out_ref[...] = jnp.where(place_ref[0] == 0, rows[slots:], rows[:slots]).astype(BF16)

    return pl.pallas_call(
        body,
        grid=(3,),
        in_specs=[IN_SMEM, pl.BlockSpec((2 * slots, chunk), lambda i: (0, i))],
        out_specs=pl.BlockSpec((slots, chunk), lambda i: (0, i)),
        out_shape=jax.ShapeDtypeStruct((slots, got.shape[1]), BF16),
        compiler_params=params(1, 16),
        name="partner_rows",
    )(lax.axis_index("k").reshape(1), got)


def unpick(got, swapped, gates, picks, counts, t_dev, width):
    experts, slots = picks.shape
    steps = 4
    chunk = width // steps

    def body(k_ref, got_ref, swapped_ref, gate_ref, pick_ref, count_ref, out_hbm, gates_ref, out_v, sems):
        k = k_ref[0]

        def own(span):
            rows = got_ref[:, span].astype(F32)
            return jnp.where(k == 0, rows[:slots], rows[slots:])

        index = pick_ref[...]
        index = jnp.concatenate(
            [jnp.where(k == 0, index[i : i + 1], index[1 - i : 2 - i]) for i in range(2)], 1
        )
        row = lax.broadcasted_iota(jnp.int32, (t_dev, experts * slots), 0)
        hit = jnp.where(row == index, 1.0, 0.0).astype(BF16)
        copies = []
        for i in range(steps):
            span = pl.ds(i * chunk, chunk)
            values = jnp.concatenate([own(span), swapped_ref[:, span].astype(F32)], 0).astype(BF16)
            out_v[i] = jnp.dot(hit, values, preferred_element_type=F32).astype(BF16)
            copies.append(pltpu.make_async_copy(out_v.at[i], out_hbm.at[:, span], sems.at[i]))
            copies[-1].start()

        ones = jnp.where(lax.broadcasted_iota(jnp.int32, (8, LANES), 1) < 2, 1.0, 0.0).astype(BF16)

        def line(rows):
            dims = (((1,), (1,)), ((), ()))
            return lax.dot_general(ones, rows, dims, preferred_element_type=F32)[:1]

        last = pl.ds(width, LANES)
        mine = line(own(last).astype(BF16))
        theirs = line(swapped_ref[:, last])
        sums = jnp.concatenate([jnp.where(k == 0, mine, theirs), jnp.where(k == 0, theirs, mine)], 0)
        slot = lax.broadcasted_iota(jnp.int32, (experts, slots), 1)
        which = lax.broadcasted_iota(jnp.int32, (experts, slots), 0)
        count = jnp.where(which == 0, count_ref[0, 0], count_ref[0, 1])
        gates_ref[...] = jnp.where(slot < count, sums / gate_ref[...].astype(F32), 0.0)
        for copy in copies:
            copy.wait()

    return pl.pallas_call(
        body,
        in_specs=[IN_SMEM] + [IN_VMEM] * 4 + [IN_SMEM],
        out_specs=[ANYWHERE, IN_VMEM],
        out_shape=[
            jax.ShapeDtypeStruct((t_dev, width), BF16),
            jax.ShapeDtypeStruct((experts, slots), F32),
        ],
        scratch_shapes=[
            pltpu.VMEM((steps, t_dev, chunk), BF16),
            pltpu.SemaphoreType.DMA((steps,)),
        ],
        compiler_params=params(0, 32),
        name="unpick",
    )(lax.axis_index("k").reshape(1), got, swapped, gates, picks, counts)


def local(tokens, out_grad, gates, picks, counts, w_in, w_out):
    t_dev, width = tokens.shape
    experts, slots = picks.shape[1:]
    weight_in = w_in[0]
    weight_out = w_out[0]
    mine, other, both_dy = pick_rows(tokens, out_grad, gates[0], picks[0], counts)

    z_blocks = [mine, over_z(mine, 1), over_z(other, 2), over_z(other, 3)]
    below = lax.ppermute(both_dy, "x", UP)
    above = lax.ppermute(both_dy, "x", DOWN)
    pass_mine, pass_other = stack_rows([[(below, 0)], [(above, slots)]])
    far_mine = lax.ppermute(pass_mine, "x", UP)
    far_other = lax.ppermute(pass_other, "x", DOWN)
    (z_rows,) = stack_rows([[(v, 0) for v in z_blocks]], (pass_mine, pass_other))
    rows_x = lax.all_gather(z_rows, ("x", "c"), axis=0, tiled=True)

    x_mine, x_other = stack_rows(
        [
            [(both_dy, 0), (below, 0), (above, 0), (far_mine, 0)],
            [(both_dy, slots), (below, slots), (above, slots), (far_other, 0)],
        ]
    )
    pieces = []
    for block in (x_mine, over_z(x_mine, 1), over_z(x_other, 2), over_z(x_other, 3)):
        pieces += [block, lax.ppermute(block, "c", PAIR)]

    grads, rows_dy = grad_pass(pieces, weight_out)
    pre_x, hidden_x, hidden, payload, far_up, far_down = core_pass(
        rows_x, grads, rows_dy, weight_in, weight_out, slots
    )
    lefts, rights = (rows_x, rows_dy), (pre_x, hidden, hidden_x)
    half = width // 8
    far_up = lax.ppermute(far_up, "dp", UP)
    far_down = lax.ppermute(far_down, "dp", DOWN)
    near_up, near_down = slice_grads(
        lefts,
        rights,
        [(m, s, side, out, m * half, ()) for s, side, out in ((1, 1, 0), (3, 0, 1)) for m in range(2)],
        (),
        2,
    )
    near_up = lax.ppermute(near_up, "dp", UP)
    near_down = lax.ppermute(near_down, "dp", DOWN)
    got = lax.psum_scatter(payload, ("zz", "x", "c"), scatter_dimension=0, tiled=True)
    own_in, own_out = slice_grads(
        lefts,
        rights,
        [(m, 0, side, m, side * half, ()) for m in range(2) for side in range(2)],
        (),
        2,
    )
    sum_up, sum_down = slice_grads(
        lefts,
        rights,
        [
            (m, s, side, out, m * half, ((out, m * half),))
            for s, side, out in ((1, 0, 0), (3, 1, 1))
            for m in range(2)
        ],
        (far_up, far_down),
        2,
        after=(own_in,),
    )
    sum_up = lax.ppermute(sum_up, "dp", UP)
    sum_down = lax.ppermute(sum_down, "dp", DOWN)
    w_in_grad, w_out_grad = add_up(
        own_in, own_out, near_up, near_down, sum_up, sum_down
    )
    swapped = lax.ppermute(partner_rows(got, slots), "k", PAIR)
    tokens_grad, gates_grad = unpick(got, swapped, gates[0], picks[0], counts, t_dev, width)
    return (tokens_grad, gates_grad[None], w_in_grad[None], w_out_grad[None])


def solution(mesh):
    dp = mesh.devices.shape[1]
    fine = Mesh(mesh.devices.reshape(2, 2, 4, 2, dp), ("k", "zz", "x", "c", "dp"))
    expert = ("k", "zz", "x", "c")
    rows = expert + ("dp",)
    placed = (
        P(rows, None),
        P(rows, None),
        P(rows, None, None),
        P(rows, None, None),
        P(rows, None),
        P(expert, None, None),
        P(expert, None, None),
    )
    return jax.shard_map(
        local,
        mesh=fine,
        in_specs=placed,
        out_specs=(
            P(rows, None),
            P(rows, None, None),
            P(expert, "dp", None),
            P(expert, "dp", None),
        ),
        check_vma=False,
    )
```

time: 203 us -> 192 us (0.946)
  waiting for transfers between devices: 89.7 us -> 83 us
  other arithmetic: 3.53 us -> 0.65 us
    ppermute x6, waiting for transfers between devices: 39.3 us -> 28.9 us  [over_z(): return lax.ppermute(v, ('k', 'zz'), [(i, i ^ flip) for i in range(4)])]
    ppermute x4, waiting for transfers between devices: 0.01 us -> 2.71 us  [local(): pieces += [block, lax.ppermute(block, 'c', PAIR)]]
    unnamed x22 -> x34, local copies, waits for them, and re-layouts: 4.02 us -> 5.14 us
    pallas_call x4 -> x5, Pallas kernels: 35 us -> 34.2 us  [the longest x1 17.9 us: core_pass(): pl.pallas_call(body, in_specs=[IN_SMEM, IN_VMEM] + [ANYWHERE] * 4, out_sp...]
  transfers between devices with their start and end apart: 23 -> 23, of which waited for: 11 -> 14; matrix products, arithmetic and copies ran while one was open for 2% -> 0% of each run, Pallas kernels for 16% -> 16%
where the time goes in v3:
time: 192 us
  waiting for transfers between devices  83 us (43%)
  Pallas kernels  59.3 us (31%)
  starting transfers between devices  29.3 us (15%)
  between operations  14.3 us (7%)
  local copies, waits for them, and re-layouts  5.14 us (3%)
    reduce_scatter x1, waiting for transfers between devices, local(): lax.psum_scatter(payload, ('zz', 'x', 'c'), scatter_dimension=0, tiled=True)  33 us
    ppermute x6, waiting for transfers between devices, over_z(): return lax.ppermute(v, ('k', 'zz'), [(i, i ^ flip) for i in range(4)])  28.9 us
    pallas_call x3, Pallas kernels, slice_grads(): pl.pallas_call(body, in_specs=[IN_SMEM, ANYWHERE, ANYWHERE] + [IN_VMEM] *...  19.2 us
    pallas_call x1, Pallas kernels, core_pass(): pl.pallas_call(body, in_specs=[IN_SMEM, IN_VMEM] + [ANYWHERE] * 4, out_sp...  17.9 us
    ppermute x6, starting transfers between devices, over_z(): return lax.ppermute(v, ('k', 'zz'), [(i, i ^ flip) for i in range(4)])  9.68 us
    ppermute x1, waiting for transfers between devices, local(): far_up = lax.ppermute(far_up, 'dp', UP)  8.5 us
    pallas_call x1, Pallas kernels, grad_pass(): pl.pallas_call(body, in_specs=[IN_SMEM] + [ANYWHERE] * (parts + 1), out_s...  7.07 us
    pallas_call x1, Pallas kernels, pick_rows(): pl.pallas_call(body, in_specs=[IN_SMEM, IN_SMEM, ANYWHERE, ANYWHERE, IN_V...  5.48 us
  transfers between devices with their start and end apart: 23, of which 14 were waited for; matrix products, arithmetic and copies ran while one was open for 0% of the time, Pallas kernels for 16%

profile of v3, /device:TPU:0, one launch (start us, length us, event | category | flops | bytes accessed | tf_op | source)
XLA Modules:
  0.0 191.7 jit_solution(18423025362115079838)
XLA Ops:
  7.2 0.0 all-gather.2.cloned.1.call-start
  7.2 5.5 %pick_rows.1 = (bf16[24,5120]{1,0:T(8,128)(2,1)}, bf16[24,5120]{1,0:T(8,128)(2,1)}, bf16[48,3072]{1,0:T(8,128)(2,1)}) custom-call(s32[1]{0:T(128)} %bitcast.k_ref.place_ref, s32[1]{0:T(128)} %bitcast.3.dp_ref.place_ref, bf16[512,4096]{1,0:T(8,128)(2,1)} %t_hbm.1, bf16[512,4096]{1,0:T(8,128)(2,1)} %g_hbm.1, bf16[2,24]{1,0:T(2,128)(2,1)} %bitcast.14, ...), custom_call_target="tpu_custom_call" | custom-call | tf_op jit(solution)/shard_map/pick_rows/pallas_call | solution.py:81
  12.7 2.9 %collective-permute-start.1 = (bf16[48,3072]{1,0:T(8,128)(2,1)}, bf16[48,3072]{1,0:T(8,128)(2,1)S(1)}, u32[]{:S(2)}, u32[]{:S(2)}) collective-permute-start(bf16[48,3072]{1,0:T(8,128)(2,1)} %get-tuple-element.29.refs_0_.refs_4_), channel_id=1, source_target_pairs={{0,24},{8,0},{16,8},{24,16},{1,25},{9,1},{17,9},{25,17},{2,26},{10... | collective-permute-start | bytes 884744 | tf_op jit(solution)/shard_map/ppermute | solution.py:500
  15.6 1.9 collective-permute-start.11
  17.5 2.5 %collective-permute-start.13 = (bf16[24,5120]{1,0:T(8,128)(2,1)}, bf16[24,5120]{1,0:T(8,128)(2,1)S(1)}, u32[]{:S(2)}, u32[]{:S(2)}) collective-permute-start(bf16[24,5120]{1,0:T(8,128)(2,1)} %get-tuple-element.36), channel_id=1, source_target_pairs={{0,96},{32,64},{64,32},{96,0},{1,97},{33,65},{65,33},{97,1},{2,98}... | collective-permute-start | bytes 737288 | tf_op jit(solution)/shard_map/ppermute | solution.py:24
  20.1 1.1 collective-permute-start.12
  21.1 1.1 collective-permute-done.1.refs_1_.refs_2_.refs_6_
  22.2 3.3 %collective-permute-done.refs_0_.refs_1_.refs_5_ = bf16[48,3072]{1,0:T(8,128)(2,1)S(1)} collective-permute-done((bf16[48,3072]{1,0:T(8,128)(2,1)}, bf16[48,3072]{1,0:T(8,128)(2,1)S(1)}, u32[]{:S(2)}, u32[]{:S(2)}) %collective-permute-start) | collective-permute-done | bytes 294944 | tf_op jit(solution)/shard_map/ppermute | solution.py:499
  25.5 0.1 stack_rows.3
  25.7 4.6 %collective-permute-done.13.refs_3_ = bf16[24,5120]{1,0:T(8,128)(2,1)S(1)} collective-permute-done((bf16[24,5120]{1,0:T(8,128)(2,1)}, bf16[24,5120]{1,0:T(8,128)(2,1)S(1)}, u32[]{:S(2)}, u32[]{:S(2)}) %collective-permute-start.13) | collective-permute-done | bytes 245792 | tf_op jit(solution)/shard_map/ppermute | solution.py:24
  30.3 1.7 collective-permute-done.12.refs_2_
  32.0 0.9 copy-done.4
  32.9 1.1 stack_rows.5
  34.0 0.0 all-gather.2.cloned.1.call-update
  34.0 0.0 reduce-scatter.2.cloned.1.call-start
  34.1 0.5 collective-permute-start.2
  34.6 2.8 %collective-permute-start.3 = (bf16[24,3072]{1,0:T(8,128)(2,1)S(1)}, bf16[24,3072]{1,0:T(8,128)(2,1)S(1)}, u32[]{:S(2)}, u32[]{:S(2)}) collective-permute-start(bf16[24,3072]{1,0:T(8,128)(2,1)S(1)} %get-tuple-element.31.refs_5_), channel_id=1, source_target_pairs={{0,24},{8,0},{16,8},{24,16},{1,25},{9,1},{17,9},{25,17},{2,26},{10... | collective-permute-start | bytes 442376 | tf_op jit(solution)/shard_map/ppermute | solution.py:503
  37.4 3.1 %collective-permute-done.2.refs_3_ = bf16[24,3072]{1,0:T(8,128)(2,1)S(1)} collective-permute-done((bf16[24,3072]{1,0:T(8,128)(2,1)S(1)}, bf16[24,3072]{1,0:T(8,128)(2,1)S(1)}, u32[]{:S(2)}, u32[]{:S(2)}) %collective-permute-start.2) | collective-permute-done | bytes 147488 | tf_op jit(solution)/shard_map/ppermute | solution.py:502
  40.5 1.0 copy-done.2
  41.5 0.4 stack_rows.4
  41.9 0.0 copy-start.3
  41.9 2.0 %collective-permute-start.9 = (bf16[96,3072]{1,0:T(8,128)(2,1)S(1)}, bf16[96,3072]{1,0:T(8,128)(2,1)S(1)}, u32[]{:S(2)}, u32[]{:S(2)}) collective-permute-start(bf16[96,3072]{1,0:T(8,128)(2,1)S(1)} %get-tuple-element.33), channel_id=1, source_target_pairs={{0,96},{32,64},{64,32},{96,0},{1,97},{33,65},{65,33},{97,1},{2,98}... | collective-permute-start | bytes 1769480 | tf_op jit(solution)/shard_map/ppermute | solution.py:24
  43.9 0.1 collective-permute-start.7
  44.0 2.1 %collective-permute-start.5 = (bf16[96,3072]{1,0:T(8,128)(2,1)S(1)}, bf16[96,3072]{1,0:T(8,128)(2,1)S(1)}, u32[]{:S(2)}, u32[]{:S(2)}) collective-permute-start(bf16[96,3072]{1,0:T(8,128)(2,1)S(1)} %get-tuple-element.32.refs_0_), channel_id=1, source_target_pairs={{0,32},{32,0},{64,96},{96,64},{1,33},{33,1},{65,97},{97,65},{2,34}... | collective-permute-start | bytes 1769480 | tf_op jit(solution)/shard_map/ppermute | solution.py:24
  46.0 22.5 %collective-permute-done.9.refs_6_ = bf16[96,3072]{1,0:T(8,128)(2,1)S(1)} collective-permute-done((bf16[96,3072]{1,0:T(8,128)(2,1)S(1)}, bf16[96,3072]{1,0:T(8,128)(2,1)S(1)}, u32[]{:S(2)}, u32[]{:S(2)}) %collective-permute-start.9) | collective-permute-done | bytes 589856 | tf_op jit(solution)/shard_map/ppermute | solution.py:24
  68.6 0.5 collective-permute-start.8
  69.0 0.1 collective-permute-done.5.refs_2_
  69.2 0.2 collective-permute-start.6
  69.3 0.7 pad_add_fusion.place_ref
  70.0 0.0 collective-permute-done.4.refs_1_
  70.0 0.5 collective-permute-done.10.refs_7_
  70.5 1.3 collective-permute-done.8.refs_5_
  71.9 0.8 collective-permute-done.6.refs_3_
  72.7 7.1 %grad_pass.1 = (f32[768,512]{1,0:T(8,128)}, bf16[768,3072]{1,0:T(8,128)(2,1)}) custom-call(s32[1]{0:T(128)} %bitcast.3.dp_ref.place_ref, bf16[96,3072]{1,0:T(8,128)(2,1)} %copy-done.3, bf16[96,3072]{1,0:T(8,128)(2,1)} %copy-done.15, bf16[96,3072]{1,0:T(8,128)(2,1)} %copy-done.14, bf16[96,3072]{1,0:T(8,128)(2,1)} %collective-permute-done.6.refs_3_, ...), custom_call_target="tpu_custom_call" | custom-call | tf_op jit(solution)/shard_map/grad_pass/pallas_call | solution.py:174
  79.8 2.0 %all-gather.2.cloned.1.call-done.x_hbm = bf16[768,5120]{1,0:T(8,128)(2,1)} async-done(((bf16[96,5120]{1,0:T(8,128)(2,1)}), bf16[768,5120]{1,0:T(8,128)(2,1)}) %all-gather.2.cloned.1.call-update) | async-done | bytes 7864336 | tf_op jit(solution)/shard_map/all_gather | solution.py:505
  81.8 17.9 %core_pass.1 = (bf16[768,512]{1,0:T(8,128)(2,1)}, bf16[768,512]{1,0:T(8,128)(2,1)}, bf16[768,512]{1,0:T(8,128)(2,1)}, bf16[768,4224]{1,0:T(8,128)(2,1)}, bf16[10...) custom-call(s32[4]{0:T(128)} %pad_add_fusion.place_ref, f32[768,512]{1,0:T(8,128)} %get-tuple-element.34.grad_ref, ...), custom_call_target="tpu_custom_call" | custom-call | tf_op jit(solution)/shard_map/core_pass/pallas_call | solution.py:302
  99.7 0.0 reduce-scatter.2.cloned.1.call-update
  99.8 1.5 collective-permute-start.17
  101.3 1.8 collective-permute-start.18
  103.1 6.2 %slice_grads.4 = (bf16[1024,512]{1,0:T(8,128)(2,1)}, bf16[1024,512]{1,0:T(8,128)(2,1)}) custom-call(s32[1]{0:T(128)} %bitcast.3.dp_ref.place_ref, bf16[768,5120]{1,0:T(8,128)(2,1)} %all-gather.2.cloned.1.call-done.x_hbm, bf16[768,3072]{1,0:T(8,128)(2,1)} %get-tuple-element.37.dy_hbm, bf16[768,512]{1,0:T(8,128)(2,1)} %get-tuple-element.41.refs_0_, ...), custom_call_target="tpu_custom_call" | custom-call | tf_op jit(solution)/shard_map/slice_grads/pallas_call | solution.py:367
  109.3 0.3 collective-permute-start.15
  109.6 3.0 %collective-permute-start.16 = (bf16[1024,512]{1,0:T(8,128)(2,1)}, bf16[1024,512]{1,0:T(8,128)(2,1)S(1)}, u32[]{:S(2)}, u32[]{:S(2)}) collective-permute-start(bf16[1024,512]{1,0:T(8,128)(2,1)} %get-tuple-element.47), channel_id=1, source_target_pairs={{0,3},{1,0},{2,1},{3,2},{4,7},{5,4},{6,5},{7,6},{8,11},{9,8},{10,9... | collective-permute-start | bytes 3145736 | tf_op jit(solution)/shard_map/ppermute | solution.py:533
  112.6 6.2 %slice_grads.3 = (bf16[1024,512]{1,0:T(8,128)(2,1)}, bf16[1024,512]{1,0:T(8,128)(2,1)}) custom-call(s32[1]{0:T(128)} %bitcast.3.dp_ref.place_ref, bf16[768,5120]{1,0:T(8,128)(2,1)} %all-gather.2.cloned.1.call-done.x_hbm, bf16[768,3072]{1,0:T(8,128)(2,1)} %get-tuple-element.37.dy_hbm, bf16[768,512]{1,0:T(8,128)(2,1)} %get-tuple-element.41.refs_0_, ...), custom_call_target="tpu_custom_call" | custom-call | tf_op jit(solution)/shard_map/slice_grads/pallas_call | solution.py:367
  118.7 8.5 %collective-permute-done.17.refs_3_ = bf16[1024,512]{1,0:T(8,128)(2,1)S(1)} collective-permute-done((bf16[1024,512]{1,0:T(8,128)(2,1)}, bf16[1024,512]{1,0:T(8,128)(2,1)S(1)}, u32[]{:S(2)}, u32[]{:S(2)}) %collective-permute-start.17) | collective-permute-done | bytes 1048608 | tf_op jit(solution)/shard_map/ppermute | solution.py:523
  127.2 0.4 collective-permute-done.18.refs_4_
  127.6 0.6 copy-done.11
  128.2 6.8 %slice_grads.5 = (bf16[1024,512]{1,0:T(8,128)(2,1)}, bf16[1024,512]{1,0:T(8,128)(2,1)}) custom-call(s32[1]{0:T(128)} %bitcast.3.dp_ref.place_ref, bf16[768,5120]{1,0:T(8,128)(2,1)} %all-gather.2.cloned.1.call-done.x_hbm, bf16[768,3072]{1,0:T(8,128)(2,1)} %get-tuple-element.37.dy_hbm, bf16[768,512]{1,0:T(8,128)(2,1)} %get-tuple-element.41.refs_0_, ...), custom_call_target="tpu_custom_call" | custom-call | tf_op jit(solution)/shard_map/slice_grads/pallas_call | solution.py:367
  135.1 0.0 copy-start.5
  135.1 0.0 copy-start.6
  135.1 0.0 copy-start.7
  135.1 1.0 collective-permute-start.19
  136.1 2.3 %collective-permute-start.20 = (bf16[1024,512]{1,0:T(8,128)(2,1)}, bf16[1024,512]{1,0:T(8,128)(2,1)}, u32[]{:S(2)}, u32[]{:S(2)}) collective-permute-start(bf16[1024,512]{1,0:T(8,128)(2,1)} %get-tuple-element.51), channel_id=1, source_target_pairs={{0,3},{1,0},{2,1},{3,2},{4,7},{5,4},{6,5},{7,6},{8,11},{9,8},{10,9... | collective-permute-start | bytes 3145736 | tf_op jit(solution)/shard_map/ppermute | solution.py:555
  138.4 33.0 %reduce-scatter.2.cloned.1.call-done.got_ref = bf16[48,4224]{1,0:T(8,128)(2,1)} async-done(((bf16[768,4224]{1,0:T(8,128)(2,1)}), bf16[48,4224]{1,0:T(8,128)(2,1)}) %reduce-scatter.2.cloned.1.call-update) | async-done | bytes 405520 | tf_op jit(solution)/shard_map/reduce_scatter | solution.py:534
  171.4 1.0 copy-done
  172.4 0.2 partner_rows.1
  172.5 2.8 %collective-permute-start.14 = (bf16[24,4224]{1,0:T(8,128)(2,1)S(1)}, bf16[24,4224]{1,0:T(8,128)(2,1)S(1)}, u32[]{:S(2)}, u32[]{:S(2)}) collective-permute-start(bf16[24,4224]{1,0:T(8,128)(2,1)S(1)} %partner_rows.1), channel_id=1, source_target_pairs={{0,64},{64,0},{1,65},{65,1},{2,66},{66,2},{3,67},{67,3},{4,68},{68... | collective-permute-start | bytes 608264 | tf_op jit(solution)/shard_map/ppermute | solution.py:559
  175.3 0.0 collective-permute-done.15.near_up_ref
  175.3 0.0 collective-permute-done.19.sum_up_ref
  175.3 0.0 collective-permute-done.20.sum_down_ref
  175.3 0.9 copy-done.8
  176.3 0.3 copy-done.9
  176.6 0.3 copy-done.10
  177.0 4.3 %add_up.1 = (bf16[1024,512]{1,0:T(8,128)(2,1)}, bf16[1024,512]{1,0:T(8,128)(2,1)}) custom-call(bf16[1024,512]{1,0:T(8,128)(2,1)} %get-tuple-element.44.refs_5_.in_ref, bf16[1024,512]{1,0:T(8,128)(2,1)} %get-tuple-element.45.out_ref, bf16[1024,512]{1,0:T(8,128)(2,1)} %copy-done.8, bf16[1024,512]{1,0:T(8,128)(2,1)} %copy-done.9, bf16[1024,512]{1,0:T(8,128)(2,1)} %copy-done.10, ...), custom_call_target="tpu_custom_call" | custom-call | tf_op jit(solution)/shard_map/add_up/pallas_call | solution.py:402
  181.3 3.6 %unpick.1 = (bf16[512,4096]{1,0:T(8,128)(2,1)}, f32[2,24]{1,0:T(2,128)}) custom-call(s32[1]{0:T(128)} %bitcast.k_ref.place_ref, bf16[48,4224]{1,0:T(8,128)(2,1)S(1)} %copy-done.1, bf16[24,4224]{1,0:T(8,128)(2,1)S(1)} %collective-permute-done.14.swapped_ref, bf16[2,24]{1,0:T(2,128)(2,1)S(1)} %bitcast.15, s32[2,24]{1,0:T(2,128)S(1)} %bitcast.13, ...), custom_call_target="tpu_custom_call" | custom-call | tf_op jit(solution)/shard_map/unpick/pallas_call | solution.py:474
  (31 shorter events, 0.1 us)
Async XLA Ops:
  7.2 74.7 %all-gather.2.cloned.1.call-start = ((), (), s32[]{:S(2)}) async-start(), calls=%async_computation.1 | async-start | bytes 8847360 | tf_op jit(solution)/shard_map/all_gather | solution.py:505
  12.7 9.5 %collective-permute-start.1 = (bf16[48,3072]{1,0:T(8,128)(2,1)}, bf16[48,3072]{1,0:T(8,128)(2,1)S(1)}, u32[]{:S(2)}, u32[]{:S(2)}) collective-permute-start(bf16[48,3072]{1,0:T(8,128)(2,1)} %get-tuple-element.29.refs_0_.refs_4_), channel_id=1, source_target_pairs={{0,24},{8,0},{16,8},{24,16},{1,25},{9,1},{17,9},{25,17},{2,26},{10... | collective-permute-start | bytes 884744 | tf_op jit(solution)/shard_map/ppermute | solution.py:500
  15.6 9.9 %collective-permute-start = (bf16[48,3072]{1,0:T(8,128)(2,1)}, bf16[48,3072]{1,0:T(8,128)(2,1)S(1)}, u32[]{:S(2)}, u32[]{:S(2)}) collective-permute-start(bf16[48,3072]{1,0:T(8,128)(2,1)} %get-tuple-element.29.refs_0_.refs_4_), channel_id=1, source_target_pairs={{0,8},{8,16},{16,24},{24,0},{1,9},{9,17},{17,25},{25,1},{2,10},{10... | collective-permute-start | bytes 884744 | tf_op jit(solution)/shard_map/ppermute | solution.py:499
  15.6 10.0 %collective-permute-start.11 = (bf16[24,5120]{1,0:T(8,128)(2,1)}, bf16[24,5120]{1,0:T(8,128)(2,1)S(1)}, u32[]{:S(2)}, u32[]{:S(2)}) collective-permute-start(bf16[24,5120]{1,0:T(8,128)(2,1)} %get-tuple-element.35.refs_0_), channel_id=1, source_target_pairs={{0,32},{32,0},{64,96},{96,64},{1,33},{33,1},{65,97},{97,65},{2,34}... | collective-permute-start | bytes 737288 | tf_op jit(solution)/shard_map/ppermute | solution.py:24
  17.5 12.8 %collective-permute-start.13 = (bf16[24,5120]{1,0:T(8,128)(2,1)}, bf16[24,5120]{1,0:T(8,128)(2,1)S(1)}, u32[]{:S(2)}, u32[]{:S(2)}) collective-permute-start(bf16[24,5120]{1,0:T(8,128)(2,1)} %get-tuple-element.36), channel_id=1, source_target_pairs={{0,96},{32,64},{64,32},{96,0},{1,97},{33,65},{65,33},{97,1},{2,98}... | collective-permute-start | bytes 737288 | tf_op jit(solution)/shard_map/ppermute | solution.py:24
  20.1 11.9 %collective-permute-start.12 = (bf16[24,5120]{1,0:T(8,128)(2,1)}, bf16[24,5120]{1,0:T(8,128)(2,1)S(1)}, u32[]{:S(2)}, u32[]{:S(2)}) collective-permute-start(bf16[24,5120]{1,0:T(8,128)(2,1)} %get-tuple-element.36), channel_id=1, source_target_pairs={{0,64},{32,96},{64,0},{96,32},{1,65},{33,97},{65,1},{97,33},{2,66}... | collective-permute-start | bytes 737288 | tf_op jit(solution)/shard_map/ppermute | solution.py:24
  32.0 0.9 copy-start.4
  34.0 137.3 %reduce-scatter.2.cloned.1.call-start = ((), (), s32[]{:S(2)}) async-start(), calls=%async_computation.2 | async-start | bytes 6893568 | tf_op jit(solution)/shard_map/reduce_scatter | solution.py:534
  34.1 6.4 %collective-permute-start.2 = (bf16[24,3072]{1,0:T(8,128)(2,1)S(1)}, bf16[24,3072]{1,0:T(8,128)(2,1)S(1)}, u32[]{:S(2)}, u32[]{:S(2)}) collective-permute-start(bf16[24,3072]{1,0:T(8,128)(2,1)S(1)} %get-tuple-element.30.refs_4_), channel_id=1, source_target_pairs={{0,8},{8,16},{16,24},{24,0},{1,9},{9,17},{17,25},{25,1},{2,10},{10... | collective-permute-start | bytes 442376 | tf_op jit(solution)/shard_map/ppermute | solution.py:502
  34.6 5.9 %collective-permute-start.3 = (bf16[24,3072]{1,0:T(8,128)(2,1)S(1)}, bf16[24,3072]{1,0:T(8,128)(2,1)S(1)}, u32[]{:S(2)}, u32[]{:S(2)}) collective-permute-start(bf16[24,3072]{1,0:T(8,128)(2,1)S(1)} %get-tuple-element.31.refs_5_), channel_id=1, source_target_pairs={{0,24},{8,0},{16,8},{24,16},{1,25},{9,1},{17,9},{25,17},{2,26},{10... | collective-permute-start | bytes 442376 | tf_op jit(solution)/shard_map/ppermute | solution.py:503
  40.5 1.0 copy-start.2
  41.9 30.9 %copy-start.3 = (bf16[96,3072]{1,0:T(8,128)(2,1)}, bf16[96,3072]{1,0:T(8,128)(2,1)S(1)}, u32[]{:S(2)}) copy-start(bf16[96,3072]{1,0:T(8,128)(2,1)S(1)} %get-tuple-element.32.refs_0_) | copy-start | bytes 1769476
  41.9 26.7 %collective-permute-start.9 = (bf16[96,3072]{1,0:T(8,128)(2,1)S(1)}, bf16[96,3072]{1,0:T(8,128)(2,1)S(1)}, u32[]{:S(2)}, u32[]{:S(2)}) collective-permute-start(bf16[96,3072]{1,0:T(8,128)(2,1)S(1)} %get-tuple-element.33), channel_id=1, source_target_pairs={{0,96},{32,64},{64,32},{96,0},{1,97},{33,65},{65,33},{97,1},{2,98}... | collective-permute-start | bytes 1769480 | tf_op jit(solution)/shard_map/ppermute | solution.py:24
  43.9 24.7 %collective-permute-start.7 = (bf16[96,3072]{1,0:T(8,128)(2,1)S(1)}, bf16[96,3072]{1,0:T(8,128)(2,1)S(1)}, u32[]{:S(2)}, u32[]{:S(2)}) collective-permute-start(bf16[96,3072]{1,0:T(8,128)(2,1)S(1)} %get-tuple-element.33), channel_id=1, source_target_pairs={{0,64},{32,96},{64,0},{96,32},{1,65},{33,97},{65,1},{97,33},{2,66}... | collective-permute-start | bytes 1769480 | tf_op jit(solution)/shard_map/ppermute | solution.py:24
  44.0 25.2 %collective-permute-start.5 = (bf16[96,3072]{1,0:T(8,128)(2,1)S(1)}, bf16[96,3072]{1,0:T(8,128)(2,1)S(1)}, u32[]{:S(2)}, u32[]{:S(2)}) collective-permute-start(bf16[96,3072]{1,0:T(8,128)(2,1)S(1)} %get-tuple-element.32.refs_0_), channel_id=1, source_target_pairs={{0,32},{32,0},{64,96},{96,64},{1,33},{33,1},{65,97},{97,65},{2,34}... | collective-permute-start | bytes 1769480 | tf_op jit(solution)/shard_map/ppermute | solution.py:24
  46.0 23.9 %collective-permute-start.4 = (bf16[96,3072]{1,0:T(8,128)(2,1)S(1)}, bf16[96,3072]{1,0:T(8,128)(2,1)S(1)}, u32[]{:S(2)}, u32[]{:S(2)}) collective-permute-start(bf16[96,3072]{1,0:T(8,128)(2,1)S(1)} %get-tuple-element.32.refs_0_), channel_id=1, source_target_pairs={{0,4},{4,0},{1,5},{5,1},{2,6},{6,2},{3,7},{7,3},{8,12},{12,8},{9,1... | collective-permute-start | bytes 1769480 | tf_op jit(solution)/shard_map/ppermute | solution.py:515
  68.5 4.2 %copy-start.12 = (bf16[96,3072]{1,0:T(8,128)(2,1)}, bf16[96,3072]{1,0:T(8,128)(2,1)S(1)}, u32[]{:S(2)}) copy-start(bf16[96,3072]{1,0:T(8,128)(2,1)S(1)} %collective-permute-done.9.refs_6_) | copy-start | bytes 1769476
  68.5 2.0 %collective-permute-start.10 = (bf16[96,3072]{1,0:T(8,128)(2,1)S(1)}, bf16[96,3072]{1,0:T(8,128)(2,1)S(1)}, u32[]{:S(2)}, u32[]{:S(2)}) collective-permute-start(bf16[96,3072]{1,0:T(8,128)(2,1)S(1)} %collective-permute-done.9.refs_6_), channel_id=1, source_target_pairs={{0,4},{4,0},{1,5},{5,1},{2,6},{6,2},{3,7},{7,3},{8,12},{12,8},{9,1... | collective-permute-start | bytes 1769480 | tf_op jit(solution)/shard_map/ppermute | solution.py:515
  68.5 4.2 %copy-start.13 = (bf16[96,3072]{1,0:T(8,128)(2,1)}, bf16[96,3072]{1,0:T(8,128)(2,1)S(1)}, u32[]{:S(2)}) copy-start(bf16[96,3072]{1,0:T(8,128)(2,1)S(1)} %collective-permute-done.7.refs_4_) | copy-start | bytes 1769476
  68.6 3.3 %collective-permute-start.8 = (bf16[96,3072]{1,0:T(8,128)(2,1)S(1)}, bf16[96,3072]{1,0:T(8,128)(2,1)}, u32[]{:S(2)}, u32[]{:S(2)}) collective-permute-start(bf16[96,3072]{1,0:T(8,128)(2,1)S(1)} %collective-permute-done.7.refs_4_), channel_id=1, source_target_pairs={{0,4},{4,0},{1,5},{5,1},{2,6},{6,2},{3,7},{7,3},{8,12},{12,8},{9,1... | collective-permute-start | bytes 1769480 | tf_op jit(solution)/shard_map/ppermute | solution.py:515
  69.2 3.6 %copy-start.14 = (bf16[96,3072]{1,0:T(8,128)(2,1)}, bf16[96,3072]{1,0:T(8,128)(2,1)S(1)}, u32[]{:S(2)}) copy-start(bf16[96,3072]{1,0:T(8,128)(2,1)S(1)} %collective-permute-done.5.refs_2_) | copy-start | bytes 1769476
  69.2 3.6 %collective-permute-start.6 = (bf16[96,3072]{1,0:T(8,128)(2,1)S(1)}, bf16[96,3072]{1,0:T(8,128)(2,1)}, u32[]{:S(2)}, u32[]{:S(2)}) collective-permute-start(bf16[96,3072]{1,0:T(8,128)(2,1)S(1)} %collective-permute-done.5.refs_2_), channel_id=1, source_target_pairs={{0,4},{4,0},{1,5},{5,1},{2,6},{6,2},{3,7},{7,3},{8,12},{12,8},{9,1... | collective-permute-start | bytes 1769480 | tf_op jit(solution)/shard_map/ppermute | solution.py:515
  70.0 2.7 %copy-start.15 = (bf16[96,3072]{1,0:T(8,128)(2,1)}, bf16[96,3072]{1,0:T(8,128)(2,1)S(1)}, u32[]{:S(2)}) copy-start(bf16[96,3072]{1,0:T(8,128)(2,1)S(1)} %collective-permute-done.4.refs_1_) | copy-start | bytes 1769476
  70.5 2.2 %copy-start.16 = (bf16[96,3072]{1,0:T(8,128)(2,1)}, bf16[96,3072]{1,0:T(8,128)(2,1)S(1)}, u32[]{:S(2)}) copy-start(bf16[96,3072]{1,0:T(8,128)(2,1)S(1)} %collective-permute-done.10.refs_7_) | copy-start | bytes 1769476
  99.8 27.5 %collective-permute-start.17 = (bf16[1024,512]{1,0:T(8,128)(2,1)}, bf16[1024,512]{1,0:T(8,128)(2,1)S(1)}, u32[]{:S(2)}, u32[]{:S(2)}) collective-permute-start(bf16[1024,512]{1,0:T(8,128)(2,1)} %get-tuple-element.48), channel_id=1, source_target_pairs={{0,1},{1,2},{2,3},{3,0},{4,5},{5,6},{6,7},{7,4},{8,9},{9,10},{10,1... | collective-permute-start | bytes 3145736 | tf_op jit(solution)/shard_map/ppermute | solution.py:523
  101.3 26.3 %collective-permute-start.18 = (bf16[1024,512]{1,0:T(8,128)(2,1)}, bf16[1024,512]{1,0:T(8,128)(2,1)}, u32[]{:S(2)}, u32[]{:S(2)}) collective-permute-start(bf16[1024,512]{1,0:T(8,128)(2,1)} %get-tuple-element.49), channel_id=1, source_target_pairs={{0,3},{1,0},{2,1},{3,2},{4,7},{5,4},{6,5},{7,6},{8,11},{9,8},{10,9... | collective-permute-start | bytes 3145736 | tf_op jit(solution)/shard_map/ppermute | solution.py:524
  109.3 66.0 %collective-permute-start.15 = (bf16[1024,512]{1,0:T(8,128)(2,1)}, bf16[1024,512]{1,0:T(8,128)(2,1)S(1)}, u32[]{:S(2)}, u32[]{:S(2)}) collective-permute-start(bf16[1024,512]{1,0:T(8,128)(2,1)} %get-tuple-element.46), channel_id=1, source_target_pairs={{0,1},{1,2},{2,3},{3,0},{4,5},{5,6},{6,7},{7,4},{8,9},{9,10},{10,1... | collective-permute-start | bytes 3145736 | tf_op jit(solution)/shard_map/ppermute | solution.py:532
  109.6 65.7 %collective-permute-start.16 = (bf16[1024,512]{1,0:T(8,128)(2,1)}, bf16[1024,512]{1,0:T(8,128)(2,1)S(1)}, u32[]{:S(2)}, u32[]{:S(2)}) collective-permute-start(bf16[1024,512]{1,0:T(8,128)(2,1)} %get-tuple-element.47), channel_id=1, source_target_pairs={{0,3},{1,0},{2,1},{3,2},{4,7},{5,4},{6,5},{7,6},{8,11},{9,8},{10,9... | collective-permute-start | bytes 3145736 | tf_op jit(solution)/shard_map/ppermute | solution.py:533
  127.2 1.0 copy-start.11
  135.1 46.2 %copy-start.5 = (s32[1,2,24]{2,1,0:T(2,128)S(1)}, s32[1,2,24]{2,1,0:T(2,128)}, u32[]{:S(2)}) copy-start(s32[1,2,24]{2,1,0:T(2,128)} %param.10) | copy-start | bytes 580
  135.1 46.2 %copy-start.6 = (bf16[1,2,24]{2,1,0:T(2,128)(2,1)S(1)}, bf16[1,2,24]{2,1,0:T(2,128)(2,1)}, u32[]{:S(2)}) copy-start(bf16[1,2,24]{2,1,0:T(2,128)(2,1)} %param.9) | copy-start | bytes 292
  135.1 46.2 %copy-start.7 = (s32[1,2]{1,0:T(1,128)S(1)}, s32[1,2]{1,0:T(1,128)}, u32[]{:S(2)}) copy-start(s32[1,2]{1,0:T(1,128)} %count_ref.3) | copy-start | bytes 28
  135.1 40.2 %collective-permute-start.19 = (bf16[1024,512]{1,0:T(8,128)(2,1)}, bf16[1024,512]{1,0:T(8,128)(2,1)S(1)}, u32[]{:S(2)}, u32[]{:S(2)}) collective-permute-start(bf16[1024,512]{1,0:T(8,128)(2,1)} %get-tuple-element.50), channel_id=1, source_target_pairs={{0,1},{1,2},{2,3},{3,0},{4,5},{5,6},{6,7},{7,4},{8,9},{9,10},{10,1... | collective-permute-start | bytes 3145736 | tf_op jit(solution)/shard_map/ppermute | solution.py:554
  136.1 39.3 %collective-permute-start.20 = (bf16[1024,512]{1,0:T(8,128)(2,1)}, bf16[1024,512]{1,0:T(8,128)(2,1)}, u32[]{:S(2)}, u32[]{:S(2)}) collective-permute-start(bf16[1024,512]{1,0:T(8,128)(2,1)} %get-tuple-element.51), channel_id=1, source_target_pairs={{0,3},{1,0},{2,1},{3,2},{4,7},{5,4},{6,5},{7,6},{8,11},{9,8},{10,9... | collective-permute-start | bytes 3145736 | tf_op jit(solution)/shard_map/ppermute | solution.py:555
  171.4 1.0 copy-start
  172.4 8.9 %copy-start.1 = (bf16[48,4224]{1,0:T(8,128)(2,1)S(1)}, bf16[48,4224]{1,0:T(8,128)(2,1)}, u32[]{:S(2)}) copy-start(bf16[48,4224]{1,0:T(8,128)(2,1)} %reduce-scatter.2.cloned.1.call-done.got_ref) | copy-start | bytes 1216516
  172.5 8.7 %collective-permute-start.14 = (bf16[24,4224]{1,0:T(8,128)(2,1)S(1)}, bf16[24,4224]{1,0:T(8,128)(2,1)S(1)}, u32[]{:S(2)}, u32[]{:S(2)}) collective-permute-start(bf16[24,4224]{1,0:T(8,128)(2,1)S(1)} %partner_rows.1), channel_id=1, source_target_pairs={{0,64},{64,0},{1,65},{65,1},{2,66},{66,2},{3,67},{67,3},{4,68},{68... | collective-permute-start | bytes 608264 | tf_op jit(solution)/shard_map/ppermute | solution.py:559
  175.3 1.0 copy-start.8
  175.3 1.3 copy-start.9
  175.3 1.6 copy-start.10
Sparse Core Ops, SparseCore 0:
  34.1 47.6 all-gather.1
  99.9 71.4 reduce-scatter.1

commit v4 on v3

--- a/solution.py
+++ b/solution.py
@@ -197,20 +197,22 @@
     chunk = width // steps
     piece = chunk // 2
 
-    def body(place_ref, grad_ref, x_hbm, dy_hbm, w1_hbm, w2_hbm, *refs):
-        pre_x_ref, hidden_x_ref, hidden_ref, row_out, far_up, far_down = refs[:6]
+    def body(c_ref, k_ref, zz_ref, dp_ref, me_x_ref, grad_hbm, x_hbm, dy_hbm, w1_hbm, w2_hbm, *refs):
+        pre_x_out, hidden_x_out, hidden_out, row_out, far_up, far_down = refs[:6]
         (
-            x_v, dy_v, far_v, w1_v, w2_v, pre, grad, hid, pre_home, gate_home, pre_b, row_v, up_v, down_v, sems, out_sems,
+            x_v, dy_v, far_v, w1_v, w2_v, pre, grad, hid, pre_home, gate_home, pre_b, row_v, up_v, down_v, grad_ref,
+            pre_x_ref, hidden_x_ref, hidden_ref, sems, out_sems,
         ) = refs[6:]
-        core = place_ref[0]
-        spot = place_ref[1]
-        dp = place_ref[2]
-        me_x = place_ref[3]
+        core = c_ref[0]
+        spot = k_ref[0] * 2 + zz_ref[0]
+        dp = dp_ref[0]
+        me_x = me_x_ref[0]
         own = pl.ds(pl.multiple_of(dp * chunk, LANES), chunk)
         late = [
             pltpu.make_async_copy(x_hbm.at[:, pl.ds(width, chunk)], dy_v, sems.at[steps, 0]),
             pltpu.make_async_copy(w2_hbm.at[own, :], w2_v, sems.at[steps, 1]),
-            pltpu.make_async_copy(dy_hbm.at[:, pl.ds(chunk, chunk)], far_v, sems.at[steps, 2]),
+            pltpu.make_async_copy(grad_hbm, grad_ref, sems.at[steps, 2]),
+            pltpu.make_async_copy(dy_hbm.at[:, pl.ds(chunk, chunk)], far_v, sems.at[steps, 3]),
         ]
         copies = []
         for i in range(steps):
@@ -236,6 +238,7 @@
         late[0].wait()
         late[1].wait()
         grad[...] = jnp.dot(dy_v[...], w2_v[...], preferred_element_type=F32)
+        late[2].wait()
 
         @pl.loop(0, 4)
         def _(z):
@@ -267,9 +270,14 @@
         pre_x_ref[...] = pre[...].astype(BF16)
         hidden_x_ref[...] = grad[...].astype(BF16)
         hidden_ref[...] = hid[...].astype(BF16)
+        outs = []
+        for i, (value, out) in enumerate(
+            ((pre_x_ref, pre_x_out), (hidden_x_ref, hidden_x_out), (hidden_ref, hidden_out))
+        ):
+            outs.append(pltpu.make_async_copy(value, out, out_sems.at[2 + steps + i]))
+            outs[-1].start()
         pre_b[...] = pre_home[...].astype(BF16)
-        late[2].wait()
-        outs = []
+        late[3].wait()
         for side, buffer, out in ((0, up_v, far_up), (1, down_v, far_down)):
             start = pl.multiple_of(((dp + 2) % 4) * chunk + side * piece, LANES)
             buffer[:piece, :] = rows_dot(x_v[:, pl.ds(start, piece)], pre_x_ref[...]).astype(BF16)
@@ -291,18 +299,10 @@
         for copy in outs:
             copy.wait()
 
-    place = jnp.stack(
-        [
-            lax.axis_index("c"),
-            lax.axis_index("k") * 2 + lax.axis_index("zz"),
-            lax.axis_index("dp"),
-            lax.axis_index("x"),
-        ]
-    )
-    return pl.pallas_call(
-        body,
-        in_specs=[IN_SMEM, IN_VMEM] + [ANYWHERE] * 4,
-        out_specs=[IN_VMEM] * 3 + [ANYWHERE] * 3,
+    return pl.pallas_call(
+        body,
+        in_specs=[IN_SMEM] * 5 + [ANYWHERE] * 5,
+        out_specs=[ANYWHERE] * 6,
         out_shape=[
             jax.ShapeDtypeStruct((count, units), BF16),
             jax.ShapeDtypeStruct((count, units), BF16),
@@ -326,12 +326,19 @@
             pltpu.VMEM((count, width + LANES), BF16),
             pltpu.VMEM((chunk, units), BF16),
             pltpu.VMEM((chunk, units), BF16),
-            pltpu.SemaphoreType.DMA((steps + 1, 3)),
-            pltpu.SemaphoreType.DMA((2 + steps,)),
+            pltpu.VMEM((count, units), F32),
+            pltpu.VMEM((count, units), BF16),
+            pltpu.VMEM((count, units), BF16),
+            pltpu.VMEM((count, units), BF16),
+            pltpu.SemaphoreType.DMA((steps + 1, 4)),
+            pltpu.SemaphoreType.DMA((5 + steps,)),
         ],
         compiler_params=params(),
         name="core_pass",
-    )(place, grads, rows_x, rows_dy, weight_in, weight_out)
+    )(
+        *[lax.axis_index(name).reshape(1) for name in ("c", "k", "zz", "dp", "x")],
+        grads, rows_x, rows_dy, weight_in, weight_out,
+    )
 
 
 def slice_grads(lefts, rights, jobs, extras, out_count, kind=BF16, after=()):
@@ -382,30 +389,52 @@
     rows, units = own_in.shape
     half = rows // 2
 
-    def body(in_ref, out_ref, near_up_ref, near_down_ref, sum_up_ref, sum_down_ref, *results):
-        side = pl.program_id(0)
-        for m, (own, result) in enumerate(zip((in_ref, out_ref), results)):
-            span = slice(m * half, (m + 1) * half)
-
-            @pl.when(side == 0)
-            def _():
-                total = own[...].astype(F32) + near_down_ref[span, :].astype(F32) + sum_up_ref[span, :].astype(F32)
-                result[...] = total.astype(BF16)
-
-            @pl.when(side == 1)
-            def _():
-                total = own[...].astype(F32) + near_up_ref[span, :].astype(F32) + sum_down_ref[span, :].astype(F32)
-                result[...] = total.astype(BF16)
-
-    own_spec = pl.BlockSpec((half, units), lambda i: (i, 0))
-    full = pl.BlockSpec((rows, units), lambda i: (0, 0))
-    return pl.pallas_call(
-        body,
-        grid=(2,),
-        in_specs=[own_spec, own_spec] + [full] * 4,
-        out_specs=[own_spec, own_spec],
+    def body(*refs):
+        owns, terms, results = refs[:2], refs[2:6], refs[6:8]
+        own_v, term_v, sems, out_sems = refs[8:]
+        loads = []
+        for m in range(2):
+            for side, pair in enumerate(((1, 2), (0, 3))):
+                job = 2 * m + side
+                group = [pltpu.make_async_copy(owns[m].at[pl.ds(side * half, half), :], own_v.at[job], sems.at[job, 0])]
+                for i, term in enumerate(pair):
+                    group.append(
+                        pltpu.make_async_copy(
+                            terms[term].at[pl.ds(m * half, half), :], term_v.at[job, i], sems.at[job, 1 + i]
+                        )
+                    )
+                for copy in group:
+                    copy.start()
+                loads.append(group)
+        outs = []
+        for m in range(2):
+            for side in range(2):
+                job = 2 * m + side
+                for copy in loads[job]:
+                    copy.wait()
+                total = own_v[job].astype(F32) + term_v[job, 0].astype(F32) + term_v[job, 1].astype(F32)
+                own_v[job] = total.astype(BF16)
+                outs.append(
+                    pltpu.make_async_copy(
+                        own_v.at[job], results[m].at[pl.ds(side * half, half), :], out_sems.at[job]
+                    )
+                )
+                outs[-1].start()
+        for copy in outs:
+            copy.wait()
+
+    return pl.pallas_call(
+        body,
+        in_specs=[ANYWHERE] * 6,
+        out_specs=[ANYWHERE] * 2,
         out_shape=[jax.ShapeDtypeStruct((rows, units), BF16)] * 2,
-        compiler_params=params(1),
+        scratch_shapes=[
+            pltpu.VMEM((4, half, units), BF16),
+            pltpu.VMEM((4, 2, half, units), BF16),
+            pltpu.SemaphoreType.DMA((4, 3)),
+            pltpu.SemaphoreType.DMA((4,)),
+        ],
+        compiler_params=params(),
         name="add_up",
     )(own_in, own_out, near_up, near_down, sum_up, sum_down)
 

time: 192 us -> 189 us (0.984)
  Pallas kernels: 59.3 us -> 56.4 us
    pallas_call x2, Pallas kernels: 22.2 us -> 19.2 us  [the longest x1 15.1 us: core_pass(): pl.pallas_call(body, in_specs=[IN_SMEM] * 5 + [ANYWHERE] * 5, out_specs=[...]
where the time goes in v4:
time: 189 us
  waiting for transfers between devices  83.7 us (44%)
  Pallas kernels  56.4 us (30%)
  starting transfers between devices  29.3 us (16%)
  between operations  14.3 us (8%)
  local copies, waits for them, and re-layouts  5.12 us (3%)
    reduce_scatter x1, waiting for transfers between devices, local(): lax.psum_scatter(payload, ('zz', 'x', 'c'), scatter_dimension=0, tiled=True)  33 us
    ppermute x6, waiting for transfers between devices, over_z(): return lax.ppermute(v, ('k', 'zz'), [(i, i ^ flip) for i in range(4)])  28.9 us
    pallas_call x3, Pallas kernels, slice_grads(): pl.pallas_call(body, in_specs=[IN_SMEM, ANYWHERE, ANYWHERE] + [IN_VMEM] *...  19.2 us
    pallas_call x1, Pallas kernels, core_pass(): pl.pallas_call(body, in_specs=[IN_SMEM] * 5 + [ANYWHERE] * 5, out_specs=[...  15.1 us
    ppermute x6, starting transfers between devices, over_z(): return lax.ppermute(v, ('k', 'zz'), [(i, i ^ flip) for i in range(4)])  9.68 us
    ppermute x1, waiting for transfers between devices, local(): far_up = lax.ppermute(far_up, 'dp', UP)  8.5 us
    pallas_call x1, Pallas kernels, grad_pass(): pl.pallas_call(body, in_specs=[IN_SMEM] + [ANYWHERE] * (parts + 1), out_s...  7.07 us
    pallas_call x1, Pallas kernels, pick_rows(): pl.pallas_call(body, in_specs=[IN_SMEM, IN_SMEM, ANYWHERE, ANYWHERE, IN_V...  5.48 us
  transfers between devices with their start and end apart: 23, of which 14 were waited for; matrix products, arithmetic and copies ran while one was open for 0% of the time, Pallas kernels for 16%

profile of v4, /device:TPU:0, one launch (start us, length us, event | category | flops | bytes accessed | tf_op | source)
XLA Modules:
  0.0 188.9 jit_solution(87994286521861355)
XLA Ops:
  7.2 0.0 all-gather.2.cloned.1.call-start
  7.2 5.5 %pick_rows.1 = (bf16[24,5120]{1,0:T(8,128)(2,1)}, bf16[24,5120]{1,0:T(8,128)(2,1)}, bf16[48,3072]{1,0:T(8,128)(2,1)}) custom-call(s32[1]{0:T(128)} %bitcast.k_ref.place_ref, s32[1]{0:T(128)} %bitcast.3.dp_ref.place_ref, bf16[512,4096]{1,0:T(8,128)(2,1)} %t_hbm.1, bf16[512,4096]{1,0:T(8,128)(2,1)} %g_hbm.1, bf16[2,24]{1,0:T(2,128)(2,1)} %bitcast.14, ...), custom_call_target="tpu_custom_call" | custom-call | tf_op jit(solution)/shard_map/pick_rows/pallas_call | solution.py:81
  12.7 2.9 %collective-permute-start.1 = (bf16[48,3072]{1,0:T(8,128)(2,1)}, bf16[48,3072]{1,0:T(8,128)(2,1)S(1)}, u32[]{:S(2)}, u32[]{:S(2)}) collective-permute-start(bf16[48,3072]{1,0:T(8,128)(2,1)} %get-tuple-element.29.refs_0_.refs_4_), channel_id=1, source_target_pairs={{0,24},{8,0},{16,8},{24,16},{1,25},{9,1},{17,9},{25,17},{2,26},{10... | collective-permute-start | bytes 884744 | tf_op jit(solution)/shard_map/ppermute | solution.py:529
  15.6 0.0 collective-permute-start
  15.6 1.9 %collective-permute-start.11 = (bf16[24,5120]{1,0:T(8,128)(2,1)}, bf16[24,5120]{1,0:T(8,128)(2,1)S(1)}, u32[]{:S(2)}, u32[]{:S(2)}) collective-permute-start(bf16[24,5120]{1,0:T(8,128)(2,1)} %get-tuple-element.35.refs_0_), channel_id=1, source_target_pairs={{0,32},{32,0},{64,96},{96,64},{1,33},{33,1},{65,97},{97,65},{2,34}... | collective-permute-start | bytes 737288 | tf_op jit(solution)/shard_map/ppermute | solution.py:24
  17.5 2.5 %collective-permute-start.13 = (bf16[24,5120]{1,0:T(8,128)(2,1)}, bf16[24,5120]{1,0:T(8,128)(2,1)S(1)}, u32[]{:S(2)}, u32[]{:S(2)}) collective-permute-start(bf16[24,5120]{1,0:T(8,128)(2,1)} %get-tuple-element.36), channel_id=1, source_target_pairs={{0,96},{32,64},{64,32},{96,0},{1,97},{33,65},{65,33},{97,1},{2,98}... | collective-permute-start | bytes 737288 | tf_op jit(solution)/shard_map/ppermute | solution.py:24
  20.1 1.1 collective-permute-start.12
  21.1 1.1 collective-permute-done.1.refs_1_.refs_2_.refs_6_
  22.2 3.3 %collective-permute-done.refs_0_.refs_1_.refs_5_ = bf16[48,3072]{1,0:T(8,128)(2,1)S(1)} collective-permute-done((bf16[48,3072]{1,0:T(8,128)(2,1)}, bf16[48,3072]{1,0:T(8,128)(2,1)S(1)}, u32[]{:S(2)}, u32[]{:S(2)}) %collective-permute-start) | collective-permute-done | bytes 294944 | tf_op jit(solution)/shard_map/ppermute | solution.py:528
  25.5 0.1 stack_rows.3
  25.7 0.0 collective-permute-done.11.refs_1_
  25.7 4.6 %collective-permute-done.13.refs_3_ = bf16[24,5120]{1,0:T(8,128)(2,1)S(1)} collective-permute-done((bf16[24,5120]{1,0:T(8,128)(2,1)}, bf16[24,5120]{1,0:T(8,128)(2,1)S(1)}, u32[]{:S(2)}, u32[]{:S(2)}) %collective-permute-start.13) | collective-permute-done | bytes 245792 | tf_op jit(solution)/shard_map/ppermute | solution.py:24
  30.3 1.7 collective-permute-done.12.refs_2_
  32.0 0.9 copy-done.4
  32.9 1.1 stack_rows.5
  34.0 0.0 all-gather.2.cloned.1.call-update
  34.0 0.0 reduce-scatter.2.cloned.1.call-start
  34.1 0.5 collective-permute-start.2
  34.6 2.8 %collective-permute-start.3 = (bf16[24,3072]{1,0:T(8,128)(2,1)S(1)}, bf16[24,3072]{1,0:T(8,128)(2,1)S(1)}, u32[]{:S(2)}, u32[]{:S(2)}) collective-permute-start(bf16[24,3072]{1,0:T(8,128)(2,1)S(1)} %get-tuple-element.31.refs_5_), channel_id=1, source_target_pairs={{0,24},{8,0},{16,8},{24,16},{1,25},{9,1},{17,9},{25,17},{2,26},{10... | collective-permute-start | bytes 442376 | tf_op jit(solution)/shard_map/ppermute | solution.py:532
  37.4 3.1 %collective-permute-done.2.refs_3_ = bf16[24,3072]{1,0:T(8,128)(2,1)S(1)} collective-permute-done((bf16[24,3072]{1,0:T(8,128)(2,1)S(1)}, bf16[24,3072]{1,0:T(8,128)(2,1)S(1)}, u32[]{:S(2)}, u32[]{:S(2)}) %collective-permute-start.2) | collective-permute-done | bytes 147488 | tf_op jit(solution)/shard_map/ppermute | solution.py:531
  40.5 0.0 collective-permute-done.3.refs_7_
  40.5 1.0 copy-done.2
  41.5 0.4 stack_rows.4
  41.9 0.0 copy-start.3
  41.9 2.0 %collective-permute-start.9 = (bf16[96,3072]{1,0:T(8,128)(2,1)S(1)}, bf16[96,3072]{1,0:T(8,128)(2,1)S(1)}, u32[]{:S(2)}, u32[]{:S(2)}) collective-permute-start(bf16[96,3072]{1,0:T(8,128)(2,1)S(1)} %get-tuple-element.33), channel_id=1, source_target_pairs={{0,96},{32,64},{64,32},{96,0},{1,97},{33,65},{65,33},{97,1},{2,98}... | collective-permute-start | bytes 1769480 | tf_op jit(solution)/shard_map/ppermute | solution.py:24
  43.9 0.1 collective-permute-start.7
  44.0 2.1 %collective-permute-start.5 = (bf16[96,3072]{1,0:T(8,128)(2,1)S(1)}, bf16[96,3072]{1,0:T(8,128)(2,1)S(1)}, u32[]{:S(2)}, u32[]{:S(2)}) collective-permute-start(bf16[96,3072]{1,0:T(8,128)(2,1)S(1)} %get-tuple-element.32.refs_0_), channel_id=1, source_target_pairs={{0,32},{32,0},{64,96},{96,64},{1,33},{33,1},{65,97},{97,65},{2,34}... | collective-permute-start | bytes 1769480 | tf_op jit(solution)/shard_map/ppermute | solution.py:24
  46.0 0.0 collective-permute-start.4
  46.0 22.5 %collective-permute-done.9.refs_6_ = bf16[96,3072]{1,0:T(8,128)(2,1)S(1)} collective-permute-done((bf16[96,3072]{1,0:T(8,128)(2,1)S(1)}, bf16[96,3072]{1,0:T(8,128)(2,1)S(1)}, u32[]{:S(2)}, u32[]{:S(2)}) %collective-permute-start.9) | collective-permute-done | bytes 589856 | tf_op jit(solution)/shard_map/ppermute | solution.py:24
  68.5 0.0 collective-permute-start.10
  68.6 0.5 collective-permute-start.8
  69.0 0.1 collective-permute-done.5.refs_2_
  69.2 0.2 collective-permute-start.6
  69.3 1.2 collective-permute-done.10.refs_7_
  70.5 1.3 collective-permute-done.8.refs_5_
  71.9 0.8 collective-permute-done.6.refs_3_
  72.7 7.1 %grad_pass.1 = (f32[768,512]{1,0:T(8,128)}, bf16[768,3072]{1,0:T(8,128)(2,1)}) custom-call(s32[1]{0:T(128)} %bitcast.3.dp_ref.place_ref, bf16[96,3072]{1,0:T(8,128)(2,1)} %copy-done.3, bf16[96,3072]{1,0:T(8,128)(2,1)} %copy-done.15, bf16[96,3072]{1,0:T(8,128)(2,1)} %copy-done.14, bf16[96,3072]{1,0:T(8,128)(2,1)} %collective-permute-done.6.refs_3_, ...), custom_call_target="tpu_custom_call" | custom-call | tf_op jit(solution)/shard_map/grad_pass/pallas_call | solution.py:174
  79.8 2.0 %all-gather.2.cloned.1.call-done.x_hbm = bf16[768,5120]{1,0:T(8,128)(2,1)} async-done(((bf16[96,5120]{1,0:T(8,128)(2,1)}), bf16[768,5120]{1,0:T(8,128)(2,1)}) %all-gather.2.cloned.1.call-update) | async-done | bytes 7864336 | tf_op jit(solution)/shard_map/all_gather | solution.py:534
  81.8 15.1 %core_pass.1 = (bf16[768,512]{1,0:T(8,128)(2,1)}, bf16[768,512]{1,0:T(8,128)(2,1)}, bf16[768,512]{1,0:T(8,128)(2,1)}, bf16[768,4224]{1,0:T(8,128)(2,1)}, bf16[10...) custom-call(s32[1]{0:T(128)} %bitcast.1.c_ref, s32[1]{0:T(128)} %bitcast.k_ref.place_ref, s32[1]{0:T(128)} %bitcast.2.zz_ref, ...), custom_call_target="tpu_custom_call" | custom-call | tf_op jit(solution)/shard_map/core_pass/pallas_call | solution.py:302
  96.9 0.0 reduce-scatter.2.cloned.1.call-update
  97.0 1.6 collective-permute-start.17
  98.5 1.8 collective-permute-start.18
  100.3 6.2 %slice_grads.4 = (bf16[1024,512]{1,0:T(8,128)(2,1)}, bf16[1024,512]{1,0:T(8,128)(2,1)}) custom-call(s32[1]{0:T(128)} %bitcast.3.dp_ref.place_ref, bf16[768,5120]{1,0:T(8,128)(2,1)} %all-gather.2.cloned.1.call-done.x_hbm, bf16[768,3072]{1,0:T(8,128)(2,1)} %get-tuple-element.37.dy_hbm, bf16[768,512]{1,0:T(8,128)(2,1)} %get-tuple-element.41.refs_0_, ...), custom_call_target="tpu_custom_call" | custom-call | tf_op jit(solution)/shard_map/slice_grads/pallas_call | solution.py:374
  106.4 0.4 collective-permute-start.15
  106.8 3.0 %collective-permute-start.16 = (bf16[1024,512]{1,0:T(8,128)(2,1)}, bf16[1024,512]{1,0:T(8,128)(2,1)S(1)}, u32[]{:S(2)}, u32[]{:S(2)}) collective-permute-start(bf16[1024,512]{1,0:T(8,128)(2,1)} %get-tuple-element.47), channel_id=1, source_target_pairs={{0,3},{1,0},{2,1},{3,2},{4,7},{5,4},{6,5},{7,6},{8,11},{9,8},{10,9... | collective-permute-start | bytes 3145736 | tf_op jit(solution)/shard_map/ppermute | solution.py:562
  109.8 6.2 %slice_grads.3 = (bf16[1024,512]{1,0:T(8,128)(2,1)}, bf16[1024,512]{1,0:T(8,128)(2,1)}) custom-call(s32[1]{0:T(128)} %bitcast.3.dp_ref.place_ref, bf16[768,5120]{1,0:T(8,128)(2,1)} %all-gather.2.cloned.1.call-done.x_hbm, bf16[768,3072]{1,0:T(8,128)(2,1)} %get-tuple-element.37.dy_hbm, bf16[768,512]{1,0:T(8,128)(2,1)} %get-tuple-element.41.refs_0_, ...), custom_call_target="tpu_custom_call" | custom-call | tf_op jit(solution)/shard_map/slice_grads/pallas_call | solution.py:374
  115.9 8.5 %collective-permute-done.17.refs_3_ = bf16[1024,512]{1,0:T(8,128)(2,1)S(1)} collective-permute-done((bf16[1024,512]{1,0:T(8,128)(2,1)}, bf16[1024,512]{1,0:T(8,128)(2,1)S(1)}, u32[]{:S(2)}, u32[]{:S(2)}) %collective-permute-start.17) | collective-permute-done | bytes 1048608 | tf_op jit(solution)/shard_map/ppermute | solution.py:552
  124.4 0.4 collective-permute-done.18.refs_4_
  124.8 0.6 copy-done.11
  125.4 6.8 %slice_grads.5 = (bf16[1024,512]{1,0:T(8,128)(2,1)}, bf16[1024,512]{1,0:T(8,128)(2,1)}) custom-call(s32[1]{0:T(128)} %bitcast.3.dp_ref.place_ref, bf16[768,5120]{1,0:T(8,128)(2,1)} %all-gather.2.cloned.1.call-done.x_hbm, bf16[768,3072]{1,0:T(8,128)(2,1)} %get-tuple-element.37.dy_hbm, bf16[768,512]{1,0:T(8,128)(2,1)} %get-tuple-element.41.refs_0_, ...), custom_call_target="tpu_custom_call" | custom-call | tf_op jit(solution)/shard_map/slice_grads/pallas_call | solution.py:374
  132.2 0.0 copy-start.5
  132.2 0.0 copy-start.6
  132.3 0.0 copy-start.7
  132.3 1.0 collective-permute-start.19
  133.3 2.3 %collective-permute-start.20 = (bf16[1024,512]{1,0:T(8,128)(2,1)}, bf16[1024,512]{1,0:T(8,128)(2,1)}, u32[]{:S(2)}, u32[]{:S(2)}) collective-permute-start(bf16[1024,512]{1,0:T(8,128)(2,1)} %get-tuple-element.51), channel_id=1, source_target_pairs={{0,3},{1,0},{2,1},{3,2},{4,7},{5,4},{6,5},{7,6},{8,11},{9,8},{10,9... | collective-permute-start | bytes 3145736 | tf_op jit(solution)/shard_map/ppermute | solution.py:584
  135.6 33.0 %reduce-scatter.2.cloned.1.call-done.got_ref = bf16[48,4224]{1,0:T(8,128)(2,1)} async-done(((bf16[768,4224]{1,0:T(8,128)(2,1)}), bf16[48,4224]{1,0:T(8,128)(2,1)}) %reduce-scatter.2.cloned.1.call-update) | async-done | bytes 405520 | tf_op jit(solution)/shard_map/reduce_scatter | solution.py:563
  168.5 1.0 copy-done
  169.5 0.2 partner_rows.1
  169.7 2.8 %collective-permute-start.14 = (bf16[24,4224]{1,0:T(8,128)(2,1)S(1)}, bf16[24,4224]{1,0:T(8,128)(2,1)S(1)}, u32[]{:S(2)}, u32[]{:S(2)}) collective-permute-start(bf16[24,4224]{1,0:T(8,128)(2,1)S(1)} %partner_rows.1), channel_id=1, source_target_pairs={{0,64},{64,0},{1,65},{65,1},{2,66},{66,2},{3,67},{67,3},{4,68},{68... | collective-permute-start | bytes 608264 | tf_op jit(solution)/shard_map/ppermute | solution.py:588
  172.6 0.9 copy-done.8
  173.5 0.3 copy-done.9
  173.8 0.3 copy-done.10
  174.2 4.2 %add_up.1 = (bf16[1024,512]{1,0:T(8,128)(2,1)}, bf16[1024,512]{1,0:T(8,128)(2,1)}) custom-call(bf16[1024,512]{1,0:T(8,128)(2,1)} %get-tuple-element.44.refs_5_.refs_0_, bf16[1024,512]{1,0:T(8,128)(2,1)} %get-tuple-element.45.refs_1_, bf16[1024,512]{1,0:T(8,128)(2,1)} %copy-done.8, bf16[1024,512]{1,0:T(8,128)(2,1)} %copy-done.9, ...), custom_call_target="tpu_custom_call" | custom-call | tf_op jit(solution)/shard_map/add_up/pallas_call | solution.py:426
  178.4 3.6 %unpick.1 = (bf16[512,4096]{1,0:T(8,128)(2,1)}, f32[2,24]{1,0:T(2,128)}) custom-call(s32[1]{0:T(128)} %bitcast.k_ref.place_ref, bf16[48,4224]{1,0:T(8,128)(2,1)S(1)} %copy-done.1, bf16[24,4224]{1,0:T(8,128)(2,1)S(1)} %collective-permute-done.14.swapped_ref, bf16[2,24]{1,0:T(2,128)(2,1)S(1)} %bitcast.15, s32[2,24]{1,0:T(2,128)S(1)} %bitcast.13, ...), custom_call_target="tpu_custom_call" | custom-call | tf_op jit(solution)/shard_map/unpick/pallas_call | solution.py:503
  (30 shorter events, 0.1 us)
Async XLA Ops:
  7.2 74.7 %all-gather.2.cloned.1.call-start = ((), (), s32[]{:S(2)}) async-start(), calls=%async_computation.1 | async-start | bytes 8847360 | tf_op jit(solution)/shard_map/all_gather | solution.py:534
  12.7 9.5 %collective-permute-start.1 = (bf16[48,3072]{1,0:T(8,128)(2,1)}, bf16[48,3072]{1,0:T(8,128)(2,1)S(1)}, u32[]{:S(2)}, u32[]{:S(2)}) collective-permute-start(bf16[48,3072]{1,0:T(8,128)(2,1)} %get-tuple-element.29.refs_0_.refs_4_), channel_id=1, source_target_pairs={{0,24},{8,0},{16,8},{24,16},{1,25},{9,1},{17,9},{25,17},{2,26},{10... | collective-permute-start | bytes 884744 | tf_op jit(solution)/shard_map/ppermute | solution.py:529
  15.6 9.9 %collective-permute-start = (bf16[48,3072]{1,0:T(8,128)(2,1)}, bf16[48,3072]{1,0:T(8,128)(2,1)S(1)}, u32[]{:S(2)}, u32[]{:S(2)}) collective-permute-start(bf16[48,3072]{1,0:T(8,128)(2,1)} %get-tuple-element.29.refs_0_.refs_4_), channel_id=1, source_target_pairs={{0,8},{8,16},{16,24},{24,0},{1,9},{9,17},{17,25},{25,1},{2,10},{10... | collective-permute-start | bytes 884744 | tf_op jit(solution)/shard_map/ppermute | solution.py:528
  15.6 10.0 %collective-permute-start.11 = (bf16[24,5120]{1,0:T(8,128)(2,1)}, bf16[24,5120]{1,0:T(8,128)(2,1)S(1)}, u32[]{:S(2)}, u32[]{:S(2)}) collective-permute-start(bf16[24,5120]{1,0:T(8,128)(2,1)} %get-tuple-element.35.refs_0_), channel_id=1, source_target_pairs={{0,32},{32,0},{64,96},{96,64},{1,33},{33,1},{65,97},{97,65},{2,34}... | collective-permute-start | bytes 737288 | tf_op jit(solution)/shard_map/ppermute | solution.py:24
  17.5 12.8 %collective-permute-start.13 = (bf16[24,5120]{1,0:T(8,128)(2,1)}, bf16[24,5120]{1,0:T(8,128)(2,1)S(1)}, u32[]{:S(2)}, u32[]{:S(2)}) collective-permute-start(bf16[24,5120]{1,0:T(8,128)(2,1)} %get-tuple-element.36), channel_id=1, source_target_pairs={{0,96},{32,64},{64,32},{96,0},{1,97},{33,65},{65,33},{97,1},{2,98}... | collective-permute-start | bytes 737288 | tf_op jit(solution)/shard_map/ppermute | solution.py:24
  20.1 11.9 %collective-permute-start.12 = (bf16[24,5120]{1,0:T(8,128)(2,1)}, bf16[24,5120]{1,0:T(8,128)(2,1)S(1)}, u32[]{:S(2)}, u32[]{:S(2)}) collective-permute-start(bf16[24,5120]{1,0:T(8,128)(2,1)} %get-tuple-element.36), channel_id=1, source_target_pairs={{0,64},{32,96},{64,0},{96,32},{1,65},{33,97},{65,1},{97,33},{2,66}... | collective-permute-start | bytes 737288 | tf_op jit(solution)/shard_map/ppermute | solution.py:24
  32.0 0.9 copy-start.4
  34.0 134.5 %reduce-scatter.2.cloned.1.call-start = ((), (), s32[]{:S(2)}) async-start(), calls=%async_computation.2 | async-start | bytes 6893568 | tf_op jit(solution)/shard_map/reduce_scatter | solution.py:563
  34.1 6.4 %collective-permute-start.2 = (bf16[24,3072]{1,0:T(8,128)(2,1)S(1)}, bf16[24,3072]{1,0:T(8,128)(2,1)S(1)}, u32[]{:S(2)}, u32[]{:S(2)}) collective-permute-start(bf16[24,3072]{1,0:T(8,128)(2,1)S(1)} %get-tuple-element.30.refs_4_), channel_id=1, source_target_pairs={{0,8},{8,16},{16,24},{24,0},{1,9},{9,17},{17,25},{25,1},{2,10},{10... | collective-permute-start | bytes 442376 | tf_op jit(solution)/shard_map/ppermute | solution.py:531
  34.6 5.9 %collective-permute-start.3 = (bf16[24,3072]{1,0:T(8,128)(2,1)S(1)}, bf16[24,3072]{1,0:T(8,128)(2,1)S(1)}, u32[]{:S(2)}, u32[]{:S(2)}) collective-permute-start(bf16[24,3072]{1,0:T(8,128)(2,1)S(1)} %get-tuple-element.31.refs_5_), channel_id=1, source_target_pairs={{0,24},{8,0},{16,8},{24,16},{1,25},{9,1},{17,9},{25,17},{2,26},{10... | collective-permute-start | bytes 442376 | tf_op jit(solution)/shard_map/ppermute | solution.py:532
  40.5 1.0 copy-start.2
  41.9 30.9 %copy-start.3 = (bf16[96,3072]{1,0:T(8,128)(2,1)}, bf16[96,3072]{1,0:T(8,128)(2,1)S(1)}, u32[]{:S(2)}) copy-start(bf16[96,3072]{1,0:T(8,128)(2,1)S(1)} %get-tuple-element.32.refs_0_) | copy-start | bytes 1769476
  41.9 26.7 %collective-permute-start.9 = (bf16[96,3072]{1,0:T(8,128)(2,1)S(1)}, bf16[96,3072]{1,0:T(8,128)(2,1)S(1)}, u32[]{:S(2)}, u32[]{:S(2)}) collective-permute-start(bf16[96,3072]{1,0:T(8,128)(2,1)S(1)} %get-tuple-element.33), channel_id=1, source_target_pairs={{0,96},{32,64},{64,32},{96,0},{1,97},{33,65},{65,33},{97,1},{2,98}... | collective-permute-start | bytes 1769480 | tf_op jit(solution)/shard_map/ppermute | solution.py:24
  43.9 24.7 %collective-permute-start.7 = (bf16[96,3072]{1,0:T(8,128)(2,1)S(1)}, bf16[96,3072]{1,0:T(8,128)(2,1)S(1)}, u32[]{:S(2)}, u32[]{:S(2)}) collective-permute-start(bf16[96,3072]{1,0:T(8,128)(2,1)S(1)} %get-tuple-element.33), channel_id=1, source_target_pairs={{0,64},{32,96},{64,0},{96,32},{1,65},{33,97},{65,1},{97,33},{2,66}... | collective-permute-start | bytes 1769480 | tf_op jit(solution)/shard_map/ppermute | solution.py:24
  44.0 25.2 %collective-permute-start.5 = (bf16[96,3072]{1,0:T(8,128)(2,1)S(1)}, bf16[96,3072]{1,0:T(8,128)(2,1)S(1)}, u32[]{:S(2)}, u32[]{:S(2)}) collective-permute-start(bf16[96,3072]{1,0:T(8,128)(2,1)S(1)} %get-tuple-element.32.refs_0_), channel_id=1, source_target_pairs={{0,32},{32,0},{64,96},{96,64},{1,33},{33,1},{65,97},{97,65},{2,34}... | collective-permute-start | bytes 1769480 | tf_op jit(solution)/shard_map/ppermute | solution.py:24
  46.0 23.3 %collective-permute-start.4 = (bf16[96,3072]{1,0:T(8,128)(2,1)S(1)}, bf16[96,3072]{1,0:T(8,128)(2,1)S(1)}, u32[]{:S(2)}, u32[]{:S(2)}) collective-permute-start(bf16[96,3072]{1,0:T(8,128)(2,1)S(1)} %get-tuple-element.32.refs_0_), channel_id=1, source_target_pairs={{0,4},{4,0},{1,5},{5,1},{2,6},{6,2},{3,7},{7,3},{8,12},{12,8},{9,1... | collective-permute-start | bytes 1769480 | tf_op jit(solution)/shard_map/ppermute | solution.py:544
  68.5 4.2 %copy-start.12 = (bf16[96,3072]{1,0:T(8,128)(2,1)}, bf16[96,3072]{1,0:T(8,128)(2,1)S(1)}, u32[]{:S(2)}) copy-start(bf16[96,3072]{1,0:T(8,128)(2,1)S(1)} %collective-permute-done.9.refs_6_) | copy-start | bytes 1769476
  68.5 2.0 %collective-permute-start.10 = (bf16[96,3072]{1,0:T(8,128)(2,1)S(1)}, bf16[96,3072]{1,0:T(8,128)(2,1)S(1)}, u32[]{:S(2)}, u32[]{:S(2)}) collective-permute-start(bf16[96,3072]{1,0:T(8,128)(2,1)S(1)} %collective-permute-done.9.refs_6_), channel_id=1, source_target_pairs={{0,4},{4,0},{1,5},{5,1},{2,6},{6,2},{3,7},{7,3},{8,12},{12,8},{9,1... | collective-permute-start | bytes 1769480 | tf_op jit(solution)/shard_map/ppermute | solution.py:544
  68.5 4.2 %copy-start.13 = (bf16[96,3072]{1,0:T(8,128)(2,1)}, bf16[96,3072]{1,0:T(8,128)(2,1)S(1)}, u32[]{:S(2)}) copy-start(bf16[96,3072]{1,0:T(8,128)(2,1)S(1)} %collective-permute-done.7.refs_4_) | copy-start | bytes 1769476
  68.6 3.3 %collective-permute-start.8 = (bf16[96,3072]{1,0:T(8,128)(2,1)S(1)}, bf16[96,3072]{1,0:T(8,128)(2,1)}, u32[]{:S(2)}, u32[]{:S(2)}) collective-permute-start(bf16[96,3072]{1,0:T(8,128)(2,1)S(1)} %collective-permute-done.7.refs_4_), channel_id=1, source_target_pairs={{0,4},{4,0},{1,5},{5,1},{2,6},{6,2},{3,7},{7,3},{8,12},{12,8},{9,1... | collective-permute-start | bytes 1769480 | tf_op jit(solution)/shard_map/ppermute | solution.py:544
  69.2 3.6 %copy-start.14 = (bf16[96,3072]{1,0:T(8,128)(2,1)}, bf16[96,3072]{1,0:T(8,128)(2,1)S(1)}, u32[]{:S(2)}) copy-start(bf16[96,3072]{1,0:T(8,128)(2,1)S(1)} %collective-permute-done.5.refs_2_) | copy-start | bytes 1769476
  69.2 3.6 %collective-permute-start.6 = (bf16[96,3072]{1,0:T(8,128)(2,1)S(1)}, bf16[96,3072]{1,0:T(8,128)(2,1)}, u32[]{:S(2)}, u32[]{:S(2)}) collective-permute-start(bf16[96,3072]{1,0:T(8,128)(2,1)S(1)} %collective-permute-done.5.refs_2_), channel_id=1, source_target_pairs={{0,4},{4,0},{1,5},{5,1},{2,6},{6,2},{3,7},{7,3},{8,12},{12,8},{9,1... | collective-permute-start | bytes 1769480 | tf_op jit(solution)/shard_map/ppermute | solution.py:544
  69.3 3.4 %copy-start.15 = (bf16[96,3072]{1,0:T(8,128)(2,1)}, bf16[96,3072]{1,0:T(8,128)(2,1)S(1)}, u32[]{:S(2)}) copy-start(bf16[96,3072]{1,0:T(8,128)(2,1)S(1)} %collective-permute-done.4.refs_1_) | copy-start | bytes 1769476
  70.5 2.2 %copy-start.16 = (bf16[96,3072]{1,0:T(8,128)(2,1)}, bf16[96,3072]{1,0:T(8,128)(2,1)S(1)}, u32[]{:S(2)}) copy-start(bf16[96,3072]{1,0:T(8,128)(2,1)S(1)} %collective-permute-done.10.refs_7_) | copy-start | bytes 1769476
  97.0 27.5 %collective-permute-start.17 = (bf16[1024,512]{1,0:T(8,128)(2,1)}, bf16[1024,512]{1,0:T(8,128)(2,1)S(1)}, u32[]{:S(2)}, u32[]{:S(2)}) collective-permute-start(bf16[1024,512]{1,0:T(8,128)(2,1)} %get-tuple-element.48), channel_id=1, source_target_pairs={{0,1},{1,2},{2,3},{3,0},{4,5},{5,6},{6,7},{7,4},{8,9},{9,10},{10,1... | collective-permute-start | bytes 3145736 | tf_op jit(solution)/shard_map/ppermute | solution.py:552
  98.5 26.3 %collective-permute-start.18 = (bf16[1024,512]{1,0:T(8,128)(2,1)}, bf16[1024,512]{1,0:T(8,128)(2,1)}, u32[]{:S(2)}, u32[]{:S(2)}) collective-permute-start(bf16[1024,512]{1,0:T(8,128)(2,1)} %get-tuple-element.49), channel_id=1, source_target_pairs={{0,3},{1,0},{2,1},{3,2},{4,7},{5,4},{6,5},{7,6},{8,11},{9,8},{10,9... | collective-permute-start | bytes 3145736 | tf_op jit(solution)/shard_map/ppermute | solution.py:553
  106.4 66.1 %collective-permute-start.15 = (bf16[1024,512]{1,0:T(8,128)(2,1)}, bf16[1024,512]{1,0:T(8,128)(2,1)S(1)}, u32[]{:S(2)}, u32[]{:S(2)}) collective-permute-start(bf16[1024,512]{1,0:T(8,128)(2,1)} %get-tuple-element.46), channel_id=1, source_target_pairs={{0,1},{1,2},{2,3},{3,0},{4,5},{5,6},{6,7},{7,4},{8,9},{9,10},{10,1... | collective-permute-start | bytes 3145736 | tf_op jit(solution)/shard_map/ppermute | solution.py:561
  106.8 65.7 %collective-permute-start.16 = (bf16[1024,512]{1,0:T(8,128)(2,1)}, bf16[1024,512]{1,0:T(8,128)(2,1)S(1)}, u32[]{:S(2)}, u32[]{:S(2)}) collective-permute-start(bf16[1024,512]{1,0:T(8,128)(2,1)} %get-tuple-element.47), channel_id=1, source_target_pairs={{0,3},{1,0},{2,1},{3,2},{4,7},{5,4},{6,5},{7,6},{8,11},{9,8},{10,9... | collective-permute-start | bytes 3145736 | tf_op jit(solution)/shard_map/ppermute | solution.py:562
  124.4 1.0 copy-start.11
  132.2 46.1 %copy-start.5 = (s32[1,2,24]{2,1,0:T(2,128)S(1)}, s32[1,2,24]{2,1,0:T(2,128)}, u32[]{:S(2)}) copy-start(s32[1,2,24]{2,1,0:T(2,128)} %param.10) | copy-start | bytes 580
  132.2 46.1 %copy-start.6 = (bf16[1,2,24]{2,1,0:T(2,128)(2,1)S(1)}, bf16[1,2,24]{2,1,0:T(2,128)(2,1)}, u32[]{:S(2)}) copy-start(bf16[1,2,24]{2,1,0:T(2,128)(2,1)} %param.9) | copy-start | bytes 292
  132.3 46.1 %copy-start.7 = (s32[1,2]{1,0:T(1,128)S(1)}, s32[1,2]{1,0:T(1,128)}, u32[]{:S(2)}) copy-start(s32[1,2]{1,0:T(1,128)} %count_ref.3) | copy-start | bytes 28
  132.3 40.3 %collective-permute-start.19 = (bf16[1024,512]{1,0:T(8,128)(2,1)}, bf16[1024,512]{1,0:T(8,128)(2,1)S(1)}, u32[]{:S(2)}, u32[]{:S(2)}) collective-permute-start(bf16[1024,512]{1,0:T(8,128)(2,1)} %get-tuple-element.50), channel_id=1, source_target_pairs={{0,1},{1,2},{2,3},{3,0},{4,5},{5,6},{6,7},{7,4},{8,9},{9,10},{10,1... | collective-permute-start | bytes 3145736 | tf_op jit(solution)/shard_map/ppermute | solution.py:583
  133.3 39.3 %collective-permute-start.20 = (bf16[1024,512]{1,0:T(8,128)(2,1)}, bf16[1024,512]{1,0:T(8,128)(2,1)}, u32[]{:S(2)}, u32[]{:S(2)}) collective-permute-start(bf16[1024,512]{1,0:T(8,128)(2,1)} %get-tuple-element.51), channel_id=1, source_target_pairs={{0,3},{1,0},{2,1},{3,2},{4,7},{5,4},{6,5},{7,6},{8,11},{9,8},{10,9... | collective-permute-start | bytes 3145736 | tf_op jit(solution)/shard_map/ppermute | solution.py:584
  168.5 1.0 copy-start
  169.5 8.8 %copy-start.1 = (bf16[48,4224]{1,0:T(8,128)(2,1)S(1)}, bf16[48,4224]{1,0:T(8,128)(2,1)}, u32[]{:S(2)}) copy-start(bf16[48,4224]{1,0:T(8,128)(2,1)} %reduce-scatter.2.cloned.1.call-done.got_ref) | copy-start | bytes 1216516
  169.7 8.6 %collective-permute-start.14 = (bf16[24,4224]{1,0:T(8,128)(2,1)S(1)}, bf16[24,4224]{1,0:T(8,128)(2,1)S(1)}, u32[]{:S(2)}, u32[]{:S(2)}) collective-permute-start(bf16[24,4224]{1,0:T(8,128)(2,1)S(1)} %partner_rows.1), channel_id=1, source_target_pairs={{0,64},{64,0},{1,65},{65,1},{2,66},{66,2},{3,67},{67,3},{4,68},{68... | collective-permute-start | bytes 608264 | tf_op jit(solution)/shard_map/ppermute | solution.py:588
  172.5 1.0 copy-start.8
  172.5 1.3 copy-start.9
  172.5 1.6 copy-start.10
Sparse Core Ops, SparseCore 0:
  34.1 47.6 all-gather.1
  97.1 71.4 reduce-scatter.1

commit v5 on v4

--- a/solution.py
+++ b/solution.py
@@ -92,7 +92,7 @@
             pltpu.VMEM((steps, t_dev, chunk), BF16),
             pltpu.SemaphoreType.DMA((2, steps)),
         ],
-        compiler_params=params(),
+        compiler_params=params(0, 58),
         name="pick_rows",
     )(lax.axis_index("k").reshape(1), lax.axis_index("dp").reshape(1), tokens, out_grad, gates, picks, counts)
 
@@ -434,7 +434,7 @@
             pltpu.SemaphoreType.DMA((4, 3)),
             pltpu.SemaphoreType.DMA((4,)),
         ],
-        compiler_params=params(),
+        compiler_params=params(0, 16),
         name="add_up",
     )(own_in, own_out, near_up, near_down, sum_up, sum_down)
 

time: 189 us -> 188 us (level)
    unnamed x34 -> x32, local copies, waits for them, and re-layouts: 5.12 us -> 4.73 us
  transfers between devices with their start and end apart: 23 -> 23, of which waited for: 14 -> 15; matrix products, arithmetic and copies ran while one was open for 0% -> 0% of each run, Pallas kernels for 16% -> 16%
where the time goes in v5:
time: 188 us; the launch traced here: 187 us
  waiting for transfers between devices  83.9 us (45%)
  Pallas kernels  55.1 us (29%)
  starting transfers between devices  29.5 us (16%)
  between operations  14.3 us (8%)
  local copies, waits for them, and re-layouts  4.73 us (3%)
    reduce_scatter x1, waiting for transfers between devices, local(): lax.psum_scatter(payload, ('zz', 'x', 'c'), scatter_dimension=0, tiled=True)  32.9 us
    ppermute x6, waiting for transfers between devices, over_z(): return lax.ppermute(v, ('k', 'zz'), [(i, i ^ flip) for i in range(4)])  28.9 us
    pallas_call x3, Pallas kernels, slice_grads(): pl.pallas_call(body, in_specs=[IN_SMEM, ANYWHERE, ANYWHERE] + [IN_VMEM] *...  19.3 us
    pallas_call x1, Pallas kernels, core_pass(): pl.pallas_call(body, in_specs=[IN_SMEM] * 5 + [ANYWHERE] * 5, out_specs=[...  15 us
    ppermute x6, starting transfers between devices, over_z(): return lax.ppermute(v, ('k', 'zz'), [(i, i ^ flip) for i in range(4)])  9.68 us
    ppermute x1, waiting for transfers between devices, local(): far_up = lax.ppermute(far_up, 'dp', UP)  8.51 us
    pallas_call x1, Pallas kernels, grad_pass(): pl.pallas_call(body, in_specs=[IN_SMEM] + [ANYWHERE] * (parts + 1), out_s...  7.08 us
    pallas_call x1, Pallas kernels, pick_rows(): pl.pallas_call(body, in_specs=[IN_SMEM, IN_SMEM, ANYWHERE, ANYWHERE, IN_V...  5.48 us
  transfers between devices with their start and end apart: 23, of which 15 were waited for; matrix products, arithmetic and copies ran while one was open for 0% of the time, Pallas kernels for 16%

profile of v5, /device:TPU:0, one launch (start us, length us, event | category | flops | bytes accessed | tf_op | source)
XLA Modules:
  0.0 187.5 jit_solution(2994176083849348477)
XLA Ops:
  7.2 0.0 all-gather.2.cloned.1.call-start
  7.2 5.5 %pick_rows.1 = (bf16[24,5120]{1,0:T(8,128)(2,1)}, bf16[24,5120]{1,0:T(8,128)(2,1)}, bf16[48,3072]{1,0:T(8,128)(2,1)}) custom-call(s32[1]{0:T(128)} %bitcast.k_ref.place_ref, s32[1]{0:T(128)} %bitcast.3.dp_ref.place_ref, bf16[512,4096]{1,0:T(8,128)(2,1)} %t_hbm.1, bf16[512,4096]{1,0:T(8,128)(2,1)} %g_hbm.1, bf16[2,24]{1,0:T(2,128)(2,1)} %bitcast.14, ...), custom_call_target="tpu_custom_call" | custom-call | tf_op jit(solution)/shard_map/pick_rows/pallas_call | solution.py:81
  12.7 2.9 %collective-permute-start.1 = (bf16[48,3072]{1,0:T(8,128)(2,1)}, bf16[48,3072]{1,0:T(8,128)(2,1)S(1)}, u32[]{:S(2)}, u32[]{:S(2)}) collective-permute-start(bf16[48,3072]{1,0:T(8,128)(2,1)} %get-tuple-element.29.refs_0_.refs_4_), channel_id=1, source_target_pairs={{0,24},{8,0},{16,8},{24,16},{1,25},{9,1},{17,9},{25,17},{2,26},{10... | collective-permute-start | bytes 884744 | tf_op jit(solution)/shard_map/ppermute | solution.py:529
  15.6 0.0 collective-permute-start
  15.6 1.9 %collective-permute-start.11 = (bf16[24,5120]{1,0:T(8,128)(2,1)}, bf16[24,5120]{1,0:T(8,128)(2,1)S(1)}, u32[]{:S(2)}, u32[]{:S(2)}) collective-permute-start(bf16[24,5120]{1,0:T(8,128)(2,1)} %get-tuple-element.35.refs_0_), channel_id=1, source_target_pairs={{0,32},{32,0},{64,96},{96,64},{1,33},{33,1},{65,97},{97,65},{2,34}... | collective-permute-start | bytes 737288 | tf_op jit(solution)/shard_map/ppermute | solution.py:24
  17.5 2.5 %collective-permute-start.13 = (bf16[24,5120]{1,0:T(8,128)(2,1)}, bf16[24,5120]{1,0:T(8,128)(2,1)S(1)}, u32[]{:S(2)}, u32[]{:S(2)}) collective-permute-start(bf16[24,5120]{1,0:T(8,128)(2,1)} %get-tuple-element.36), channel_id=1, source_target_pairs={{0,96},{32,64},{64,32},{96,0},{1,97},{33,65},{65,33},{97,1},{2,98}... | collective-permute-start | bytes 737288 | tf_op jit(solution)/shard_map/ppermute | solution.py:24
  20.1 1.1 collective-permute-start.12
  21.1 1.1 collective-permute-done.1.refs_1_.refs_2_.refs_6_
  22.2 3.3 %collective-permute-done.refs_0_.refs_1_.refs_5_ = bf16[48,3072]{1,0:T(8,128)(2,1)S(1)} collective-permute-done((bf16[48,3072]{1,0:T(8,128)(2,1)}, bf16[48,3072]{1,0:T(8,128)(2,1)S(1)}, u32[]{:S(2)}, u32[]{:S(2)}) %collective-permute-start) | collective-permute-done | bytes 294944 | tf_op jit(solution)/shard_map/ppermute | solution.py:528
  25.5 0.1 stack_rows.3
  25.7 4.6 %collective-permute-done.13.refs_3_ = bf16[24,5120]{1,0:T(8,128)(2,1)S(1)} collective-permute-done((bf16[24,5120]{1,0:T(8,128)(2,1)}, bf16[24,5120]{1,0:T(8,128)(2,1)S(1)}, u32[]{:S(2)}, u32[]{:S(2)}) %collective-permute-start.13) | collective-permute-done | bytes 245792 | tf_op jit(solution)/shard_map/ppermute | solution.py:24
  30.3 1.7 collective-permute-done.12.refs_2_
  32.0 0.9 copy-done.6
  32.9 1.1 stack_rows.5
  34.0 0.0 all-gather.2.cloned.1.call-update
  34.0 0.0 reduce-scatter.2.cloned.1.call-start
  34.1 0.5 collective-permute-start.2
  34.6 2.8 %collective-permute-start.3 = (bf16[24,3072]{1,0:T(8,128)(2,1)S(1)}, bf16[24,3072]{1,0:T(8,128)(2,1)S(1)}, u32[]{:S(2)}, u32[]{:S(2)}) collective-permute-start(bf16[24,3072]{1,0:T(8,128)(2,1)S(1)} %get-tuple-element.31.refs_5_), channel_id=1, source_target_pairs={{0,24},{8,0},{16,8},{24,16},{1,25},{9,1},{17,9},{25,17},{2,26},{10... | collective-permute-start | bytes 442376 | tf_op jit(solution)/shard_map/ppermute | solution.py:532
  37.4 3.1 %collective-permute-done.2.refs_3_ = bf16[24,3072]{1,0:T(8,128)(2,1)S(1)} collective-permute-done((bf16[24,3072]{1,0:T(8,128)(2,1)S(1)}, bf16[24,3072]{1,0:T(8,128)(2,1)S(1)}, u32[]{:S(2)}, u32[]{:S(2)}) %collective-permute-start.2) | collective-permute-done | bytes 147488 | tf_op jit(solution)/shard_map/ppermute | solution.py:531
  40.5 1.0 copy-done.3
  41.5 0.4 stack_rows.4
  41.9 0.0 copy-start.5
  41.9 2.0 %collective-permute-start.9 = (bf16[96,3072]{1,0:T(8,128)(2,1)S(1)}, bf16[96,3072]{1,0:T(8,128)(2,1)S(1)}, u32[]{:S(2)}, u32[]{:S(2)}) collective-permute-start(bf16[96,3072]{1,0:T(8,128)(2,1)S(1)} %get-tuple-element.33), channel_id=1, source_target_pairs={{0,96},{32,64},{64,32},{96,0},{1,97},{33,65},{65,33},{97,1},{2,98}... | collective-permute-start | bytes 1769480 | tf_op jit(solution)/shard_map/ppermute | solution.py:24
  43.9 0.1 collective-permute-start.7
  44.0 2.1 %collective-permute-start.5 = (bf16[96,3072]{1,0:T(8,128)(2,1)S(1)}, bf16[96,3072]{1,0:T(8,128)(2,1)S(1)}, u32[]{:S(2)}, u32[]{:S(2)}) collective-permute-start(bf16[96,3072]{1,0:T(8,128)(2,1)S(1)} %get-tuple-element.32.refs_0_), channel_id=1, source_target_pairs={{0,32},{32,0},{64,96},{96,64},{1,33},{33,1},{65,97},{97,65},{2,34}... | collective-permute-start | bytes 1769480 | tf_op jit(solution)/shard_map/ppermute | solution.py:24
  46.0 0.0 collective-permute-start.4
  46.0 22.5 %collective-permute-done.9.refs_6_ = bf16[96,3072]{1,0:T(8,128)(2,1)S(1)} collective-permute-done((bf16[96,3072]{1,0:T(8,128)(2,1)S(1)}, bf16[96,3072]{1,0:T(8,128)(2,1)S(1)}, u32[]{:S(2)}, u32[]{:S(2)}) %collective-permute-start.9) | collective-permute-done | bytes 589856 | tf_op jit(solution)/shard_map/ppermute | solution.py:24
  68.5 0.0 collective-permute-start.10
  68.6 0.5 collective-permute-start.8
  69.0 0.1 collective-permute-done.5.refs_2_
  69.2 0.2 collective-permute-start.6
  69.3 1.2 collective-permute-done.10.refs_7_
  70.5 1.3 collective-permute-done.8.refs_5_
  71.9 0.8 collective-permute-done.6.refs_3_
  72.7 7.1 %grad_pass.1 = (f32[768,512]{1,0:T(8,128)}, bf16[768,3072]{1,0:T(8,128)(2,1)}) custom-call(s32[1]{0:T(128)} %bitcast.3.dp_ref.place_ref, bf16[96,3072]{1,0:T(8,128)(2,1)} %copy-done.5, bf16[96,3072]{1,0:T(8,128)(2,1)} %copy-done.14, bf16[96,3072]{1,0:T(8,128)(2,1)} %copy-done.13, bf16[96,3072]{1,0:T(8,128)(2,1)} %collective-permute-done.6.refs_3_, ...), custom_call_target="tpu_custom_call" | custom-call | tf_op jit(solution)/shard_map/grad_pass/pallas_call | solution.py:174
  79.8 2.0 %all-gather.2.cloned.1.call-done.x_hbm = bf16[768,5120]{1,0:T(8,128)(2,1)} async-done(((bf16[96,5120]{1,0:T(8,128)(2,1)}), bf16[768,5120]{1,0:T(8,128)(2,1)}) %all-gather.2.cloned.1.call-update) | async-done | bytes 7864336 | tf_op jit(solution)/shard_map/all_gather | solution.py:534
  81.8 15.0 %core_pass.1 = (bf16[768,512]{1,0:T(8,128)(2,1)}, bf16[768,512]{1,0:T(8,128)(2,1)}, bf16[768,512]{1,0:T(8,128)(2,1)}, bf16[768,4224]{1,0:T(8,128)(2,1)}, bf16[10...) custom-call(s32[1]{0:T(128)} %bitcast.1.c_ref, s32[1]{0:T(128)} %bitcast.k_ref.place_ref, s32[1]{0:T(128)} %bitcast.2.zz_ref, ...), custom_call_target="tpu_custom_call" | custom-call | tf_op jit(solution)/shard_map/core_pass/pallas_call | solution.py:302
  96.9 0.0 reduce-scatter.2.cloned.1.call-update
  96.9 1.6 collective-permute-start.17
  98.4 1.8 collective-permute-start.18
  100.2 6.2 %slice_grads.4 = (bf16[1024,512]{1,0:T(8,128)(2,1)}, bf16[1024,512]{1,0:T(8,128)(2,1)}) custom-call(s32[1]{0:T(128)} %bitcast.3.dp_ref.place_ref, bf16[768,5120]{1,0:T(8,128)(2,1)} %all-gather.2.cloned.1.call-done.x_hbm, bf16[768,3072]{1,0:T(8,128)(2,1)} %get-tuple-element.37.dy_hbm, bf16[768,512]{1,0:T(8,128)(2,1)} %get-tuple-element.41.refs_0_, ...), custom_call_target="tpu_custom_call" | custom-call | tf_op jit(solution)/shard_map/slice_grads/pallas_call | solution.py:374
  106.4 0.3 collective-permute-start.15
  106.7 3.0 %collective-permute-start.16 = (bf16[1024,512]{1,0:T(8,128)(2,1)}, bf16[1024,512]{1,0:T(8,128)(2,1)S(1)}, u32[]{:S(2)}, u32[]{:S(2)}) collective-permute-start(bf16[1024,512]{1,0:T(8,128)(2,1)} %get-tuple-element.47), channel_id=1, source_target_pairs={{0,3},{1,0},{2,1},{3,2},{4,7},{5,4},{6,5},{7,6},{8,11},{9,8},{10,9... | collective-permute-start | bytes 3145736 | tf_op jit(solution)/shard_map/ppermute | solution.py:562
  109.7 6.2 %slice_grads.3 = (bf16[1024,512]{1,0:T(8,128)(2,1)}, bf16[1024,512]{1,0:T(8,128)(2,1)}) custom-call(s32[1]{0:T(128)} %bitcast.3.dp_ref.place_ref, bf16[768,5120]{1,0:T(8,128)(2,1)} %all-gather.2.cloned.1.call-done.x_hbm, bf16[768,3072]{1,0:T(8,128)(2,1)} %get-tuple-element.37.dy_hbm, bf16[768,512]{1,0:T(8,128)(2,1)} %get-tuple-element.41.refs_0_, ...), custom_call_target="tpu_custom_call" | custom-call | tf_op jit(solution)/shard_map/slice_grads/pallas_call | solution.py:374
  115.8 8.5 %collective-permute-done.17.refs_3_ = bf16[1024,512]{1,0:T(8,128)(2,1)S(1)} collective-permute-done((bf16[1024,512]{1,0:T(8,128)(2,1)}, bf16[1024,512]{1,0:T(8,128)(2,1)S(1)}, u32[]{:S(2)}, u32[]{:S(2)}) %collective-permute-start.17) | collective-permute-done | bytes 1048608 | tf_op jit(solution)/shard_map/ppermute | solution.py:552
  124.4 0.4 collective-permute-done.18.refs_4_
  124.8 0.6 copy-done.10
  125.3 6.9 %slice_grads.5 = (bf16[1024,512]{1,0:T(8,128)(2,1)}, bf16[1024,512]{1,0:T(8,128)(2,1)}) custom-call(s32[1]{0:T(128)} %bitcast.3.dp_ref.place_ref, bf16[768,5120]{1,0:T(8,128)(2,1)} %all-gather.2.cloned.1.call-done.x_hbm, bf16[768,3072]{1,0:T(8,128)(2,1)} %get-tuple-element.37.dy_hbm, bf16[768,512]{1,0:T(8,128)(2,1)} %get-tuple-element.41.refs_0_, ...), custom_call_target="tpu_custom_call" | custom-call | tf_op jit(solution)/shard_map/slice_grads/pallas_call | solution.py:374
  132.3 0.0 copy-start.7
  132.3 0.0 copy-start.8
  132.3 0.0 copy-start.9
  132.3 1.0 collective-permute-start.19
  133.3 2.3 %collective-permute-start.20 = (bf16[1024,512]{1,0:T(8,128)(2,1)}, bf16[1024,512]{1,0:T(8,128)(2,1)}, u32[]{:S(2)}, u32[]{:S(2)}) collective-permute-start(bf16[1024,512]{1,0:T(8,128)(2,1)} %get-tuple-element.51), channel_id=1, source_target_pairs={{0,3},{1,0},{2,1},{3,2},{4,7},{5,4},{6,5},{7,6},{8,11},{9,8},{10,9... | collective-permute-start | bytes 3145736 | tf_op jit(solution)/shard_map/ppermute | solution.py:584
  135.6 32.9 %reduce-scatter.2.cloned.1.call-done.got_ref = bf16[48,4224]{1,0:T(8,128)(2,1)} async-done(((bf16[768,4224]{1,0:T(8,128)(2,1)}), bf16[48,4224]{1,0:T(8,128)(2,1)}) %reduce-scatter.2.cloned.1.call-update) | async-done | bytes 405520 | tf_op jit(solution)/shard_map/reduce_scatter | solution.py:563
  168.5 1.0 copy-done.1
  169.5 0.2 partner_rows.1
  169.7 2.9 %collective-permute-start.14 = (bf16[24,4224]{1,0:T(8,128)(2,1)S(1)}, bf16[24,4224]{1,0:T(8,128)(2,1)S(1)}, u32[]{:S(2)}, u32[]{:S(2)}) collective-permute-start(bf16[24,4224]{1,0:T(8,128)(2,1)S(1)} %partner_rows.1), channel_id=1, source_target_pairs={{0,64},{64,0},{1,65},{65,1},{2,66},{66,2},{3,67},{67,3},{4,68},{68... | collective-permute-start | bytes 608264 | tf_op jit(solution)/shard_map/ppermute | solution.py:588
  172.6 0.0 collective-permute-done.15.refs_2_
  172.6 0.0 collective-permute-done.16.refs_3_
  172.6 0.0 collective-permute-done.19.refs_4_
  172.6 1.2 copy-done.4
  173.9 2.8 %add_up.1 = (bf16[1024,512]{1,0:T(8,128)(2,1)}, bf16[1024,512]{1,0:T(8,128)(2,1)}) custom-call(bf16[1024,512]{1,0:T(8,128)(2,1)S(1)} %copy-done, bf16[1024,512]{1,0:T(8,128)(2,1)S(1)} %copy-done.4, bf16[1024,512]{1,0:T(8,128)(2,1)S(1)} %collective-permute-done.15.refs_2_, bf16[1024,512]{1,0:T(8,128)(2,1)S(1)} %collective-permute-done.16.refs_3_, ...), custom_call_target="tpu_custom_call" | custom-call | tf_op jit(solution)/shard_map/add_up/pallas_call | solution.py:426
  176.7 0.3 collective-permute-done.14.swapped_ref
  177.0 3.6 %unpick.1 = (bf16[512,4096]{1,0:T(8,128)(2,1)}, f32[2,24]{1,0:T(2,128)}) custom-call(s32[1]{0:T(128)} %bitcast.k_ref.place_ref, bf16[48,4224]{1,0:T(8,128)(2,1)S(1)} %copy-done.2, bf16[24,4224]{1,0:T(8,128)(2,1)S(1)} %collective-permute-done.14.swapped_ref, bf16[2,24]{1,0:T(2,128)(2,1)S(1)} %bitcast.15, s32[2,24]{1,0:T(2,128)S(1)} %bitcast.13, ...), custom_call_target="tpu_custom_call" | custom-call | tf_op jit(solution)/shard_map/unpick/pallas_call | solution.py:503
  (28 shorter events, 0.1 us)
Async XLA Ops:
  7.2 74.7 %all-gather.2.cloned.1.call-start = ((), (), s32[]{:S(2)}) async-start(), calls=%async_computation.1 | async-start | bytes 8847360 | tf_op jit(solution)/shard_map/all_gather | solution.py:534
  12.7 9.5 %collective-permute-start.1 = (bf16[48,3072]{1,0:T(8,128)(2,1)}, bf16[48,3072]{1,0:T(8,128)(2,1)S(1)}, u32[]{:S(2)}, u32[]{:S(2)}) collective-permute-start(bf16[48,3072]{1,0:T(8,128)(2,1)} %get-tuple-element.29.refs_0_.refs_4_), channel_id=1, source_target_pairs={{0,24},{8,0},{16,8},{24,16},{1,25},{9,1},{17,9},{25,17},{2,26},{10... | collective-permute-start | bytes 884744 | tf_op jit(solution)/shard_map/ppermute | solution.py:529
  15.6 9.9 %collective-permute-start = (bf16[48,3072]{1,0:T(8,128)(2,1)}, bf16[48,3072]{1,0:T(8,128)(2,1)S(1)}, u32[]{:S(2)}, u32[]{:S(2)}) collective-permute-start(bf16[48,3072]{1,0:T(8,128)(2,1)} %get-tuple-element.29.refs_0_.refs_4_), channel_id=1, source_target_pairs={{0,8},{8,16},{16,24},{24,0},{1,9},{9,17},{17,25},{25,1},{2,10},{10... | collective-permute-start | bytes 884744 | tf_op jit(solution)/shard_map/ppermute | solution.py:528
  15.6 10.0 %collective-permute-start.11 = (bf16[24,5120]{1,0:T(8,128)(2,1)}, bf16[24,5120]{1,0:T(8,128)(2,1)S(1)}, u32[]{:S(2)}, u32[]{:S(2)}) collective-permute-start(bf16[24,5120]{1,0:T(8,128)(2,1)} %get-tuple-element.35.refs_0_), channel_id=1, source_target_pairs={{0,32},{32,0},{64,96},{96,64},{1,33},{33,1},{65,97},{97,65},{2,34}... | collective-permute-start | bytes 737288 | tf_op jit(solution)/shard_map/ppermute | solution.py:24
  17.5 12.8 %collective-permute-start.13 = (bf16[24,5120]{1,0:T(8,128)(2,1)}, bf16[24,5120]{1,0:T(8,128)(2,1)S(1)}, u32[]{:S(2)}, u32[]{:S(2)}) collective-permute-start(bf16[24,5120]{1,0:T(8,128)(2,1)} %get-tuple-element.36), channel_id=1, source_target_pairs={{0,96},{32,64},{64,32},{96,0},{1,97},{33,65},{65,33},{97,1},{2,98}... | collective-permute-start | bytes 737288 | tf_op jit(solution)/shard_map/ppermute | solution.py:24
  20.1 11.9 %collective-permute-start.12 = (bf16[24,5120]{1,0:T(8,128)(2,1)}, bf16[24,5120]{1,0:T(8,128)(2,1)S(1)}, u32[]{:S(2)}, u32[]{:S(2)}) collective-permute-start(bf16[24,5120]{1,0:T(8,128)(2,1)} %get-tuple-element.36), channel_id=1, source_target_pairs={{0,64},{32,96},{64,0},{96,32},{1,65},{33,97},{65,1},{97,33},{2,66}... | collective-permute-start | bytes 737288 | tf_op jit(solution)/shard_map/ppermute | solution.py:24
  32.0 0.9 copy-start.6
  34.0 134.4 %reduce-scatter.2.cloned.1.call-start = ((), (), s32[]{:S(2)}) async-start(), calls=%async_computation.2 | async-start | bytes 6893568 | tf_op jit(solution)/shard_map/reduce_scatter | solution.py:563
  34.1 6.4 %collective-permute-start.2 = (bf16[24,3072]{1,0:T(8,128)(2,1)S(1)}, bf16[24,3072]{1,0:T(8,128)(2,1)S(1)}, u32[]{:S(2)}, u32[]{:S(2)}) collective-permute-start(bf16[24,3072]{1,0:T(8,128)(2,1)S(1)} %get-tuple-element.30.refs_4_), channel_id=1, source_target_pairs={{0,8},{8,16},{16,24},{24,0},{1,9},{9,17},{17,25},{25,1},{2,10},{10... | collective-permute-start | bytes 442376 | tf_op jit(solution)/shard_map/ppermute | solution.py:531
  34.6 5.9 %collective-permute-start.3 = (bf16[24,3072]{1,0:T(8,128)(2,1)S(1)}, bf16[24,3072]{1,0:T(8,128)(2,1)S(1)}, u32[]{:S(2)}, u32[]{:S(2)}) collective-permute-start(bf16[24,3072]{1,0:T(8,128)(2,1)S(1)} %get-tuple-element.31.refs_5_), channel_id=1, source_target_pairs={{0,24},{8,0},{16,8},{24,16},{1,25},{9,1},{17,9},{25,17},{2,26},{10... | collective-permute-start | bytes 442376 | tf_op jit(solution)/shard_map/ppermute | solution.py:532
  40.5 1.0 copy-start.3
  41.9 30.9 %copy-start.5 = (bf16[96,3072]{1,0:T(8,128)(2,1)}, bf16[96,3072]{1,0:T(8,128)(2,1)S(1)}, u32[]{:S(2)}) copy-start(bf16[96,3072]{1,0:T(8,128)(2,1)S(1)} %get-tuple-element.32.refs_0_) | copy-start | bytes 1769476
  41.9 26.7 %collective-permute-start.9 = (bf16[96,3072]{1,0:T(8,128)(2,1)S(1)}, bf16[96,3072]{1,0:T(8,128)(2,1)S(1)}, u32[]{:S(2)}, u32[]{:S(2)}) collective-permute-start(bf16[96,3072]{1,0:T(8,128)(2,1)S(1)} %get-tuple-element.33), channel_id=1, source_target_pairs={{0,96},{32,64},{64,32},{96,0},{1,97},{33,65},{65,33},{97,1},{2,98}... | collective-permute-start | bytes 1769480 | tf_op jit(solution)/shard_map/ppermute | solution.py:24
  43.9 24.7 %collective-permute-start.7 = (bf16[96,3072]{1,0:T(8,128)(2,1)S(1)}, bf16[96,3072]{1,0:T(8,128)(2,1)S(1)}, u32[]{:S(2)}, u32[]{:S(2)}) collective-permute-start(bf16[96,3072]{1,0:T(8,128)(2,1)S(1)} %get-tuple-element.33), channel_id=1, source_target_pairs={{0,64},{32,96},{64,0},{96,32},{1,65},{33,97},{65,1},{97,33},{2,66}... | collective-permute-start | bytes 1769480 | tf_op jit(solution)/shard_map/ppermute | solution.py:24
  44.0 25.2 %collective-permute-start.5 = (bf16[96,3072]{1,0:T(8,128)(2,1)S(1)}, bf16[96,3072]{1,0:T(8,128)(2,1)S(1)}, u32[]{:S(2)}, u32[]{:S(2)}) collective-permute-start(bf16[96,3072]{1,0:T(8,128)(2,1)S(1)} %get-tuple-element.32.refs_0_), channel_id=1, source_target_pairs={{0,32},{32,0},{64,96},{96,64},{1,33},{33,1},{65,97},{97,65},{2,34}... | collective-permute-start | bytes 1769480 | tf_op jit(solution)/shard_map/ppermute | solution.py:24
  46.0 23.3 %collective-permute-start.4 = (bf16[96,3072]{1,0:T(8,128)(2,1)S(1)}, bf16[96,3072]{1,0:T(8,128)(2,1)S(1)}, u32[]{:S(2)}, u32[]{:S(2)}) collective-permute-start(bf16[96,3072]{1,0:T(8,128)(2,1)S(1)} %get-tuple-element.32.refs_0_), channel_id=1, source_target_pairs={{0,4},{4,0},{1,5},{5,1},{2,6},{6,2},{3,7},{7,3},{8,12},{12,8},{9,1... | collective-permute-start | bytes 1769480 | tf_op jit(solution)/shard_map/ppermute | solution.py:544
  68.5 4.2 %copy-start.11 = (bf16[96,3072]{1,0:T(8,128)(2,1)}, bf16[96,3072]{1,0:T(8,128)(2,1)S(1)}, u32[]{:S(2)}) copy-start(bf16[96,3072]{1,0:T(8,128)(2,1)S(1)} %collective-permute-done.9.refs_6_) | copy-start | bytes 1769476
  68.5 2.0 %collective-permute-start.10 = (bf16[96,3072]{1,0:T(8,128)(2,1)S(1)}, bf16[96,3072]{1,0:T(8,128)(2,1)S(1)}, u32[]{:S(2)}, u32[]{:S(2)}) collective-permute-start(bf16[96,3072]{1,0:T(8,128)(2,1)S(1)} %collective-permute-done.9.refs_6_), channel_id=1, source_target_pairs={{0,4},{4,0},{1,5},{5,1},{2,6},{6,2},{3,7},{7,3},{8,12},{12,8},{9,1... | collective-permute-start | bytes 1769480 | tf_op jit(solution)/shard_map/ppermute | solution.py:544
  68.5 4.2 %copy-start.12 = (bf16[96,3072]{1,0:T(8,128)(2,1)}, bf16[96,3072]{1,0:T(8,128)(2,1)S(1)}, u32[]{:S(2)}) copy-start(bf16[96,3072]{1,0:T(8,128)(2,1)S(1)} %collective-permute-done.7.refs_4_) | copy-start | bytes 1769476
  68.6 3.3 %collective-permute-start.8 = (bf16[96,3072]{1,0:T(8,128)(2,1)S(1)}, bf16[96,3072]{1,0:T(8,128)(2,1)}, u32[]{:S(2)}, u32[]{:S(2)}) collective-permute-start(bf16[96,3072]{1,0:T(8,128)(2,1)S(1)} %collective-permute-done.7.refs_4_), channel_id=1, source_target_pairs={{0,4},{4,0},{1,5},{5,1},{2,6},{6,2},{3,7},{7,3},{8,12},{12,8},{9,1... | collective-permute-start | bytes 1769480 | tf_op jit(solution)/shard_map/ppermute | solution.py:544
  69.2 3.6 %copy-start.13 = (bf16[96,3072]{1,0:T(8,128)(2,1)}, bf16[96,3072]{1,0:T(8,128)(2,1)S(1)}, u32[]{:S(2)}) copy-start(bf16[96,3072]{1,0:T(8,128)(2,1)S(1)} %collective-permute-done.5.refs_2_) | copy-start | bytes 1769476
  69.2 3.6 %collective-permute-start.6 = (bf16[96,3072]{1,0:T(8,128)(2,1)S(1)}, bf16[96,3072]{1,0:T(8,128)(2,1)}, u32[]{:S(2)}, u32[]{:S(2)}) collective-permute-start(bf16[96,3072]{1,0:T(8,128)(2,1)S(1)} %collective-permute-done.5.refs_2_), channel_id=1, source_target_pairs={{0,4},{4,0},{1,5},{5,1},{2,6},{6,2},{3,7},{7,3},{8,12},{12,8},{9,1... | collective-permute-start | bytes 1769480 | tf_op jit(solution)/shard_map/ppermute | solution.py:544
  69.3 3.4 %copy-start.14 = (bf16[96,3072]{1,0:T(8,128)(2,1)}, bf16[96,3072]{1,0:T(8,128)(2,1)S(1)}, u32[]{:S(2)}) copy-start(bf16[96,3072]{1,0:T(8,128)(2,1)S(1)} %collective-permute-done.4.refs_1_) | copy-start | bytes 1769476
  70.5 2.2 %copy-start.15 = (bf16[96,3072]{1,0:T(8,128)(2,1)}, bf16[96,3072]{1,0:T(8,128)(2,1)S(1)}, u32[]{:S(2)}) copy-start(bf16[96,3072]{1,0:T(8,128)(2,1)S(1)} %collective-permute-done.10.refs_7_) | copy-start | bytes 1769476
  96.9 27.5 %collective-permute-start.17 = (bf16[1024,512]{1,0:T(8,128)(2,1)}, bf16[1024,512]{1,0:T(8,128)(2,1)S(1)}, u32[]{:S(2)}, u32[]{:S(2)}) collective-permute-start(bf16[1024,512]{1,0:T(8,128)(2,1)} %get-tuple-element.48), channel_id=1, source_target_pairs={{0,1},{1,2},{2,3},{3,0},{4,5},{5,6},{6,7},{7,4},{8,9},{9,10},{10,1... | collective-permute-start | bytes 3145736 | tf_op jit(solution)/shard_map/ppermute | solution.py:552
  98.4 26.3 %collective-permute-start.18 = (bf16[1024,512]{1,0:T(8,128)(2,1)}, bf16[1024,512]{1,0:T(8,128)(2,1)}, u32[]{:S(2)}, u32[]{:S(2)}) collective-permute-start(bf16[1024,512]{1,0:T(8,128)(2,1)} %get-tuple-element.49), channel_id=1, source_target_pairs={{0,3},{1,0},{2,1},{3,2},{4,7},{5,4},{6,5},{7,6},{8,11},{9,8},{10,9... | collective-permute-start | bytes 3145736 | tf_op jit(solution)/shard_map/ppermute | solution.py:553
  106.4 66.2 %collective-permute-start.15 = (bf16[1024,512]{1,0:T(8,128)(2,1)}, bf16[1024,512]{1,0:T(8,128)(2,1)S(1)}, u32[]{:S(2)}, u32[]{:S(2)}) collective-permute-start(bf16[1024,512]{1,0:T(8,128)(2,1)} %get-tuple-element.46), channel_id=1, source_target_pairs={{0,1},{1,2},{2,3},{3,0},{4,5},{5,6},{6,7},{7,4},{8,9},{9,10},{10,1... | collective-permute-start | bytes 3145736 | tf_op jit(solution)/shard_map/ppermute | solution.py:561
  106.7 65.9 %collective-permute-start.16 = (bf16[1024,512]{1,0:T(8,128)(2,1)}, bf16[1024,512]{1,0:T(8,128)(2,1)S(1)}, u32[]{:S(2)}, u32[]{:S(2)}) collective-permute-start(bf16[1024,512]{1,0:T(8,128)(2,1)} %get-tuple-element.47), channel_id=1, source_target_pairs={{0,3},{1,0},{2,1},{3,2},{4,7},{5,4},{6,5},{7,6},{8,11},{9,8},{10,9... | collective-permute-start | bytes 3145736 | tf_op jit(solution)/shard_map/ppermute | solution.py:562
  124.4 1.0 copy-start.10
  125.3 47.3 %copy-start = (bf16[1024,512]{1,0:T(8,128)(2,1)S(1)}, bf16[1024,512]{1,0:T(8,128)(2,1)}, u32[]{:S(2)}) copy-start(bf16[1024,512]{1,0:T(8,128)(2,1)} %get-tuple-element.44.refs_5_.refs_0_) | copy-start | bytes 3145732
  132.3 44.7 %copy-start.7 = (s32[1,2,24]{2,1,0:T(2,128)S(1)}, s32[1,2,24]{2,1,0:T(2,128)}, u32[]{:S(2)}) copy-start(s32[1,2,24]{2,1,0:T(2,128)} %param.10) | copy-start | bytes 580
  132.3 44.7 %copy-start.8 = (bf16[1,2,24]{2,1,0:T(2,128)(2,1)S(1)}, bf16[1,2,24]{2,1,0:T(2,128)(2,1)}, u32[]{:S(2)}) copy-start(bf16[1,2,24]{2,1,0:T(2,128)(2,1)} %param.9) | copy-start | bytes 292
  132.3 44.7 %copy-start.9 = (s32[1,2]{1,0:T(1,128)S(1)}, s32[1,2]{1,0:T(1,128)}, u32[]{:S(2)}) copy-start(s32[1,2]{1,0:T(1,128)} %count_ref.3) | copy-start | bytes 28
  132.3 40.3 %collective-permute-start.19 = (bf16[1024,512]{1,0:T(8,128)(2,1)}, bf16[1024,512]{1,0:T(8,128)(2,1)}, u32[]{:S(2)}, u32[]{:S(2)}) collective-permute-start(bf16[1024,512]{1,0:T(8,128)(2,1)} %get-tuple-element.50), channel_id=1, source_target_pairs={{0,1},{1,2},{2,3},{3,0},{4,5},{5,6},{6,7},{7,4},{8,9},{9,10},{10,1... | collective-permute-start | bytes 3145736 | tf_op jit(solution)/shard_map/ppermute | solution.py:583
  133.3 39.3 %collective-permute-start.20 = (bf16[1024,512]{1,0:T(8,128)(2,1)}, bf16[1024,512]{1,0:T(8,128)(2,1)}, u32[]{:S(2)}, u32[]{:S(2)}) collective-permute-start(bf16[1024,512]{1,0:T(8,128)(2,1)} %get-tuple-element.51), channel_id=1, source_target_pairs={{0,3},{1,0},{2,1},{3,2},{4,7},{5,4},{6,5},{7,6},{8,11},{9,8},{10,9... | collective-permute-start | bytes 3145736 | tf_op jit(solution)/shard_map/ppermute | solution.py:584
  168.5 1.0 copy-start.1
  169.5 7.5 %copy-start.2 = (bf16[48,4224]{1,0:T(8,128)(2,1)S(1)}, bf16[48,4224]{1,0:T(8,128)(2,1)}, u32[]{:S(2)}) copy-start(bf16[48,4224]{1,0:T(8,128)(2,1)} %reduce-scatter.2.cloned.1.call-done.got_ref) | copy-start | bytes 1216516
  169.7 7.3 %collective-permute-start.14 = (bf16[24,4224]{1,0:T(8,128)(2,1)S(1)}, bf16[24,4224]{1,0:T(8,128)(2,1)S(1)}, u32[]{:S(2)}, u32[]{:S(2)}) collective-permute-start(bf16[24,4224]{1,0:T(8,128)(2,1)S(1)} %partner_rows.1), channel_id=1, source_target_pairs={{0,64},{64,0},{1,65},{65,1},{2,66},{66,2},{3,67},{67,3},{4,68},{68... | collective-permute-start | bytes 608264 | tf_op jit(solution)/shard_map/ppermute | solution.py:588
  172.6 1.2 copy-start.4
Sparse Core Ops, SparseCore 0:
  34.1 47.6 all-gather.1
  97.0 71.4 reduce-scatter.1

commit v6 on v5

--- a/solution.py
+++ b/solution.py
@@ -100,8 +100,7 @@
 def stack_rows(groups, after=()):
     flat = [block for group in groups for block in group]
     slots = 24
-    width = flat[0][0].shape[1]
-    chunk = width // 2
+    steps = 2
     n = len(flat)
 
     def body(*refs):
@@ -115,11 +114,13 @@
 
     return pl.pallas_call(
         body,
-        grid=(width // chunk,),
-        in_specs=[pl.BlockSpec((v.shape[0], chunk), lambda i: (0, i)) for v, _ in flat]
+        grid=(steps,),
+        in_specs=[pl.BlockSpec((v.shape[0], v.shape[1] // steps), lambda i: (0, i)) for v, _ in flat]
         + [ANYWHERE] * len(after),
-        out_specs=[pl.BlockSpec((slots * len(g), chunk), lambda i: (0, i)) for g in groups],
-        out_shape=[jax.ShapeDtypeStruct((slots * len(g), width), BF16) for g in groups],
+        out_specs=[
+            pl.BlockSpec((slots * len(g), g[0][0].shape[1] // steps), lambda i: (0, i)) for g in groups
+        ],
+        out_shape=[jax.ShapeDtypeStruct((slots * len(g), g[0][0].shape[1]), BF16) for g in groups],
         compiler_params=params(1, 16),
         name="stack_rows",
     )(*[v for v, _ in flat], *after)
@@ -277,6 +278,16 @@
             outs.append(pltpu.make_async_copy(value, out, out_sems.at[2 + steps + i]))
             outs[-1].start()
         pre_b[...] = pre_home[...].astype(BF16)
+        row_v[:, width:] = gate_lanes(gate_home[...]).astype(BF16)
+        for i in range(steps):
+            span = pl.ds(i * chunk, chunk)
+            row_v[:, span] = lax.dot_general(
+                pre_b[...], w1_v[span, :], (((1,), (1,)), ((), ())), preferred_element_type=F32
+            ).astype(BF16)
+            if i == steps - 1:
+                span = pl.ds(i * chunk, chunk + LANES)
+            outs.append(pltpu.make_async_copy(row_v.at[:, span], row_out.at[:, span], out_sems.at[2 + i]))
+            outs[-1].start()
         late[3].wait()
         for side, buffer, out in ((0, up_v, far_up), (1, down_v, far_down)):
             start = pl.multiple_of(((dp + 2) % 4) * chunk + side * piece, LANES)
@@ -285,16 +296,6 @@
                 far_v[:, side * piece : (side + 1) * piece], hidden_ref[...]
             ).astype(BF16)
             outs.append(pltpu.make_async_copy(buffer, out, out_sems.at[side]))
-            outs[-1].start()
-        row_v[:, width:] = gate_lanes(gate_home[...]).astype(BF16)
-        for i in range(steps):
-            span = pl.ds(i * chunk, chunk)
-            row_v[:, span] = lax.dot_general(
-                pre_b[...], w1_v[span, :], (((1,), (1,)), ((), ())), preferred_element_type=F32
-            ).astype(BF16)
-            if i == steps - 1:
-                span = pl.ds(i * chunk, chunk + LANES)
-            outs.append(pltpu.make_async_copy(row_v.at[:, span], row_out.at[:, span], out_sems.at[2 + i]))
             outs[-1].start()
         for copy in outs:
             copy.wait()
@@ -527,16 +528,18 @@
     z_blocks = [mine, over_z(mine, 1), over_z(other, 2), over_z(other, 3)]
     below = lax.ppermute(both_dy, "x", UP)
     above = lax.ppermute(both_dy, "x", DOWN)
-    pass_mine, pass_other = stack_rows([[(below, 0)], [(above, slots)]])
+    pass_mine, pass_other, near_mine, near_dy = stack_rows(
+        [[(below, 0)], [(above, slots)], [(mine, 0)], [(both_dy, 0), (both_dy, slots)]]
+    )
     far_mine = lax.ppermute(pass_mine, "x", UP)
     far_other = lax.ppermute(pass_other, "x", DOWN)
-    (z_rows,) = stack_rows([[(v, 0) for v in z_blocks]], (pass_mine, pass_other))
+    (z_rows,) = stack_rows([[(v, 0) for v in [near_mine] + z_blocks[1:]]], (pass_mine, pass_other))
     rows_x = lax.all_gather(z_rows, ("x", "c"), axis=0, tiled=True)
 
     x_mine, x_other = stack_rows(
         [
-            [(both_dy, 0), (below, 0), (above, 0), (far_mine, 0)],
-            [(both_dy, slots), (below, slots), (above, slots), (far_other, 0)],
+            [(near_dy, 0), (below, 0), (above, 0), (far_mine, 0)],
+            [(near_dy, slots), (below, slots), (above, slots), (far_other, 0)],
         ]
     )
     pieces = []

time: 188 us -> 187 us (level)
    ppermute x6, waiting for transfers between devices: 28.9 us -> 26.8 us  [over_z(): return lax.ppermute(v, ('k', 'zz'), [(i, i ^ flip) for i in range(4)])]
    unnamed x32 -> x30, local copies, waits for them, and re-layouts: 4.73 us -> 4.72 us
where the time goes in v6:
time: 187 us; the launch traced here: 186 us
  waiting for transfers between devices  83 us (44%)
  Pallas kernels  55 us (29%)
  starting transfers between devices  29.3 us (16%)
  between operations  14.3 us (8%)
  local copies, waits for them, and re-layouts  4.72 us (3%)
    reduce_scatter x1, waiting for transfers between devices, local(): lax.psum_scatter(payload, ('zz', 'x', 'c'), scatter_dimension=0, tiled=True)  32.9 us
    ppermute x6, waiting for transfers between devices, over_z(): return lax.ppermute(v, ('k', 'zz'), [(i, i ^ flip) for i in range(4)])  26.8 us
    pallas_call x3, Pallas kernels, slice_grads(): pl.pallas_call(body, in_specs=[IN_SMEM, ANYWHERE, ANYWHERE] + [IN_VMEM] *...  19.3 us
    pallas_call x1, Pallas kernels, core_pass(): pl.pallas_call(body, in_specs=[IN_SMEM] * 5 + [ANYWHERE] * 5, out_specs=[...  14.8 us
    ppermute x6, starting transfers between devices, over_z(): return lax.ppermute(v, ('k', 'zz'), [(i, i ^ flip) for i in range(4)])  9.68 us
    ppermute x1, waiting for transfers between devices, local(): far_up = lax.ppermute(far_up, 'dp', UP)  8.49 us
    pallas_call x1, Pallas kernels, grad_pass(): pl.pallas_call(body, in_specs=[IN_SMEM] + [ANYWHERE] * (parts + 1), out_s...  7.08 us
    pallas_call x1, Pallas kernels, pick_rows(): pl.pallas_call(body, in_specs=[IN_SMEM, IN_SMEM, ANYWHERE, ANYWHERE, IN_V...  5.48 us
  transfers between devices with their start and end apart: 23, of which 15 were waited for; matrix products, arithmetic and copies ran while one was open for 0% of the time, Pallas kernels for 16%

profile of v6, /device:TPU:0, one launch (start us, length us, event | category | flops | bytes accessed | tf_op | source)
XLA Modules:
  0.0 186.3 jit_solution(1948244406412720032)
XLA Ops:
  7.2 0.0 all-gather.2.cloned.1.call-start
  7.2 5.5 %pick_rows.1 = (bf16[24,5120]{1,0:T(8,128)(2,1)}, bf16[24,5120]{1,0:T(8,128)(2,1)}, bf16[48,3072]{1,0:T(8,128)(2,1)}) custom-call(s32[1]{0:T(128)} %bitcast.k_ref.place_ref, s32[1]{0:T(128)} %bitcast.3.dp_ref.place_ref, bf16[512,4096]{1,0:T(8,128)(2,1)} %t_hbm.1, bf16[512,4096]{1,0:T(8,128)(2,1)} %g_hbm.1, bf16[2,24]{1,0:T(2,128)(2,1)} %bitcast.14, ...), custom_call_target="tpu_custom_call" | custom-call | tf_op jit(solution)/shard_map/pick_rows/pallas_call | solution.py:81
  12.7 2.9 %collective-permute-start.1 = (bf16[48,3072]{1,0:T(8,128)(2,1)}, bf16[48,3072]{1,0:T(8,128)(2,1)S(1)}, u32[]{:S(2)}, u32[]{:S(2)}) collective-permute-start(bf16[48,3072]{1,0:T(8,128)(2,1)} %get-tuple-element.31.refs_3_.refs_4_), channel_id=1, source_target_pairs={{0,24},{8,0},{16,8},{24,16},{1,25},{9,1},{17,9},{25,17},{2,26},{10... | collective-permute-start | bytes 884744 | tf_op jit(solution)/shard_map/ppermute | solution.py:530
  15.6 0.0 collective-permute-start
  15.6 1.9 %collective-permute-start.11 = (bf16[24,5120]{1,0:T(8,128)(2,1)}, bf16[24,5120]{1,0:T(8,128)(2,1)S(1)}, u32[]{:S(2)}, u32[]{:S(2)}) collective-permute-start(bf16[24,5120]{1,0:T(8,128)(2,1)} %get-tuple-element.32.refs_2_), channel_id=1, source_target_pairs={{0,32},{32,0},{64,96},{96,64},{1,33},{33,1},{65,97},{97,65},{2,34}... | collective-permute-start | bytes 737288 | tf_op jit(solution)/shard_map/ppermute | solution.py:24
  17.5 2.5 %collective-permute-start.13 = (bf16[24,5120]{1,0:T(8,128)(2,1)}, bf16[24,5120]{1,0:T(8,128)(2,1)S(1)}, u32[]{:S(2)}, u32[]{:S(2)}) collective-permute-start(bf16[24,5120]{1,0:T(8,128)(2,1)} %get-tuple-element.40), channel_id=1, source_target_pairs={{0,96},{32,64},{64,32},{96,0},{1,97},{33,65},{65,33},{97,1},{2,98}... | collective-permute-start | bytes 737288 | tf_op jit(solution)/shard_map/ppermute | solution.py:24
  20.1 1.1 collective-permute-start.12
  21.1 1.1 collective-permute-done.1.refs_1_.refs_2_.refs_6_
  22.2 3.3 %collective-permute-done.refs_0_.refs_1_.refs_5_ = bf16[48,3072]{1,0:T(8,128)(2,1)S(1)} collective-permute-done((bf16[48,3072]{1,0:T(8,128)(2,1)}, bf16[48,3072]{1,0:T(8,128)(2,1)S(1)}, u32[]{:S(2)}, u32[]{:S(2)}) %collective-permute-start) | collective-permute-done | bytes 294944 | tf_op jit(solution)/shard_map/ppermute | solution.py:529
  25.5 1.0 copy-done.3
  26.5 0.9 copy-done.6
  27.4 0.3 stack_rows.3
  27.7 0.0 collective-permute-done.11.refs_1_
  27.7 2.6 %collective-permute-done.13.refs_3_ = bf16[24,5120]{1,0:T(8,128)(2,1)S(1)} collective-permute-done((bf16[24,5120]{1,0:T(8,128)(2,1)}, bf16[24,5120]{1,0:T(8,128)(2,1)S(1)}, u32[]{:S(2)}, u32[]{:S(2)}) %collective-permute-start.13) | collective-permute-done | bytes 245792 | tf_op jit(solution)/shard_map/ppermute | solution.py:24
  30.3 1.7 collective-permute-done.12.refs_2_
  32.0 1.1 stack_rows.5
  33.1 0.0 all-gather.2.cloned.1.call-update
  33.1 0.0 reduce-scatter.2.cloned.1.call-start
  33.1 0.5 collective-permute-start.2
  33.7 2.8 %collective-permute-start.3 = (bf16[24,3072]{1,0:T(8,128)(2,1)S(1)}, bf16[24,3072]{1,0:T(8,128)(2,1)S(1)}, u32[]{:S(2)}, u32[]{:S(2)}) collective-permute-start(bf16[24,3072]{1,0:T(8,128)(2,1)S(1)} %get-tuple-element.35.refs_5_), channel_id=1, source_target_pairs={{0,24},{8,0},{16,8},{24,16},{1,25},{9,1},{17,9},{25,17},{2,26},{10... | collective-permute-start | bytes 442376 | tf_op jit(solution)/shard_map/ppermute | solution.py:535
  36.4 3.1 %collective-permute-done.2.refs_3_ = bf16[24,3072]{1,0:T(8,128)(2,1)S(1)} collective-permute-done((bf16[24,3072]{1,0:T(8,128)(2,1)S(1)}, bf16[24,3072]{1,0:T(8,128)(2,1)S(1)}, u32[]{:S(2)}, u32[]{:S(2)}) %collective-permute-start.2) | collective-permute-done | bytes 147488 | tf_op jit(solution)/shard_map/ppermute | solution.py:534
  39.6 0.0 collective-permute-done.3.refs_7_
  39.6 0.4 stack_rows.4
  40.0 0.0 copy-start.5
  40.0 2.0 %collective-permute-start.9 = (bf16[96,3072]{1,0:T(8,128)(2,1)S(1)}, bf16[96,3072]{1,0:T(8,128)(2,1)S(1)}, u32[]{:S(2)}, u32[]{:S(2)}) collective-permute-start(bf16[96,3072]{1,0:T(8,128)(2,1)S(1)} %get-tuple-element.37), channel_id=1, source_target_pairs={{0,96},{32,64},{64,32},{96,0},{1,97},{33,65},{65,33},{97,1},{2,98}... | collective-permute-start | bytes 1769480 | tf_op jit(solution)/shard_map/ppermute | solution.py:24
  41.9 0.1 collective-permute-start.7
  42.1 2.1 %collective-permute-start.5 = (bf16[96,3072]{1,0:T(8,128)(2,1)S(1)}, bf16[96,3072]{1,0:T(8,128)(2,1)S(1)}, u32[]{:S(2)}, u32[]{:S(2)}) collective-permute-start(bf16[96,3072]{1,0:T(8,128)(2,1)S(1)} %get-tuple-element.36.refs_0_), channel_id=1, source_target_pairs={{0,32},{32,0},{64,96},{96,64},{1,33},{33,1},{65,97},{97,65},{2,34}... | collective-permute-start | bytes 1769480 | tf_op jit(solution)/shard_map/ppermute | solution.py:24
  44.1 0.0 collective-permute-start.4
  44.1 22.5 %collective-permute-done.9.refs_6_ = bf16[96,3072]{1,0:T(8,128)(2,1)S(1)} collective-permute-done((bf16[96,3072]{1,0:T(8,128)(2,1)S(1)}, bf16[96,3072]{1,0:T(8,128)(2,1)S(1)}, u32[]{:S(2)}, u32[]{:S(2)}) %collective-permute-start.9) | collective-permute-done | bytes 589856 | tf_op jit(solution)/shard_map/ppermute | solution.py:24
  66.6 0.0 collective-permute-start.10
  66.6 0.5 collective-permute-start.8
  67.1 0.1 collective-permute-done.5.refs_2_
  67.2 0.2 collective-permute-start.6
  67.4 1.3 collective-permute-done.10.refs_7_
  68.8 0.8 collective-permute-done.8.refs_5_
  69.6 1.2 collective-permute-done.6.refs_3_
  70.8 7.1 %grad_pass.1 = (f32[768,512]{1,0:T(8,128)}, bf16[768,3072]{1,0:T(8,128)(2,1)}) custom-call(s32[1]{0:T(128)} %bitcast.3.dp_ref.place_ref, bf16[96,3072]{1,0:T(8,128)(2,1)} %copy-done.5, bf16[96,3072]{1,0:T(8,128)(2,1)} %copy-done.14, bf16[96,3072]{1,0:T(8,128)(2,1)} %copy-done.13, bf16[96,3072]{1,0:T(8,128)(2,1)} %collective-permute-done.6.refs_3_, ...), custom_call_target="tpu_custom_call" | custom-call | tf_op jit(solution)/shard_map/grad_pass/pallas_call | solution.py:175
  77.9 3.0 %all-gather.2.cloned.1.call-done.x_hbm = bf16[768,5120]{1,0:T(8,128)(2,1)} async-done(((bf16[96,5120]{1,0:T(8,128)(2,1)}), bf16[768,5120]{1,0:T(8,128)(2,1)}) %all-gather.2.cloned.1.call-update) | async-done | bytes 7864336 | tf_op jit(solution)/shard_map/all_gather | solution.py:537
  80.9 14.8 %core_pass.1 = (bf16[768,512]{1,0:T(8,128)(2,1)}, bf16[768,512]{1,0:T(8,128)(2,1)}, bf16[768,512]{1,0:T(8,128)(2,1)}, bf16[768,4224]{1,0:T(8,128)(2,1)}, bf16[10...) custom-call(s32[1]{0:T(128)} %bitcast.1.c_ref, s32[1]{0:T(128)} %bitcast.k_ref.place_ref, s32[1]{0:T(128)} %bitcast.2.zz_ref, ...), custom_call_target="tpu_custom_call" | custom-call | tf_op jit(solution)/shard_map/core_pass/pallas_call | solution.py:303
  95.7 0.0 reduce-scatter.2.cloned.1.call-update
  95.7 1.6 collective-permute-start.17
  97.3 1.8 collective-permute-start.18
  99.0 6.2 %slice_grads.4 = (bf16[1024,512]{1,0:T(8,128)(2,1)}, bf16[1024,512]{1,0:T(8,128)(2,1)}) custom-call(s32[1]{0:T(128)} %bitcast.3.dp_ref.place_ref, bf16[768,5120]{1,0:T(8,128)(2,1)} %all-gather.2.cloned.1.call-done.x_hbm, bf16[768,3072]{1,0:T(8,128)(2,1)} %get-tuple-element.41.dy_hbm, bf16[768,512]{1,0:T(8,128)(2,1)} %get-tuple-element.45.refs_0_, ...), custom_call_target="tpu_custom_call" | custom-call | tf_op jit(solution)/shard_map/slice_grads/pallas_call | solution.py:375
  105.2 0.3 collective-permute-start.15
  105.5 3.0 %collective-permute-start.16 = (bf16[1024,512]{1,0:T(8,128)(2,1)}, bf16[1024,512]{1,0:T(8,128)(2,1)S(1)}, u32[]{:S(2)}, u32[]{:S(2)}) collective-permute-start(bf16[1024,512]{1,0:T(8,128)(2,1)} %get-tuple-element.51), channel_id=1, source_target_pairs={{0,3},{1,0},{2,1},{3,2},{4,7},{5,4},{6,5},{7,6},{8,11},{9,8},{10,9... | collective-permute-start | bytes 3145736 | tf_op jit(solution)/shard_map/ppermute | solution.py:565
  108.5 6.2 %slice_grads.3 = (bf16[1024,512]{1,0:T(8,128)(2,1)}, bf16[1024,512]{1,0:T(8,128)(2,1)}) custom-call(s32[1]{0:T(128)} %bitcast.3.dp_ref.place_ref, bf16[768,5120]{1,0:T(8,128)(2,1)} %all-gather.2.cloned.1.call-done.x_hbm, bf16[768,3072]{1,0:T(8,128)(2,1)} %get-tuple-element.41.dy_hbm, bf16[768,512]{1,0:T(8,128)(2,1)} %get-tuple-element.45.refs_0_, ...), custom_call_target="tpu_custom_call" | custom-call | tf_op jit(solution)/shard_map/slice_grads/pallas_call | solution.py:375
  114.7 8.5 %collective-permute-done.17.refs_3_ = bf16[1024,512]{1,0:T(8,128)(2,1)S(1)} collective-permute-done((bf16[1024,512]{1,0:T(8,128)(2,1)}, bf16[1024,512]{1,0:T(8,128)(2,1)S(1)}, u32[]{:S(2)}, u32[]{:S(2)}) %collective-permute-start.17) | collective-permute-done | bytes 1048608 | tf_op jit(solution)/shard_map/ppermute | solution.py:555
  123.2 0.4 collective-permute-done.18.refs_4_
  123.6 0.6 copy-done.10
  124.2 6.9 %slice_grads.5 = (bf16[1024,512]{1,0:T(8,128)(2,1)}, bf16[1024,512]{1,0:T(8,128)(2,1)}) custom-call(s32[1]{0:T(128)} %bitcast.3.dp_ref.place_ref, bf16[768,5120]{1,0:T(8,128)(2,1)} %all-gather.2.cloned.1.call-done.x_hbm, bf16[768,3072]{1,0:T(8,128)(2,1)} %get-tuple-element.41.dy_hbm, bf16[768,512]{1,0:T(8,128)(2,1)} %get-tuple-element.45.refs_0_, ...), custom_call_target="tpu_custom_call" | custom-call | tf_op jit(solution)/shard_map/slice_grads/pallas_call | solution.py:375
  131.1 0.0 copy-start.7
  131.1 0.0 copy-start.8
  131.1 0.0 copy-start.9
  131.2 1.0 collective-permute-start.19
  132.1 2.3 %collective-permute-start.20 = (bf16[1024,512]{1,0:T(8,128)(2,1)}, bf16[1024,512]{1,0:T(8,128)(2,1)}, u32[]{:S(2)}, u32[]{:S(2)}) collective-permute-start(bf16[1024,512]{1,0:T(8,128)(2,1)} %get-tuple-element.55), channel_id=1, source_target_pairs={{0,3},{1,0},{2,1},{3,2},{4,7},{5,4},{6,5},{7,6},{8,11},{9,8},{10,9... | collective-permute-start | bytes 3145736 | tf_op jit(solution)/shard_map/ppermute | solution.py:587
  134.5 32.9 %reduce-scatter.2.cloned.1.call-done.got_ref = bf16[48,4224]{1,0:T(8,128)(2,1)} async-done(((bf16[768,4224]{1,0:T(8,128)(2,1)}), bf16[48,4224]{1,0:T(8,128)(2,1)}) %reduce-scatter.2.cloned.1.call-update) | async-done | bytes 405520 | tf_op jit(solution)/shard_map/reduce_scatter | solution.py:566
  167.3 1.0 copy-done.1
  168.3 0.2 partner_rows.1
  168.5 2.8 %collective-permute-start.14 = (bf16[24,4224]{1,0:T(8,128)(2,1)S(1)}, bf16[24,4224]{1,0:T(8,128)(2,1)S(1)}, u32[]{:S(2)}, u32[]{:S(2)}) collective-permute-start(bf16[24,4224]{1,0:T(8,128)(2,1)S(1)} %partner_rows.1), channel_id=1, source_target_pairs={{0,64},{64,0},{1,65},{65,1},{2,66},{66,2},{3,67},{67,3},{4,68},{68... | collective-permute-start | bytes 608264 | tf_op jit(solution)/shard_map/ppermute | solution.py:591
  171.3 0.0 collective-permute-done.15.refs_2_
  171.3 1.2 copy-done.4
  172.5 2.8 %add_up.1 = (bf16[1024,512]{1,0:T(8,128)(2,1)}, bf16[1024,512]{1,0:T(8,128)(2,1)}) custom-call(bf16[1024,512]{1,0:T(8,128)(2,1)S(1)} %copy-done, bf16[1024,512]{1,0:T(8,128)(2,1)S(1)} %copy-done.4, bf16[1024,512]{1,0:T(8,128)(2,1)S(1)} %collective-permute-done.15.refs_2_, bf16[1024,512]{1,0:T(8,128)(2,1)S(1)} %collective-permute-done.16.refs_3_, ...), custom_call_target="tpu_custom_call" | custom-call | tf_op jit(solution)/shard_map/add_up/pallas_call | solution.py:427
  175.4 0.5 collective-permute-done.14.swapped_ref
  175.9 3.6 %unpick.1 = (bf16[512,4096]{1,0:T(8,128)(2,1)}, f32[2,24]{1,0:T(2,128)}) custom-call(s32[1]{0:T(128)} %bitcast.k_ref.place_ref, bf16[48,4224]{1,0:T(8,128)(2,1)S(1)} %copy-done.2, bf16[24,4224]{1,0:T(8,128)(2,1)S(1)} %collective-permute-done.14.swapped_ref, bf16[2,24]{1,0:T(2,128)(2,1)S(1)} %bitcast.15, s32[2,24]{1,0:T(2,128)S(1)} %bitcast.13, ...), custom_call_target="tpu_custom_call" | custom-call | tf_op jit(solution)/shard_map/unpick/pallas_call | solution.py:504
  (26 shorter events, 0.1 us)
Async XLA Ops:
  7.2 73.7 %all-gather.2.cloned.1.call-start = ((), (), s32[]{:S(2)}) async-start(), calls=%async_computation.1 | async-start | bytes 8847360 | tf_op jit(solution)/shard_map/all_gather | solution.py:537
  12.7 9.5 %collective-permute-start.1 = (bf16[48,3072]{1,0:T(8,128)(2,1)}, bf16[48,3072]{1,0:T(8,128)(2,1)S(1)}, u32[]{:S(2)}, u32[]{:S(2)}) collective-permute-start(bf16[48,3072]{1,0:T(8,128)(2,1)} %get-tuple-element.31.refs_3_.refs_4_), channel_id=1, source_target_pairs={{0,24},{8,0},{16,8},{24,16},{1,25},{9,1},{17,9},{25,17},{2,26},{10... | collective-permute-start | bytes 884744 | tf_op jit(solution)/shard_map/ppermute | solution.py:530
  15.6 9.9 %collective-permute-start = (bf16[48,3072]{1,0:T(8,128)(2,1)}, bf16[48,3072]{1,0:T(8,128)(2,1)S(1)}, u32[]{:S(2)}, u32[]{:S(2)}) collective-permute-start(bf16[48,3072]{1,0:T(8,128)(2,1)} %get-tuple-element.31.refs_3_.refs_4_), channel_id=1, source_target_pairs={{0,8},{8,16},{16,24},{24,0},{1,9},{9,17},{17,25},{25,1},{2,10},{10... | collective-permute-start | bytes 884744 | tf_op jit(solution)/shard_map/ppermute | solution.py:529
  15.6 12.1 %collective-permute-start.11 = (bf16[24,5120]{1,0:T(8,128)(2,1)}, bf16[24,5120]{1,0:T(8,128)(2,1)S(1)}, u32[]{:S(2)}, u32[]{:S(2)}) collective-permute-start(bf16[24,5120]{1,0:T(8,128)(2,1)} %get-tuple-element.32.refs_2_), channel_id=1, source_target_pairs={{0,32},{32,0},{64,96},{96,64},{1,33},{33,1},{65,97},{97,65},{2,34}... | collective-permute-start | bytes 737288 | tf_op jit(solution)/shard_map/ppermute | solution.py:24
  17.5 12.8 %collective-permute-start.13 = (bf16[24,5120]{1,0:T(8,128)(2,1)}, bf16[24,5120]{1,0:T(8,128)(2,1)S(1)}, u32[]{:S(2)}, u32[]{:S(2)}) collective-permute-start(bf16[24,5120]{1,0:T(8,128)(2,1)} %get-tuple-element.40), channel_id=1, source_target_pairs={{0,96},{32,64},{64,32},{96,0},{1,97},{33,65},{65,33},{97,1},{2,98}... | collective-permute-start | bytes 737288 | tf_op jit(solution)/shard_map/ppermute | solution.py:24
  20.1 11.9 %collective-permute-start.12 = (bf16[24,5120]{1,0:T(8,128)(2,1)}, bf16[24,5120]{1,0:T(8,128)(2,1)S(1)}, u32[]{:S(2)}, u32[]{:S(2)}) collective-permute-start(bf16[24,5120]{1,0:T(8,128)(2,1)} %get-tuple-element.40), channel_id=1, source_target_pairs={{0,64},{32,96},{64,0},{96,32},{1,65},{33,97},{65,1},{97,33},{2,66}... | collective-permute-start | bytes 737288 | tf_op jit(solution)/shard_map/ppermute | solution.py:24
  25.5 1.0 copy-start.3
  26.5 0.9 copy-start.6
  33.1 134.3 %reduce-scatter.2.cloned.1.call-start = ((), (), s32[]{:S(2)}) async-start(), calls=%async_computation.2 | async-start | bytes 6893568 | tf_op jit(solution)/shard_map/reduce_scatter | solution.py:566
  33.1 6.4 %collective-permute-start.2 = (bf16[24,3072]{1,0:T(8,128)(2,1)S(1)}, bf16[24,3072]{1,0:T(8,128)(2,1)S(1)}, u32[]{:S(2)}, u32[]{:S(2)}) collective-permute-start(bf16[24,3072]{1,0:T(8,128)(2,1)S(1)} %get-tuple-element.34.refs_4_), channel_id=1, source_target_pairs={{0,8},{8,16},{16,24},{24,0},{1,9},{9,17},{17,25},{25,1},{2,10},{10... | collective-permute-start | bytes 442376 | tf_op jit(solution)/shard_map/ppermute | solution.py:534
  33.7 5.9 %collective-permute-start.3 = (bf16[24,3072]{1,0:T(8,128)(2,1)S(1)}, bf16[24,3072]{1,0:T(8,128)(2,1)S(1)}, u32[]{:S(2)}, u32[]{:S(2)}) collective-permute-start(bf16[24,3072]{1,0:T(8,128)(2,1)S(1)} %get-tuple-element.35.refs_5_), channel_id=1, source_target_pairs={{0,24},{8,0},{16,8},{24,16},{1,25},{9,1},{17,9},{25,17},{2,26},{10... | collective-permute-start | bytes 442376 | tf_op jit(solution)/shard_map/ppermute | solution.py:535
  40.0 30.9 %copy-start.5 = (bf16[96,3072]{1,0:T(8,128)(2,1)}, bf16[96,3072]{1,0:T(8,128)(2,1)S(1)}, u32[]{:S(2)}) copy-start(bf16[96,3072]{1,0:T(8,128)(2,1)S(1)} %get-tuple-element.36.refs_0_) | copy-start | bytes 1769476
  40.0 26.7 %collective-permute-start.9 = (bf16[96,3072]{1,0:T(8,128)(2,1)S(1)}, bf16[96,3072]{1,0:T(8,128)(2,1)S(1)}, u32[]{:S(2)}, u32[]{:S(2)}) collective-permute-start(bf16[96,3072]{1,0:T(8,128)(2,1)S(1)} %get-tuple-element.37), channel_id=1, source_target_pairs={{0,96},{32,64},{64,32},{96,0},{1,97},{33,65},{65,33},{97,1},{2,98}... | collective-permute-start | bytes 1769480 | tf_op jit(solution)/shard_map/ppermute | solution.py:24
  41.9 24.7 %collective-permute-start.7 = (bf16[96,3072]{1,0:T(8,128)(2,1)S(1)}, bf16[96,3072]{1,0:T(8,128)(2,1)S(1)}, u32[]{:S(2)}, u32[]{:S(2)}) collective-permute-start(bf16[96,3072]{1,0:T(8,128)(2,1)S(1)} %get-tuple-element.37), channel_id=1, source_target_pairs={{0,64},{32,96},{64,0},{96,32},{1,65},{33,97},{65,1},{97,33},{2,66}... | collective-permute-start | bytes 1769480 | tf_op jit(solution)/shard_map/ppermute | solution.py:24
  42.1 25.2 %collective-permute-start.5 = (bf16[96,3072]{1,0:T(8,128)(2,1)S(1)}, bf16[96,3072]{1,0:T(8,128)(2,1)S(1)}, u32[]{:S(2)}, u32[]{:S(2)}) collective-permute-start(bf16[96,3072]{1,0:T(8,128)(2,1)S(1)} %get-tuple-element.36.refs_0_), channel_id=1, source_target_pairs={{0,32},{32,0},{64,96},{96,64},{1,33},{33,1},{65,97},{97,65},{2,34}... | collective-permute-start | bytes 1769480 | tf_op jit(solution)/shard_map/ppermute | solution.py:24
  44.1 23.3 %collective-permute-start.4 = (bf16[96,3072]{1,0:T(8,128)(2,1)S(1)}, bf16[96,3072]{1,0:T(8,128)(2,1)S(1)}, u32[]{:S(2)}, u32[]{:S(2)}) collective-permute-start(bf16[96,3072]{1,0:T(8,128)(2,1)S(1)} %get-tuple-element.36.refs_0_), channel_id=1, source_target_pairs={{0,4},{4,0},{1,5},{5,1},{2,6},{6,2},{3,7},{7,3},{8,12},{12,8},{9,1... | collective-permute-start | bytes 1769480 | tf_op jit(solution)/shard_map/ppermute | solution.py:547
  66.6 4.2 %copy-start.11 = (bf16[96,3072]{1,0:T(8,128)(2,1)}, bf16[96,3072]{1,0:T(8,128)(2,1)S(1)}, u32[]{:S(2)}) copy-start(bf16[96,3072]{1,0:T(8,128)(2,1)S(1)} %collective-permute-done.9.refs_6_) | copy-start | bytes 1769476
  66.6 2.1 %collective-permute-start.10 = (bf16[96,3072]{1,0:T(8,128)(2,1)S(1)}, bf16[96,3072]{1,0:T(8,128)(2,1)}, u32[]{:S(2)}, u32[]{:S(2)}) collective-permute-start(bf16[96,3072]{1,0:T(8,128)(2,1)S(1)} %collective-permute-done.9.refs_6_), channel_id=1, source_target_pairs={{0,4},{4,0},{1,5},{5,1},{2,6},{6,2},{3,7},{7,3},{8,12},{12,8},{9,1... | collective-permute-start | bytes 1769480 | tf_op jit(solution)/shard_map/ppermute | solution.py:547
  66.6 4.2 %copy-start.12 = (bf16[96,3072]{1,0:T(8,128)(2,1)}, bf16[96,3072]{1,0:T(8,128)(2,1)S(1)}, u32[]{:S(2)}) copy-start(bf16[96,3072]{1,0:T(8,128)(2,1)S(1)} %collective-permute-done.7.refs_4_) | copy-start | bytes 1769476
  66.6 3.0 %collective-permute-start.8 = (bf16[96,3072]{1,0:T(8,128)(2,1)S(1)}, bf16[96,3072]{1,0:T(8,128)(2,1)}, u32[]{:S(2)}, u32[]{:S(2)}) collective-permute-start(bf16[96,3072]{1,0:T(8,128)(2,1)S(1)} %collective-permute-done.7.refs_4_), channel_id=1, source_target_pairs={{0,4},{4,0},{1,5},{5,1},{2,6},{6,2},{3,7},{7,3},{8,12},{12,8},{9,1... | collective-permute-start | bytes 1769480 | tf_op jit(solution)/shard_map/ppermute | solution.py:547
  67.2 3.6 %copy-start.13 = (bf16[96,3072]{1,0:T(8,128)(2,1)}, bf16[96,3072]{1,0:T(8,128)(2,1)S(1)}, u32[]{:S(2)}) copy-start(bf16[96,3072]{1,0:T(8,128)(2,1)S(1)} %collective-permute-done.5.refs_2_) | copy-start | bytes 1769476
  67.2 3.6 %collective-permute-start.6 = (bf16[96,3072]{1,0:T(8,128)(2,1)S(1)}, bf16[96,3072]{1,0:T(8,128)(2,1)}, u32[]{:S(2)}, u32[]{:S(2)}) collective-permute-start(bf16[96,3072]{1,0:T(8,128)(2,1)S(1)} %collective-permute-done.5.refs_2_), channel_id=1, source_target_pairs={{0,4},{4,0},{1,5},{5,1},{2,6},{6,2},{3,7},{7,3},{8,12},{12,8},{9,1... | collective-permute-start | bytes 1769480 | tf_op jit(solution)/shard_map/ppermute | solution.py:547
  67.4 3.4 %copy-start.14 = (bf16[96,3072]{1,0:T(8,128)(2,1)}, bf16[96,3072]{1,0:T(8,128)(2,1)S(1)}, u32[]{:S(2)}) copy-start(bf16[96,3072]{1,0:T(8,128)(2,1)S(1)} %collective-permute-done.4.refs_1_) | copy-start | bytes 1769476
  95.7 27.5 %collective-permute-start.17 = (bf16[1024,512]{1,0:T(8,128)(2,1)}, bf16[1024,512]{1,0:T(8,128)(2,1)S(1)}, u32[]{:S(2)}, u32[]{:S(2)}) collective-permute-start(bf16[1024,512]{1,0:T(8,128)(2,1)} %get-tuple-element.52), channel_id=1, source_target_pairs={{0,1},{1,2},{2,3},{3,0},{4,5},{5,6},{6,7},{7,4},{8,9},{9,10},{10,1... | collective-permute-start | bytes 3145736 | tf_op jit(solution)/shard_map/ppermute | solution.py:555
  97.3 26.3 %collective-permute-start.18 = (bf16[1024,512]{1,0:T(8,128)(2,1)}, bf16[1024,512]{1,0:T(8,128)(2,1)}, u32[]{:S(2)}, u32[]{:S(2)}) collective-permute-start(bf16[1024,512]{1,0:T(8,128)(2,1)} %get-tuple-element.53), channel_id=1, source_target_pairs={{0,3},{1,0},{2,1},{3,2},{4,7},{5,4},{6,5},{7,6},{8,11},{9,8},{10,9... | collective-permute-start | bytes 3145736 | tf_op jit(solution)/shard_map/ppermute | solution.py:556
  105.2 66.1 %collective-permute-start.15 = (bf16[1024,512]{1,0:T(8,128)(2,1)}, bf16[1024,512]{1,0:T(8,128)(2,1)S(1)}, u32[]{:S(2)}, u32[]{:S(2)}) collective-permute-start(bf16[1024,512]{1,0:T(8,128)(2,1)} %get-tuple-element.50), channel_id=1, source_target_pairs={{0,1},{1,2},{2,3},{3,0},{4,5},{5,6},{6,7},{7,4},{8,9},{9,10},{10,1... | collective-permute-start | bytes 3145736 | tf_op jit(solution)/shard_map/ppermute | solution.py:564
  105.5 65.7 %collective-permute-start.16 = (bf16[1024,512]{1,0:T(8,128)(2,1)}, bf16[1024,512]{1,0:T(8,128)(2,1)S(1)}, u32[]{:S(2)}, u32[]{:S(2)}) collective-permute-start(bf16[1024,512]{1,0:T(8,128)(2,1)} %get-tuple-element.51), channel_id=1, source_target_pairs={{0,3},{1,0},{2,1},{3,2},{4,7},{5,4},{6,5},{7,6},{8,11},{9,8},{10,9... | collective-permute-start | bytes 3145736 | tf_op jit(solution)/shard_map/ppermute | solution.py:565
  123.2 1.0 copy-start.10
  124.2 47.1 %copy-start = (bf16[1024,512]{1,0:T(8,128)(2,1)S(1)}, bf16[1024,512]{1,0:T(8,128)(2,1)}, u32[]{:S(2)}) copy-start(bf16[1024,512]{1,0:T(8,128)(2,1)} %get-tuple-element.48.refs_5_.refs_0_) | copy-start | bytes 3145732
  131.1 44.7 %copy-start.7 = (s32[1,2,24]{2,1,0:T(2,128)S(1)}, s32[1,2,24]{2,1,0:T(2,128)}, u32[]{:S(2)}) copy-start(s32[1,2,24]{2,1,0:T(2,128)} %param.10) | copy-start | bytes 580
  131.1 44.7 %copy-start.8 = (bf16[1,2,24]{2,1,0:T(2,128)(2,1)S(1)}, bf16[1,2,24]{2,1,0:T(2,128)(2,1)}, u32[]{:S(2)}) copy-start(bf16[1,2,24]{2,1,0:T(2,128)(2,1)} %param.9) | copy-start | bytes 292
  131.1 44.7 %copy-start.9 = (s32[1,2]{1,0:T(1,128)S(1)}, s32[1,2]{1,0:T(1,128)}, u32[]{:S(2)}) copy-start(s32[1,2]{1,0:T(1,128)} %count_ref.3) | copy-start | bytes 28
  131.2 40.1 %collective-permute-start.19 = (bf16[1024,512]{1,0:T(8,128)(2,1)}, bf16[1024,512]{1,0:T(8,128)(2,1)}, u32[]{:S(2)}, u32[]{:S(2)}) collective-permute-start(bf16[1024,512]{1,0:T(8,128)(2,1)} %get-tuple-element.54), channel_id=1, source_target_pairs={{0,1},{1,2},{2,3},{3,0},{4,5},{5,6},{6,7},{7,4},{8,9},{9,10},{10,1... | collective-permute-start | bytes 3145736 | tf_op jit(solution)/shard_map/ppermute | solution.py:586
  132.1 39.1 %collective-permute-start.20 = (bf16[1024,512]{1,0:T(8,128)(2,1)}, bf16[1024,512]{1,0:T(8,128)(2,1)}, u32[]{:S(2)}, u32[]{:S(2)}) collective-permute-start(bf16[1024,512]{1,0:T(8,128)(2,1)} %get-tuple-element.55), channel_id=1, source_target_pairs={{0,3},{1,0},{2,1},{3,2},{4,7},{5,4},{6,5},{7,6},{8,11},{9,8},{10,9... | collective-permute-start | bytes 3145736 | tf_op jit(solution)/shard_map/ppermute | solution.py:587
  167.3 1.0 copy-start.1
  168.3 7.5 %copy-start.2 = (bf16[48,4224]{1,0:T(8,128)(2,1)S(1)}, bf16[48,4224]{1,0:T(8,128)(2,1)}, u32[]{:S(2)}) copy-start(bf16[48,4224]{1,0:T(8,128)(2,1)} %reduce-scatter.2.cloned.1.call-done.got_ref) | copy-start | bytes 1216516
  168.5 7.3 %collective-permute-start.14 = (bf16[24,4224]{1,0:T(8,128)(2,1)S(1)}, bf16[24,4224]{1,0:T(8,128)(2,1)S(1)}, u32[]{:S(2)}, u32[]{:S(2)}) collective-permute-start(bf16[24,4224]{1,0:T(8,128)(2,1)S(1)} %partner_rows.1), channel_id=1, source_target_pairs={{0,64},{64,0},{1,65},{65,1},{2,66},{66,2},{3,67},{67,3},{4,68},{68... | collective-permute-start | bytes 608264 | tf_op jit(solution)/shard_map/ppermute | solution.py:591
  171.3 1.2 copy-start.4
Sparse Core Ops, SparseCore 0:
  33.2 47.6 all-gather.1
  95.8 71.4 reduce-scatter.1
